TPU v7x, 32 devices: a whole 2x2x4 slice. The times are simulated.
32 devices in a mesh: star: 16 (over z, y, x), pix: 2 (over core).
Axes of the slice: x: 2, y: 2, z: 4, core: 2. Of those that a mesh axis runs over, the one named last changes fastest.
Arguments:
- flux: bfloat16 [5120, 8192], P('star', 'pix'), may hold values from -8 to 8
- inv_var: bfloat16 [5120, 8192], P('star', 'pix'), may hold values from 0.099609375 to 10
- coeffs: float32 [231, 8192], P(None, 'pix'), may hold values from -0.375 to 0.375
- labels: float32 [5120, 20], P('star'), may hold values from -4 to 4
Outputs:
- new_coeffs: float32 [231, 8192], P(None, 'pix')
- new_labels: float32 [5120, 20], P('star')
All inputs are finite; a program needn't handle non-finite values.
Results may differ from a plain program's by a relative error of at most 0.0087.
Values sent between devices are 32-bit elements; how exact they have to be, the bound alone decides.
No kernel may reach another device: no remote copies, remote signals or barrier semaphores. Data moves between devices by JAX's collectives and lax.ppermute only.
A program may use at most 64 MiB of HBM per device.

v0:
```python
import jax
import jax.numpy as jnp
import numpy as np
from jax import lax
from jax.sharding import PartitionSpec as P

ALTS = 2


step_size = 0.25


def pair_tables(count):
    left_index = []
    right_index = []
    for row_index in range(count):
        for col_index in range(row_index, count):
            left_index.append(row_index)
            right_index.append(col_index)
    pair_table = np.zeros((count, count), np.int32)
    doubling = np.ones((count, count), np.float32)
    for position in range(len(left_index)):
        pair_table[left_index[position], right_index[position]] = 1 + count + position
        pair_table[right_index[position], left_index[position]] = 1 + count + position
    for row_index in range(count):
        doubling[row_index, row_index] = 2.0
    return (np.array(left_index, np.int32), np.array(right_index, np.int32), pair_table, doubling)


def contract_rows(left, right):
    return lax.dot_general(
        left, right, (((0,), (0,)), ((), ())), preferred_element_type=jnp.float32
    )


def per_device(flux, inv_var, coeffs, labels):
    count = labels.shape[1]
    left_index, right_index, pair_table, doubling = pair_tables(count)
    flux_f = flux.astype(jnp.float32)
    ivar_f = inv_var.astype(jnp.float32)
    theta = coeffs
    lab = labels
    for turn in range(ALTS):
        quad = lab[:, left_index] * lab[:, right_index]
        feat = jnp.concatenate([jnp.ones((lab.shape[0], 1), jnp.float32), lab, quad], axis=1)
        feat_b = feat.astype(jnp.bfloat16)
        lab_b = lab.astype(jnp.bfloat16)
        sq_b = (feat * feat).astype(jnp.bfloat16)
        theta_b = theta.astype(jnp.bfloat16)
        model = jnp.dot(feat_b, theta_b, preferred_element_type=jnp.float32)
        weighted = (ivar_f * (flux_f - model)).astype(jnp.bfloat16)
        grad = contract_rows(feat_b, weighted)
        curv = contract_rows(sq_b, inv_var)
        grad, curv = lax.psum((grad, curv), "star")
        theta = theta + step_size * grad / (1.0 + curv)
        theta_b = theta.astype(jnp.bfloat16)
        model = jnp.dot(feat_b, theta_b, preferred_element_type=jnp.float32)
        rounded = lax.optimization_barrier((ivar_f * (flux_f - model)).astype(jnp.bfloat16))
        weighted2 = rounded.astype(jnp.float32)
        lead = theta_b[1 : 1 + count]
        blocks = (
            theta_b[pair_table.reshape(-1)].astype(jnp.float32) * doubling.reshape(-1, 1)
        ).astype(jnp.bfloat16)
        blocks = blocks.reshape(count, count, theta.shape[1])

        def per_label(item):
            linear, block = item
            jac = linear.astype(jnp.float32)[None, :] + jnp.dot(
                lab_b, block, preferred_element_type=jnp.float32
            )
            return (jnp.sum(weighted2 * jac, axis=1), jnp.sum(ivar_f * jac * jac, axis=1))

        grads, curvs = lax.map(per_label, (lead, blocks))
        lgrad = grads.T
        lcurv = curvs.T
        lgrad, lcurv = lax.psum((lgrad, lcurv), "pix")
        lab = lab + (lgrad - lab) / (1.0 + lcurv)
    return (theta, lab)


def solution(mesh):
    in_specs = (P("star", "pix"), P("star", "pix"), P(None, "pix"), P("star", None))
    out_specs = (P(None, "pix"), P("star", None))
    return jax.shard_map(
        per_device, mesh=mesh, in_specs=in_specs, out_specs=out_specs, check_vma=False
    )
```

profile of v0, /device:TPU:0, one launch (start us, length us, event | category | flops | bytes accessed | tf_op | source)
XLA Modules:
  0.0 826.1 jit_solution(6857875576071106708)
XLA Ops:
  16.3 7.2 fusion.21
  26.6 239.0 %all-reduce.9.cloned.1.call-done = (f32[231,4096]{1,0:T(8,128)}, f32[231,4096]{1,0:T(8,128)}) async-done(((f32[231,4096]{1,0:T(8,128)}, f32[231,4096]{1,0:T(8,128)}), (f32[231,4096]{1,0:T(8,128)}, f32[231,4096]{1,0:T(8,128)})) %all-reduce.9.cloned.1.call-update) | async-done | bytes 7569424 | tf_op jit(solution)/shard_map/psum | solution.py:54
  265.6 7.7 fusion.39
  280.3 5.8 reshape.24
  294.4 116.7 %while.24 = (s32[]{:T(128)}, f32[20,320]{1,0:T(8,128)S(1)}, f32[20,320]{1,0:T(8,128)S(1)}, bf16[20,4096]{1,0:T(8,128)(2,1)S(1)}, bf16[20,20,4096]{2,1,0:T(8,128)...) while((s32[]{:T(128)}, f32[20,320]{1,0:T(8,128)S(1)}, ...), condition=%wide.region_5.6_spmd, body=%wide.region_2.5_spmd.sunk | while | flops 60296576 | bytes 10749053 | solution.py:73
  294.4 5.6 fusion.52
  300.3 5.7 fusion.52
  306.1 5.7 fusion.52
  312.0 5.7 fusion.52
  317.8 5.7 fusion.52
  323.6 5.7 fusion.52
  329.5 5.7 fusion.52
  335.3 5.7 fusion.52
  341.1 5.7 fusion.52
  347.0 5.7 fusion.52
  352.8 5.7 fusion.52
  358.6 5.7 fusion.52
  364.5 5.7 fusion.52
  370.3 5.7 fusion.52
  376.1 5.7 fusion.52
  382.0 5.7 fusion.52
  387.8 5.7 fusion.52
  393.7 5.7 fusion.52
  399.5 5.7 fusion.52
  405.3 5.7 fusion.52
  421.5 6.8 fusion.19
  428.3 238.3 %all-reduce.7.cloned.1.call-done = (f32[231,4096]{1,0:T(8,128)}, f32[231,4096]{1,0:T(8,128)}) async-done(((f32[231,4096]{1,0:T(8,128)}, f32[231,4096]{1,0:T(8,128)}), (f32[231,4096]{1,0:T(8,128)}, f32[231,4096]{1,0:T(8,128)})) %all-reduce.7.cloned.1.call-update) | async-done | bytes 7569424 | tf_op jit(solution)/shard_map/psum | solution.py:54
  666.5 7.6 fusion.38
  683.6 5.8 reshape.25
  689.4 6.4 multiply_convert_fusion
  698.7 116.4 %while.25 = (s32[]{:T(128)}, f32[20,320]{1,0:T(8,128)S(1)}, f32[20,320]{1,0:T(8,128)S(1)}, bf16[20,4096]{1,0:T(8,128)(2,1)S(1)}, bf16[20,20,4096]{2,1,0:T(8,128)...) while((s32[]{:T(128)}, f32[20,320]{1,0:T(8,128)S(1)}, ...), condition=%wide.region_13.14_spmd, body=%wide.region_10.13_spmd.sunk | while | flops 60296576 | bytes 10749053 | solution.py:73
  698.8 5.6 fusion.54
  704.6 5.6 fusion.54
  710.4 5.6 fusion.54
  716.2 5.6 fusion.54
  722.0 5.6 fusion.54
  727.9 5.6 fusion.54
  733.7 5.6 fusion.54
  739.5 5.6 fusion.54
  745.3 5.6 fusion.54
  751.1 5.6 fusion.54
  757.0 5.6 fusion.54
  762.8 5.6 fusion.54
  768.6 5.6 fusion.54
  774.4 5.6 fusion.54
  780.2 5.6 fusion.54
  786.1 5.6 fusion.54
  791.9 5.6 fusion.54
  (254 shorter events, 76.6 us)
Async XLA Ops:
  7.2 3.4 copy-start
  7.2 6.1 copy-start.1
  7.2 258.4 %all-reduce.9.cloned.1.call-start = ((), (), s32[]{:S(2)}) async-start(), calls=%async_computation.1 | async-start | bytes 15204352 | tf_op jit(solution)/shard_map/psum | solution.py:54
  23.5 643.0 %all-reduce.7.cloned.1.call-start = ((), (), s32[]{:S(2)}) async-start(), calls=%async_computation | async-start | bytes 15204352 | tf_op jit(solution)/shard_map/psum | solution.py:54
  23.6 3.0 copy-start.7
  265.6 7.8 copy-start.2
  265.6 7.8 copy-start.3
  280.3 10.7 %copy-start.6 = (f32[20,20]{1,0:T(8,128)S(1)}, f32[20,20]{1,0:T(8,128)}, u32[]{:S(2)}) copy-start(f32[20,20]{1,0:T(8,128)} %constant.59) | copy-start | bytes 4804
  286.2 5.2 copy-start.4
  689.4 6.4 copy-start.5
Sparse Core Ops, SparseCore 0:
  23.7 241.9 all-reduce.8
  428.4 238.1 all-reduce.6
where the time goes:
time: 827 us; the launch traced here: 826 us
  waiting for transfers between devices  477 us (58%)
  matrix products  256 us (31%)
  other arithmetic  39.5 us (5%)
  local copies, waits for them, and re-layouts  30.2 us (4%)
  between operations  14.2 us (2%)
    psum x2, waiting for transfers between devices, per_device(): grad, curv = lax.psum((grad, curv), 'star')  477 us
    dot_general x40, matrix products, per_label(): jnp.dot(lab_b, block, preferred_element_type=jnp.float32)  226 us
    dot_general x4, matrix products, contract_rows(): lax.dot_general(left, right, (((0,), (0,)), ((), ())), preferred_element_...  21.8 us
  transfers between devices with their start and end apart: 2, of which 2 were waited for; matrix products, arithmetic and copies ran while one was open for 0% of the time, Pallas kernels for 0%

commit v1 on v0

--- a/solution.py
+++ b/solution.py
@@ -1,11 +1,17 @@
+import functools
+
 import jax
 import jax.numpy as jnp
 import numpy as np
 from jax import lax
+from jax.experimental import pallas as pl
+from jax.experimental.pallas import tpu as pltpu
 from jax.sharding import PartitionSpec as P
 
 ALTS = 2
-
+WAVES = 2
+LANES = 128
+VMEM_LIMIT = 48 * 1024 * 1024
 
 step_size = 0.25
 
@@ -27,13 +33,17 @@
     return (np.array(left_index, np.int32), np.array(right_index, np.int32), pair_table, doubling)
 
 
+def round_up(value, unit):
+    return -(-value // unit) * unit
+
+
 def contract_rows(left, right):
     return lax.dot_general(
         left, right, (((0,), (0,)), ((), ())), preferred_element_type=jnp.float32
     )
 
 
-def per_device(flux, inv_var, coeffs, labels):
+def plain_device(flux, inv_var, coeffs, labels):
     count = labels.shape[1]
     left_index, right_index, pair_table, doubling = pair_tables(count)
     flux_f = flux.astype(jnp.float32)
@@ -78,9 +88,420 @@
     return (theta, lab)
 
 
+def feature_maps(count, padded):
+    left_index, right_index, pair_table, doubling = pair_tables(count)
+    rows = round_up(1 + count, 32)
+    left = np.zeros((rows, padded), np.float32)
+    right = np.zeros((rows, padded), np.float32)
+    left[0, 0] = 1.0
+    right[0, : 1 + count] = 1.0
+    for label in range(count):
+        left[1 + label, 1 + label] = 1.0
+    for position in range(len(left_index)):
+        left[1 + left_index[position], 1 + count + position] = 1.0
+        right[1 + right_index[position], 1 + count + position] = 1.0
+    select = np.zeros((count, rows, padded), np.float32)
+    for label in range(count):
+        select[label, 0, 1 + label] = 1.0
+        for other in range(count):
+            select[label, 1 + other, pair_table[label, other]] = doubling[label, other]
+    return left, right, select.reshape(count * rows, padded)
+
+
+def split_exact(value):
+    high = value.astype(jnp.bfloat16)
+    rest = value - high.astype(jnp.float32)
+    middle = rest.astype(jnp.bfloat16)
+    low = (rest - middle.astype(jnp.float32)).astype(jnp.bfloat16)
+    return high, middle, low
+
+
+def mm(left, right):
+    return jnp.dot(left, right, preferred_element_type=jnp.float32)
+
+
+def write_features(lab, left_ref, right_ref, feat_ref, featt_ref, sqt_ref, lab1_ref):
+    parts = split_exact(lab)
+    first = sum(mm(part, left_ref[...]) for part in parts[::-1])
+    second = sum(mm(part, right_ref[...]) for part in parts[::-1])
+    feat = first * second
+    feat_ref[...] = feat.astype(jnp.bfloat16)
+    featt_ref[...] = feat.T.astype(jnp.bfloat16)
+    sqt_ref[...] = (feat * feat).T.astype(jnp.bfloat16)
+    lab1_ref[...] = lab.astype(jnp.bfloat16)
+
+
+def features_kernel(lab_ref, left_ref, right_ref, *outs):
+    write_features(lab_ref[...], left_ref, right_ref, *outs)
+
+
+def update_kernel(count, lab_ref, here_ref, there_ref, left_ref, right_ref, new_ref, *outs):
+    lab = lab_ref[...]
+    stars, rows = lab.shape
+    total = here_ref[...] + there_ref[...]
+    lgrad = total[:, :rows]
+    lcurv = total[:, LANES : LANES + rows]
+    column = lax.broadcasted_iota(jnp.int32, lab.shape, 1)
+    inside = (column >= 1) & (column <= count)
+    lab = jnp.where(inside, lab + (lgrad - lab) / (1.0 + lcurv), lab)
+    new_ref[...] = lab
+    write_features(lab, left_ref, right_ref, *outs)
+
+
+def theta_pair(refs, spans, first, second):
+    columns = []
+    for piece in (first, second):
+        rows = [ref[piece] for ref in refs]
+        columns.append(jnp.concatenate(rows, axis=0))
+    return jnp.concatenate(columns, axis=1)
+
+
+def grad_kernel(plan, from_coeffs, me_ref, *refs):
+    n, half, parts = plan["n"], plan["half"], plan["parts"]
+    flux_ref, ivar_ref, feat_ref, featt_ref, sqt_ref = refs[:5]
+    refs = refs[5:]
+    if from_coeffs:
+        coeffs_ref, refs = refs[0], refs[1:]
+    else:
+        thetas, refs = refs[: 2 * len(parts)], refs[2 * len(parts) :]
+    sends, keeps = refs[: len(parts)], refs[len(parts) :]
+    low = me_ref[0] & (half - 1)
+    feat = feat_ref[...]
+    for pair in range(half // 2):
+        spots = [pl.multiple_of((r ^ low) * LANES, LANES) for r in (2 * pair, 2 * pair + 1)]
+
+        def wide(ref):
+            return jnp.concatenate([ref[:, pl.ds(spot, LANES)] for spot in spots], axis=1)
+
+        flux = wide(flux_ref)
+        ivar = wide(ivar_ref)
+        if from_coeffs:
+            theta = wide(coeffs_ref).astype(jnp.bfloat16)
+            model = mm(feat[:, : theta.shape[0]], theta)
+        else:
+            theta = jnp.concatenate(
+                [
+                    jnp.concatenate(
+                        [
+                            theta_piece(plan, thetas, part, r)
+                            for part in range(len(parts))
+                        ],
+                        axis=0,
+                    )
+                    for r in (2 * pair, 2 * pair + 1)
+                ],
+                axis=1,
+            ).astype(jnp.bfloat16)
+            model = mm(feat[:, : theta.shape[0]], theta)
+        weighted = (ivar.astype(jnp.float32) * (flux.astype(jnp.float32) - model)).astype(jnp.bfloat16)
+        grad = mm(featt_ref[...], weighted)
+        curv = mm(sqt_ref[...], ivar)
+        for side, r in enumerate((2 * pair, 2 * pair + 1)):
+            lanes = slice(side * LANES, (side + 1) * LANES)
+            for index, part in enumerate(parts):
+                upper, spot = place(part["order"], r)
+                target = sends[index] if upper else keeps[index]
+                rows = slice(part["start"], part["start"] + part["rows"])
+                target[spot, 0, 0] = grad[rows, lanes]
+                target[spot, 0, 1] = curv[rows, lanes]
+
+
+def place(order, r):
+    bits = [(r >> bit) & 1 for bit in order[:-1]]
+    spot = 0
+    for bit in bits[1:]:
+        spot = 2 * spot + bit
+    return bits[0], spot
+
+
+def theta_piece(plan, thetas, part, r):
+    upper, spot = place(plan["parts"][part]["order"], r)
+    return thetas[2 * part + upper][spot, 0]
+
+
+def label_kernel(plan, count, last, me_ref, *refs):
+    n, half, parts = plan["n"], plan["half"], plan["parts"]
+    flux_ref, ivar_ref, feat_ref, lab1_ref, select_ref = refs[:5]
+    thetas = refs[5 : 5 + 2 * len(parts)]
+    refs = refs[5 + 2 * len(parts) :]
+    sums_ref, refs = refs[0], refs[1:]
+    if last:
+        new_ref, refs = refs[0], refs[1:]
+    dots_ref, squares_ref, iv_ref = refs
+    low = me_ref[0] & (half - 1)
+    step = pl.program_id(0)
+    stars = flux_ref.shape[0]
+    rows = lab1_ref.shape[1]
+
+    @pl.when(step == 0)
+    def _():
+        dots_ref[...] = jnp.zeros_like(dots_ref)
+        squares_ref[...] = jnp.zeros_like(squares_ref)
+
+    feat = feat_ref[...]
+    for pair in range(half // 2):
+        spots = [pl.multiple_of((r ^ low) * LANES, LANES) for r in (2 * pair, 2 * pair + 1)]
+
+        def wide(ref):
+            return jnp.concatenate([ref[:, pl.ds(spot, LANES)] for spot in spots], axis=1)
+
+        columns = []
+        for r, spot in zip((2 * pair, 2 * pair + 1), spots):
+            column = jnp.concatenate(
+                [theta_piece(plan, thetas, part, r) for part in range(len(parts))], axis=0
+            )
+            if last:
+                new_ref[:, pl.ds(spot, LANES)] = column[: new_ref.shape[0]]
+            columns.append(column)
+        theta = jnp.concatenate(columns, axis=1).astype(jnp.bfloat16)
+        ivar = wide(ivar_ref).astype(jnp.float32)
+        iv_ref[...] = ivar
+        model = mm(feat[:, : theta.shape[0]], theta)
+        weighted = (ivar * (wide(flux_ref).astype(jnp.float32) - model)).astype(jnp.bfloat16)
+        dots_ref[...] += lax.dot_general(
+            weighted, theta, (((1,), (1,)), ((), ())), preferred_element_type=jnp.float32
+        )
+        blocks = mm(select_ref[:, : theta.shape[0]], theta).astype(jnp.bfloat16)
+        for label in range(count):
+            jac = mm(lab1_ref[...], blocks[label * rows : (label + 1) * rows])
+            term = jac * jac * iv_ref[...]
+            squares_ref[label] += term[:, :LANES] + term[:, LANES:]
+
+    @pl.when(step == pl.num_programs(0) - 1)
+    def _():
+        dots = dots_ref[...]
+        column = lax.broadcasted_iota(jnp.int32, (stars, LANES), 1)
+        lgrad = jnp.zeros((stars, LANES), jnp.float32)
+        lcurv = jnp.zeros((stars, LANES), jnp.float32)
+        for label in range(count):
+            slopes = mm(lab1_ref[...], select_ref[label * rows : (label + 1) * rows, : dots.shape[1]])
+            here = column == 1 + label
+            lgrad = jnp.where(here, jnp.sum(slopes * dots, axis=1, keepdims=True), lgrad)
+            lcurv = jnp.where(here, jnp.sum(squares_ref[label], axis=1, keepdims=True), lcurv)
+        sums_ref[:, :LANES] = lgrad
+        sums_ref[:, LANES:] = lcurv
+
+
+def exchange(value, bit, n):
+    return lax.ppermute(value, "star", [(d, d ^ (1 << bit)) for d in range(n)])
+
+
+def pieces_device(plan, flux, inv_var, coeffs, labels):
+    n, bits, half, parts = plan["n"], plan["bits"], plan["half"], plan["parts"]
+    stars, pixels = flux.shape
+    count = labels.shape[1]
+    features = coeffs.shape[0]
+    padded = plan["padded"]
+    height = sum(part["rows"] for part in parts)
+    left, right, select = feature_maps(count, padded)
+    rows = left.shape[0]
+    left = jnp.asarray(left, jnp.bfloat16)
+    right = jnp.asarray(right, jnp.bfloat16)
+    select = jnp.asarray(select, jnp.bfloat16)
+    me = lax.axis_index("star")
+    me_vec = me.astype(jnp.int32).reshape(1)
+    block = half * LANES
+    params = pltpu.CompilerParams(vmem_limit_bytes=VMEM_LIMIT)
+    whole = pl.BlockSpec(memory_space=pltpu.VMEM)
+
+    feature_shapes = [
+        jax.ShapeDtypeStruct((stars, padded), jnp.bfloat16),
+        jax.ShapeDtypeStruct((padded, stars), jnp.bfloat16),
+        jax.ShapeDtypeStruct((padded, stars), jnp.bfloat16),
+        jax.ShapeDtypeStruct((stars, rows), jnp.bfloat16),
+    ]
+    lab = jnp.pad(
+        jnp.concatenate([jnp.ones((stars, 1), jnp.float32), labels], axis=1),
+        ((0, 0), (0, rows - 1 - count)),
+    )
+    feat, featt, sqt, lab1 = pl.pallas_call(
+        features_kernel,
+        out_shape=feature_shapes,
+        in_specs=[whole] * 3,
+        out_specs=[whole] * 4,
+        compiler_params=params,
+        name="features",
+    )(lab, left, right)
+
+    def pixel_spec(height, wave):
+        return pl.BlockSpec(
+            (height, block), lambda step, me, wave=wave: (0, 2 * wave + (step ^ (me[0] >> (bits - 1))))
+        )
+
+    def fixed(array):
+        return pl.BlockSpec(array.shape, lambda step, me: (0,) * array.ndim)
+
+    def theta_spec(part):
+        return pl.BlockSpec((half // 2, 1, part["rows"], LANES), lambda step, me: (0, step, 0, 0))
+
+    def grad_call(wave, thetas):
+        specs = [pixel_spec(stars, wave)] * 2 + [fixed(feat), fixed(featt[:height]), fixed(sqt[:height])]
+        operands = [flux, inv_var, feat, featt, sqt]
+        if thetas is None:
+            specs.append(pixel_spec(features, wave))
+            operands.append(coeffs)
+        else:
+            for part, arrays in zip(parts, thetas):
+                specs += [theta_spec(part)] * 2
+                operands += list(arrays)
+        shapes = [
+            jax.ShapeDtypeStruct((half // 2, 2, 2, part["rows"], LANES), jnp.float32) for part in parts
+        ] * 2
+        out_specs = [
+            pl.BlockSpec((half // 2, 1, 2, part["rows"], LANES), lambda step, me: (0, step, 0, 0, 0))
+            for part in parts
+        ] * 2
+        outs = pl.pallas_call(
+            functools.partial(grad_kernel, plan, thetas is None),
+            out_shape=shapes,
+            grid_spec=pltpu.PrefetchScalarGridSpec(
+                num_scalar_prefetch=1, grid=(2,), in_specs=specs, out_specs=out_specs
+            ),
+            compiler_params=params,
+            cost_estimate=pl.CostEstimate(
+                flops=6 * stars * height * 2 * block,
+                bytes_accessed=2 * block * (4 * stars + 12 * height),
+                transcendentals=0,
+            ),
+            name="gradient",
+        )(me_vec, *operands)
+        flat = [out.reshape((n // 2,) + out.shape[2:]) for out in outs]
+        return flat[: len(parts)], flat[len(parts) :]
+
+    def label_call(wave, thetas, last, new):
+        specs = [pixel_spec(stars, wave)] * 2 + [fixed(feat), fixed(lab1), fixed(select)]
+        operands = [flux, inv_var, feat, lab1, select]
+        for part, arrays in zip(parts, thetas):
+            specs += [theta_spec(part)] * 2
+            operands += list(arrays)
+        shapes = [jax.ShapeDtypeStruct((stars, 2 * LANES), jnp.float32)]
+        out_specs = [pl.BlockSpec((stars, 2 * LANES), lambda step, me: (0, 0))]
+        if last:
+            shapes.append(jax.ShapeDtypeStruct((features, 2 * block), jnp.float32))
+            out_specs.append(
+                pl.BlockSpec((features, block), lambda step, me: (0, step ^ (me[0] >> (bits - 1))))
+            )
+        outs = pl.pallas_call(
+            functools.partial(label_kernel, plan, count, last),
+            out_shape=shapes,
+            grid_spec=pltpu.PrefetchScalarGridSpec(
+                num_scalar_prefetch=1,
+                grid=(2,),
+                in_specs=specs,
+                out_specs=out_specs,
+                scratch_shapes=[
+                    pltpu.VMEM((stars, height), jnp.float32),
+                    pltpu.VMEM((count, stars, LANES), jnp.float32),
+                    pltpu.VMEM((stars, 2 * LANES), jnp.float32),
+                ],
+            ),
+            compiler_params=params,
+            cost_estimate=pl.CostEstimate(
+                flops=2 * stars * 256 * 2 * block * (count + 2),
+                bytes_accessed=2 * block * (4 * stars + 4 * height),
+                transcendentals=0,
+            ),
+            name="labels",
+        )(me_vec, *operands)
+        return outs
+
+    base = jnp.pad(
+        jnp.stack(
+            [
+                lax.dynamic_slice(coeffs, (0, (wave * n + me) * LANES), (features, LANES))
+                for wave in range(WAVES)
+            ]
+        ),
+        ((0, 0), (0, height - features), (0, 0)),
+    )
+    own = [
+        [base[wave, part["start"] : part["start"] + part["rows"]] for part in parts]
+        for wave in range(WAVES)
+    ]
+    thetas = [None] * WAVES
+    for turn in range(ALTS):
+        last = turn == ALTS - 1
+        sums = None
+        news = []
+        for wave in range(WAVES):
+            sends, keeps = grad_call(wave, thetas[wave])
+            gathered = []
+            for index, part in enumerate(parts):
+                order = part["order"]
+                kept = [keeps[index]]
+                arrived = exchange(sends[index], order[0], n)
+                size = n // 2
+                for bit in order[1:]:
+                    kept.append(arrived)
+                    size //= 2
+                    outgoing = sum(array[size : 2 * size] for array in kept)
+                    arrived = exchange(outgoing, bit, n)
+                kept.append(arrived)
+                total = sum(array[0] for array in kept)
+                own[wave][index] = own[wave][index] + step_size * total[0] / (1.0 + total[1])
+                held = own[wave][index][None]
+                for bit in order[:0:-1]:
+                    held = jnp.concatenate([held, exchange(held, bit, n)], axis=0)
+                other = exchange(held, order[0], n)
+                gathered.append(
+                    [array.reshape((n // 4, 2) + array.shape[1:]) for array in (held, other)]
+                )
+            thetas[wave] = gathered
+        for wave in range(WAVES):
+            outs = label_call(wave, thetas[wave], last, None)
+            sums = outs[0] if sums is None else sums + outs[0]
+            if last:
+                news.append(outs[1])
+        there = lax.ppermute(sums, "pix", plan["swap"])
+        new_lab, feat, featt, sqt, lab1 = pl.pallas_call(
+            functools.partial(update_kernel, count),
+            out_shape=[jax.ShapeDtypeStruct((stars, rows), jnp.float32)] + feature_shapes,
+            in_specs=[whole] * 5,
+            out_specs=[whole] * 5,
+            compiler_params=params,
+            name="update",
+        )(lab, sums, there, left, right)
+        lab = new_lab
+    return jnp.concatenate(news, axis=1), lab[:, 1 : 1 + count]
+
+
+def make_plan(mesh, flux, coeffs):
+    n = mesh.shape["star"]
+    bits = n.bit_length() - 1
+    stars = flux.shape[0] // n
+    pixels = flux.shape[1] // mesh.shape["pix"]
+    if n != 1 << bits or bits < 4 or mesh.shape["pix"] != 2:
+        return None
+    if pixels != WAVES * n * LANES or stars % 16:
+        return None
+    height = round_up(coeffs.shape[0], 8)
+    first = round_up(int(0.4 * height), 16)
+    second = round_up(int(0.34 * height), 16)
+    cuts = [0, first, first + second, height]
+    rest = list(range(3, bits))
+    orders = [[0, 1, 2] + rest, [1, 2, 0] + rest, [2, 0, 1] + rest]
+    parts = [
+        {"start": cuts[i], "rows": cuts[i + 1] - cuts[i], "order": orders[i]} for i in range(3)
+    ]
+    return {
+        "n": n,
+        "bits": bits,
+        "half": n // 2,
+        "parts": parts,
+        "padded": round_up(coeffs.shape[0], 256),
+        "swap": [(0, 1), (1, 0)],
+    }
+
+
 def solution(mesh):
     in_specs = (P("star", "pix"), P("star", "pix"), P(None, "pix"), P("star", None))
     out_specs = (P(None, "pix"), P("star", None))
-    return jax.shard_map(
-        per_device, mesh=mesh, in_specs=in_specs, out_specs=out_specs, check_vma=False
-    )
+
+    def run(flux, inv_var, coeffs, labels):
+        plan = make_plan(mesh, flux, coeffs)
+        body = plain_device if plan is None else functools.partial(pieces_device, plan)
+        return jax.shard_map(
+            body, mesh=mesh, in_specs=in_specs, out_specs=out_specs, check_vma=False
+        )(flux, inv_var, coeffs, labels)
+
+    return run

time: 827 us -> 431 us (0.52)
  waiting for transfers between devices: 477 us -> 197 us
  matrix products: 256 us -> 0 us
  starting transfers between devices: 0.08 us -> 117 us
  Pallas kernels: 0 us -> 75.1 us
  local copies, waits for them, and re-layouts: 30.2 us -> 9.95 us
  other arithmetic: 39.5 us -> 22.6 us
  between operations: 14.2 us -> 1.65 us
    psum x2 -> x0, waiting for transfers between devices: 477 us -> none  [per_device(): grad, curv = lax.psum((grad, curv), 'star')]
    dot_general x46 -> x0, matrix products: 256 us -> none  [the longest x40 226 us: per_label(): jnp.dot(lab_b, block, preferred_element_type=jnp.float32)]
    ppermute x0 -> x98, waiting for transfers between devices: none -> 197 us  [the longest x96 196 us: exchange(): return lax.ppermute(value, 'star', [(d, d ^ 1 << bit) for d in range(n)])]
    ppermute x0 -> x98, starting transfers between devices: none -> 117 us  [the longest x96 117 us: exchange(): return lax.ppermute(value, 'star', [(d, d ^ 1 << bit) for d in range(n)])]
    pallas_call x0 -> x11, Pallas kernels: none -> 75.1 us  [the longest x4 51.2 us: label_call(): pl.pallas_call(functools.partial(label_kernel, plan, count, last), out_sh...]
    convert_element_type x9 -> x0, other arithmetic: 35.4 us -> none  [the longest x2 15.2 us: per_device(): theta_b = theta.astype(jnp.bfloat16)]
    add x41 -> x61, other arithmetic: 1.5 us -> 19.6 us  [the longest x36 14.7 us: pieces_device(): outgoing = sum((array[size:2 * size] for array in kept))]
    gather x6 -> x0, local copies, waits for them, and re-layouts: 13.5 us -> none  [the longest x2 8.21 us: per_device(): theta_b[pair_table.reshape(-1)].astype(jnp.float32)]
  transfers between devices with their start and end apart: 2 -> 98, of which waited for: 2 -> 61; matrix products, arithmetic and copies ran while one was open for 0% -> 6% of each run, Pallas kernels for 0% -> 9%
where the time goes in v1:
time: 431 us; the launch traced here: 423 us
  waiting for transfers between devices  197 us (46%)
  starting transfers between devices  117 us (27%)
  Pallas kernels  75.1 us (17%)
  other arithmetic  22.6 us (5%)
  local copies, waits for them, and re-layouts  9.95 us (2%)
    ppermute x96, waiting for transfers between devices, exchange(): return lax.ppermute(value, 'star', [(d, d ^ 1 << bit) for d in range(n)])  196 us
    ppermute x96, starting transfers between devices, exchange(): return lax.ppermute(value, 'star', [(d, d ^ 1 << bit) for d in range(n)])  117 us
    pallas_call x4, Pallas kernels, label_call(): pl.pallas_call(functools.partial(label_kernel, plan, count, last), out_sh...  51.2 us
    pallas_call x4, Pallas kernels, grad_call(): pl.pallas_call(functools.partial(grad_kernel, plan, thetas is None), out_...  21.6 us
    add x36, other arithmetic, pieces_device(): outgoing = sum((array[size:2 * size] for array in kept))  14.7 us
  transfers between devices with their start and end apart: 98, of which 61 were waited for; matrix products, arithmetic and copies ran while one was open for 6% of the time, Pallas kernels for 9%

profile of v1, /device:TPU:0, one launch (start us, length us, event | category | flops | bytes accessed | tf_op | source)
XLA Modules:
  0.0 423.4 jit_solution(437590106141633265)
XLA Ops:
  3.6 5.6 %gradient.5 = (f32[4,2,2,96,128]{4,3,2,1,0:T(8,128)}, f32[4,2,2,80,128]{4,3,2,1,0:T(8,128)}, f32[4,2,2,56,128]{4,3,2,1,0:T(8,128)}, f32[4,2,2,96,128]{4,3,2,1,0:...) custom-call(s32[1]{0:T(128)} %bitcast.me_ref, bf16[320,4096]{1,0:T(8,128)(2,1)} %refs_0_.15, ...), custom_call_target="tpu_custom_call" | custom-call | flops 912261120 | bytes 8323072 | tf_op jit(solution)/shard_map/gradient/pallas_call | solution.py:354
  10.0 3.0 collective-permute-start.40
  16.0 5.5 %gradient.4 = (f32[4,2,2,96,128]{4,3,2,1,0:T(8,128)S(1)}, f32[4,2,2,80,128]{4,3,2,1,0:T(8,128)}, f32[4,2,2,56,128]{4,3,2,1,0:T(8,128)}, f32[4,2,2,96,128]{4,3,2,...) custom-call(s32[1]{0:T(128)} %bitcast.me_ref, bf16[320,4096]{1,0:T(8,128)(2,1)} %refs_0_.15, ...), custom_call_target="tpu_custom_call" | custom-call | flops 912261120 | bytes 8323072 | tf_op jit(solution)/shard_map/gradient/pallas_call | solution.py:354
  28.5 6.4 %collective-permute-done.16 = f32[8,2,56,128]{3,2,1,0:T(8,128)} collective-permute-done((f32[8,2,56,128]{3,2,1,0:T(8,128)}, f32[8,2,56,128]{3,2,1,0:T(8,128)}, u32[]{:S(2)}, u32[]{:S(2)}) %collective-permute-start.16) | collective-permute-done | bytes 458784 | tf_op jit(solution)/shard_map/ppermute | solution.py:286
  39.0 4.6 %collective-permute-done.8 = f32[8,2,80,128]{3,2,1,0:T(8,128)} collective-permute-done((f32[8,2,80,128]{3,2,1,0:T(8,128)}, f32[8,2,80,128]{3,2,1,0:T(8,128)}, u32[]{:S(2)}, u32[]{:S(2)}) %collective-permute-start.8) | collective-permute-done | bytes 655392 | tf_op jit(solution)/shard_map/ppermute | solution.py:286
  44.8 12.2 %collective-permute-done.41 = f32[4,2,56,128]{3,2,1,0:T(8,128)S(1)} collective-permute-done((f32[4,2,56,128]{3,2,1,0:T(8,128)S(1)}, f32[4,2,56,128]{3,2,1,0:T(8,128)S(1)}, u32[]{:S(2)}, u32[]{:S(2)}) %collective-permute-start.41) | collective-permute-done | bytes 229408 | tf_op jit(solution)/shard_map/ppermute | solution.py:286
  67.7 2.6 collective-permute-start.43
  76.2 3.3 collective-permute-done.19
  86.2 4.1 collective-permute-done.20
  118.1 2.7 collective-permute-start.36
  123.2 2.5 collective-permute-start.12
  129.4 3.3 collective-permute-done.37
  133.8 3.3 collective-permute-done.13
  140.2 3.0 collective-permute-start.27
  143.2 2.7 collective-permute-done.27
  145.8 3.0 collective-permute-start.3
  151.5 3.0 collective-permute-start.28
  156.5 3.3 collective-permute-start.29
  159.9 3.6 collective-permute-done.29
  171.8 3.7 collective-permute-done.5
  185.2 12.4 %labels.5 = f32[320,256]{1,0:T(8,128)S(1)} custom-call(s32[1]{0:T(128)} %bitcast.me_ref, bf16[320,4096]{1,0:T(8,128)(2,1)S(1)} %copy-done, bf16[320,4096]{1,0:T(8,128)(2,1)} %refs_1_.15, bf16[320,256]{1,0:T(8,128)(2,1)S(1)} %get-tuple-element.40.refs_2_, bf16[320,32]{1,0:T(8,128)(2,1)S(1)} %get-tuple-element.41.refs_3_, bf16[640,256]{1,0:T(8,128)(2,1)S(1)} %copy-done.11, ...), custom_call_target="tpu_custom_call" | custom-call | flops 7381975040 | bytes 4521984 | tf_op jit(solution)/shard_map/labels/pallas_call | solution.py:384
  197.7 12.6 %labels.4 = f32[320,256]{1,0:T(8,128)S(1)} custom-call(s32[1]{0:T(128)} %bitcast.me_ref, bf16[320,4096]{1,0:T(8,128)(2,1)S(1)} %copy-done, bf16[320,4096]{1,0:T(8,128)(2,1)} %refs_1_.15, bf16[320,256]{1,0:T(8,128)(2,1)S(1)} %get-tuple-element.40.refs_2_, bf16[320,32]{1,0:T(8,128)(2,1)S(1)} %get-tuple-element.41.refs_3_, bf16[640,256]{1,0:T(8,128)(2,1)S(1)} %copy-done.11, ...), custom_call_target="tpu_custom_call" | custom-call | flops 7381975040 | bytes 4521984 | tf_op jit(solution)/shard_map/labels/pallas_call | solution.py:384
  212.6 5.2 %gradient.7 = (f32[4,2,2,96,128]{4,3,2,1,0:T(8,128)S(1)}, f32[4,2,2,80,128]{4,3,2,1,0:T(8,128)S(1)}, f32[4,2,2,56,128]{4,3,2,1,0:T(8,128)S(1)}, f32[4,2,2,96,128...) custom-call(s32[1]{0:T(128)} %bitcast.me_ref, bf16[320,4096]{1,0:T(8,128)(2,1)} %refs_0_.15, ...), custom_call_target="tpu_custom_call" | custom-call | flops 912261120 | bytes 8323072 | tf_op jit(solution)/shard_map/gradient/pallas_call | solution.py:354
  219.4 5.3 %gradient.6 = (f32[4,2,2,96,128]{4,3,2,1,0:T(8,128)S(1)}, f32[4,2,2,80,128]{4,3,2,1,0:T(8,128)S(1)}, f32[4,2,2,56,128]{4,3,2,1,0:T(8,128)S(1)}, f32[4,2,2,96,128...) custom-call(s32[1]{0:T(128)} %bitcast.me_ref, bf16[320,4096]{1,0:T(8,128)(2,1)} %refs_0_.15, ...), custom_call_target="tpu_custom_call" | custom-call | flops 912261120 | bytes 8323072 | tf_op jit(solution)/shard_map/gradient/pallas_call | solution.py:354
  232.8 7.4 %collective-permute-done.65 = f32[8,2,56,128]{3,2,1,0:T(8,128)S(1)} collective-permute-done((f32[8,2,56,128]{3,2,1,0:T(8,128)S(1)}, f32[8,2,56,128]{3,2,1,0:T(8,128)S(1)}, u32[]{:S(2)}, u32[]{:S(2)}) %collective-permute-start.65) | collective-permute-done | bytes 458784 | tf_op jit(solution)/shard_map/ppermute | solution.py:286
  244.6 10.9 %collective-permute-done.57 = f32[8,2,80,128]{3,2,1,0:T(8,128)S(1)} collective-permute-done((f32[8,2,80,128]{3,2,1,0:T(8,128)S(1)}, f32[8,2,80,128]{3,2,1,0:T(8,128)S(1)}, u32[]{:S(2)}, u32[]{:S(2)}) %collective-permute-start.57) | collective-permute-done | bytes 655392 | tf_op jit(solution)/shard_map/ppermute | solution.py:286
  257.1 11.1 %collective-permute-done.90 = f32[4,2,56,128]{3,2,1,0:T(8,128)S(1)} collective-permute-done((f32[4,2,56,128]{3,2,1,0:T(8,128)S(1)}, f32[4,2,56,128]{3,2,1,0:T(8,128)S(1)}, u32[]{:S(2)}, u32[]{:S(2)}) %collective-permute-start.90) | collective-permute-done | bytes 229408 | tf_op jit(solution)/shard_map/ppermute | solution.py:286
  281.2 4.9 %collective-permute-done.92 = f32[1,2,56,128]{3,2,1,0:T(8,128)S(1)} collective-permute-done((f32[1,2,56,128]{3,2,1,0:T(8,128)S(1)}, f32[1,2,56,128]{3,2,1,0:T(8,128)S(1)}, u32[]{:S(2)}, u32[]{:S(2)}) %collective-permute-start.92) | collective-permute-done | bytes 57376 | tf_op jit(solution)/shard_map/ppermute | solution.py:286
  286.3 5.6 %collective-permute-done.68 = f32[1,2,56,128]{3,2,1,0:T(8,128)S(1)} collective-permute-done((f32[1,2,56,128]{3,2,1,0:T(8,128)S(1)}, f32[1,2,56,128]{3,2,1,0:T(8,128)S(1)}, u32[]{:S(2)}, u32[]{:S(2)}) %collective-permute-start.68) | collective-permute-done | bytes 57376 | tf_op jit(solution)/shard_map/ppermute | solution.py:286
  291.9 4.7 %collective-permute-done.93 = f32[1,56,128]{2,1,0:T(8,128)S(1)} collective-permute-done((f32[1,56,128]{2,1,0:T(8,128)S(1)}, f32[1,56,128]{2,1,0:T(8,128)S(1)}, u32[]{:S(2)}, u32[]{:S(2)}) %collective-permute-start.93) | collective-permute-done | bytes 28704 | tf_op jit(solution)/shard_map/ppermute | solution.py:286
  296.7 4.7 %collective-permute-done.69 = f32[1,56,128]{2,1,0:T(8,128)S(1)} collective-permute-done((f32[1,56,128]{2,1,0:T(8,128)S(1)}, f32[1,56,128]{2,1,0:T(8,128)S(1)}, u32[]{:S(2)}, u32[]{:S(2)}) %collective-permute-start.69) | collective-permute-done | bytes 28704 | tf_op jit(solution)/shard_map/ppermute | solution.py:286
  301.4 4.2 collective-permute-done.94
  305.6 4.2 collective-permute-done.70
  320.2 2.9 collective-permute-start.60
  323.6 3.5 collective-permute-done.84
  328.5 4.5 %collective-permute-done.85 = f32[1,80,128]{2,1,0:T(8,128)S(1)} collective-permute-done((f32[1,80,128]{2,1,0:T(8,128)S(1)}, f32[1,80,128]{2,1,0:T(8,128)S(1)}, u32[]{:S(2)}, u32[]{:S(2)}) %collective-permute-start.85) | collective-permute-done | bytes 40992 | tf_op jit(solution)/shard_map/ppermute | solution.py:286
  334.1 5.1 %collective-permute-done.61 = f32[1,80,128]{2,1,0:T(8,128)S(1)} collective-permute-done((f32[1,80,128]{2,1,0:T(8,128)S(1)}, f32[1,80,128]{2,1,0:T(8,128)S(1)}, u32[]{:S(2)}, u32[]{:S(2)}) %collective-permute-start.61) | collective-permute-done | bytes 40992 | tf_op jit(solution)/shard_map/ppermute | solution.py:286
  340.4 3.2 collective-permute-done.86
  344.9 3.2 collective-permute-done.62
  350.6 6.3 %collective-permute-done.76 = f32[1,2,96,128]{3,2,1,0:T(8,128)S(1)} collective-permute-done((f32[1,2,96,128]{3,2,1,0:T(8,128)S(1)}, f32[1,2,96,128]{3,2,1,0:T(8,128)S(1)}, u32[]{:S(2)}, u32[]{:S(2)}) %collective-permute-start.76) | collective-permute-done | bytes 98336 | tf_op jit(solution)/shard_map/ppermute | solution.py:286
  358.0 5.1 %collective-permute-done.52 = f32[1,2,96,128]{3,2,1,0:T(8,128)S(1)} collective-permute-done((f32[1,2,96,128]{3,2,1,0:T(8,128)S(1)}, f32[1,2,96,128]{3,2,1,0:T(8,128)S(1)}, u32[]{:S(2)}, u32[]{:S(2)}) %collective-permute-start.52) | collective-permute-done | bytes 98336 | tf_op jit(solution)/shard_map/ppermute | solution.py:286
  363.5 4.6 %collective-permute-done.77 = f32[1,96,128]{2,1,0:T(8,128)S(1)} collective-permute-done((f32[1,96,128]{2,1,0:T(8,128)S(1)}, f32[1,96,128]{2,1,0:T(8,128)S(1)}, u32[]{:S(2)}, u32[]{:S(2)}) %collective-permute-start.77) | collective-permute-done | bytes 49184 | tf_op jit(solution)/shard_map/ppermute | solution.py:286
  368.2 4.6 %collective-permute-done.78 = f32[2,96,128]{2,1,0:T(8,128)S(1)} collective-permute-done((f32[2,96,128]{2,1,0:T(8,128)S(1)}, f32[2,96,128]{2,1,0:T(8,128)S(1)}, u32[]{:S(2)}, u32[]{:S(2)}) %collective-permute-start.78) | collective-permute-done | bytes 98336 | tf_op jit(solution)/shard_map/ppermute | solution.py:286
  374.2 3.6 collective-permute-done.53
  379.9 3.7 collective-permute-done.54
  388.0 2.5 collective-permute-done.55
  392.4 13.0 %labels.7 = (f32[320,256]{1,0:T(8,128)S(1)}, f32[231,2048]{1,0:T(8,128)S(1)}) custom-call(s32[1]{0:T(128)} %bitcast.me_ref, bf16[320,4096]{1,0:T(8,128)(2,1)} %refs_0_.15, bf16[320,4096]{1,0:T(8,128)(2,1)} %refs_1_.15, bf16[320,256]{1,0:T(8,128)(2,1)S(1)} %get-tuple-element.56.refs_2_, bf16[320,32]{1,0:T(8,128)(2,1)S(1)} %get-tuple-element.57.refs_3_, ...), custom_call_target="tpu_custom_call" | custom-call | flops 7381975040 | bytes 4521984 | tf_op jit(solution)/shard_map/labels/pallas_call | solution.py:384
  405.4 13.2 %labels.6 = (f32[320,256]{1,0:T(8,128)S(1)}, f32[231,2048]{1,0:T(8,128)S(1)}) custom-call(s32[1]{0:T(128)} %bitcast.me_ref, bf16[320,4096]{1,0:T(8,128)(2,1)} %refs_0_.15, bf16[320,4096]{1,0:T(8,128)(2,1)} %refs_1_.15, bf16[320,256]{1,0:T(8,128)(2,1)S(1)} %get-tuple-element.56.refs_2_, bf16[320,32]{1,0:T(8,128)(2,1)S(1)} %get-tuple-element.57.refs_3_, ...), custom_call_target="tpu_custom_call" | custom-call | flops 7381975040 | bytes 4521984 | tf_op jit(solution)/shard_map/labels/pallas_call | solution.py:384
  (303 shorter events, 168.3 us)
Async XLA Ops:
  10.0 17.4 %collective-permute-start.40 = (f32[8,2,56,128]{3,2,1,0:T(8,128)}, f32[8,2,56,128]{3,2,1,0:T(8,128)}, u32[]{:S(2)}, u32[]{:S(2)}) collective-permute-start(f32[8,2,56,128]{3,2,1,0:T(8,128)} %bitcast.39), channel_id=1, source_target_pairs={{0,8},{2,10},{4,12},{6,14},{8,0},{10,2},{12,4},{14,6},{16,24},{18,... | collective-permute-start | bytes 1376264 | tf_op jit(solution)/shard_map/ppermute | solution.py:286
  13.0 23.4 %collective-permute-start.32 = (f32[8,2,80,128]{3,2,1,0:T(8,128)}, f32[8,2,80,128]{3,2,1,0:T(8,128)}, u32[]{:S(2)}, u32[]{:S(2)}) collective-permute-start(f32[8,2,80,128]{3,2,1,0:T(8,128)} %bitcast.32), channel_id=1, source_target_pairs={{0,4},{2,6},{4,0},{6,2},{8,12},{10,14},{12,8},{14,10},{16,20},{18,... | collective-permute-start | bytes 1966088 | tf_op jit(solution)/shard_map/ppermute | solution.py:286
  14.5 47.0 %collective-permute-start.24 = (f32[8,2,96,128]{3,2,1,0:T(8,128)}, f32[8,2,96,128]{3,2,1,0:T(8,128)}, u32[]{:S(2)}, u32[]{:S(2)}) collective-permute-start(f32[8,2,96,128]{3,2,1,0:T(8,128)} %bitcast.25), channel_id=1, source_target_pairs={{0,2},{2,0},{4,6},{6,4},{8,10},{10,8},{12,14},{14,12},{16,18},{18,... | collective-permute-start | bytes 2359304 | tf_op jit(solution)/shard_map/ppermute | solution.py:286
  23.2 11.7 %collective-permute-start.16 = (f32[8,2,56,128]{3,2,1,0:T(8,128)}, f32[8,2,56,128]{3,2,1,0:T(8,128)}, u32[]{:S(2)}, u32[]{:S(2)}) collective-permute-start(f32[8,2,56,128]{3,2,1,0:T(8,128)} %bitcast.18), channel_id=1, source_target_pairs={{0,8},{2,10},{4,12},{6,14},{8,0},{10,2},{12,4},{14,6},{16,24},{18,... | collective-permute-start | bytes 1376264 | tf_op jit(solution)/shard_map/ppermute | solution.py:286
  23.6 19.9 %collective-permute-start.8 = (f32[8,2,80,128]{3,2,1,0:T(8,128)}, f32[8,2,80,128]{3,2,1,0:T(8,128)}, u32[]{:S(2)}, u32[]{:S(2)}) collective-permute-start(f32[8,2,80,128]{3,2,1,0:T(8,128)} %bitcast.10), channel_id=1, source_target_pairs={{0,4},{2,6},{4,0},{6,2},{8,12},{10,14},{12,8},{14,10},{16,20},{18,... | collective-permute-start | bytes 1966088 | tf_op jit(solution)/shard_map/ppermute | solution.py:286
  27.4 53.9 %collective-permute-start = (f32[8,2,96,128]{3,2,1,0:T(8,128)S(1)}, f32[8,2,96,128]{3,2,1,0:T(8,128)S(1)}, u32[]{:S(2)}, u32[]{:S(2)}) collective-permute-start(f32[8,2,96,128]{3,2,1,0:T(8,128)S(1)} %bitcast.199), channel_id=1, source_target_pairs={{0,2},{2,0},{4,6},{6,4},{8,10},{10,8},{12,14},{14,12},{16,18},{18,... | collective-permute-start | bytes 2359304 | tf_op jit(solution)/shard_map/ppermute | solution.py:286
  34.9 22.1 %collective-permute-start.41 = (f32[4,2,56,128]{3,2,1,0:T(8,128)S(1)}, f32[4,2,56,128]{3,2,1,0:T(8,128)S(1)}, u32[]{:S(2)}, u32[]{:S(2)}) collective-permute-start(f32[4,2,56,128]{3,2,1,0:T(8,128)S(1)} %slice_add_fusion.10), channel_id=1, source_target_pairs={{0,2},{2,0},{4,6},{6,4},{8,10},{10,8},{12,14},{14,12},{16,18},{18,... | collective-permute-start | bytes 688136 | tf_op jit(solution)/shard_map/ppermute | solution.py:286
  36.4 23.7 %collective-permute-start.17 = (f32[4,2,56,128]{3,2,1,0:T(8,128)S(1)}, f32[4,2,56,128]{3,2,1,0:T(8,128)S(1)}, u32[]{:S(2)}, u32[]{:S(2)}) collective-permute-start(f32[4,2,56,128]{3,2,1,0:T(8,128)S(1)} %slice_add_fusion.11), channel_id=1, source_target_pairs={{0,2},{2,0},{4,6},{6,4},{8,10},{10,8},{12,14},{14,12},{16,18},{18,... | collective-permute-start | bytes 688136 | tf_op jit(solution)/shard_map/ppermute | solution.py:286
  43.6 56.4 %collective-permute-start.33 = (f32[4,2,80,128]{3,2,1,0:T(8,128)S(1)}, f32[4,2,80,128]{3,2,1,0:T(8,128)S(1)}, u32[]{:S(2)}, u32[]{:S(2)}) collective-permute-start(f32[4,2,80,128]{3,2,1,0:T(8,128)S(1)} %slice_add_fusion.6), channel_id=1, source_target_pairs={{0,8},{2,10},{4,12},{6,14},{8,0},{10,2},{12,4},{14,6},{16,24},{18,... | collective-permute-start | bytes 983048 | tf_op jit(solution)/shard_map/ppermute | solution.py:286
  57.0 44.7 %collective-permute-start.9 = (f32[4,2,80,128]{3,2,1,0:T(8,128)S(1)}, f32[4,2,80,128]{3,2,1,0:T(8,128)S(1)}, u32[]{:S(2)}, u32[]{:S(2)}) collective-permute-start(f32[4,2,80,128]{3,2,1,0:T(8,128)S(1)} %slice_add_fusion.7), channel_id=1, source_target_pairs={{0,8},{2,10},{4,12},{6,14},{8,0},{10,2},{12,4},{14,6},{16,24},{18,... | collective-permute-start | bytes 983048 | tf_op jit(solution)/shard_map/ppermute | solution.py:286
  64.9 47.2 %collective-permute-start.25 = (f32[4,2,96,128]{3,2,1,0:T(8,128)S(1)}, f32[4,2,96,128]{3,2,1,0:T(8,128)S(1)}, u32[]{:S(2)}, u32[]{:S(2)}) collective-permute-start(f32[4,2,96,128]{3,2,1,0:T(8,128)S(1)} %slice_add_fusion.2), channel_id=1, source_target_pairs={{0,4},{2,6},{4,0},{6,2},{8,12},{10,14},{12,8},{14,10},{16,20},{18,... | collective-permute-start | bytes 1179656 | tf_op jit(solution)/shard_map/ppermute | solution.py:286
  81.5 33.5 %collective-permute-start.1 = (f32[4,2,96,128]{3,2,1,0:T(8,128)S(1)}, f32[4,2,96,128]{3,2,1,0:T(8,128)S(1)}, u32[]{:S(2)}, u32[]{:S(2)}) collective-permute-start(f32[4,2,96,128]{3,2,1,0:T(8,128)S(1)} %slice_add_fusion.3), channel_id=1, source_target_pairs={{0,4},{2,6},{4,0},{6,2},{8,12},{10,14},{12,8},{14,10},{16,20},{18,... | collective-permute-start | bytes 1179656 | tf_op jit(solution)/shard_map/ppermute | solution.py:286
  98.6 77.9 %collective-permute-start.46 = (f32[4,56,128]{2,1,0:T(8,128)S(1)}, f32[4,56,128]{2,1,0:T(8,128)S(1)}, u32[]{:S(2)}, u32[]{:S(2)}) collective-permute-start(f32[4,56,128]{2,1,0:T(8,128)S(1)} %pad_maximum_fusion.22), channel_id=1, source_target_pairs={{0,2},{2,0},{4,6},{6,4},{8,10},{10,8},{12,14},{14,12},{16,18},{18,... | collective-permute-start | bytes 344072 | tf_op jit(solution)/shard_map/ppermute | solution.py:286
  107.1 90.5 %collective-permute-start.23 = (f32[8,56,128]{2,1,0:T(8,128)S(1)}, f32[8,56,128]{2,1,0:T(8,128)S(1)}, u32[]{:S(2)}, u32[]{:S(2)}) collective-permute-start(f32[8,56,128]{2,1,0:T(8,128)S(1)} %pad_maximum_fusion.9), channel_id=1, source_target_pairs={{0,8},{2,10},{4,12},{6,14},{8,0},{10,2},{12,4},{14,6},{16,24},{18,... | collective-permute-start | bytes 688136 | tf_op jit(solution)/shard_map/ppermute | solution.py:286
  115.0 23.8 %collective-permute-start.26 = (f32[2,2,96,128]{3,2,1,0:T(8,128)S(1)}, f32[2,2,96,128]{3,2,1,0:T(8,128)S(1)}, u32[]{:S(2)}, u32[]{:S(2)}) collective-permute-start(f32[2,2,96,128]{3,2,1,0:T(8,128)S(1)} %slice_add_fusion.16), channel_id=1, source_target_pairs={{0,8},{2,10},{4,12},{6,14},{8,0},{10,2},{12,4},{14,6},{16,24},{18,... | collective-permute-start | bytes 589832 | tf_op jit(solution)/shard_map/ppermute | solution.py:286
  116.4 23.8 %collective-permute-start.2 = (f32[2,2,96,128]{3,2,1,0:T(8,128)S(1)}, f32[2,2,96,128]{3,2,1,0:T(8,128)S(1)}, u32[]{:S(2)}, u32[]{:S(2)}) collective-permute-start(f32[2,2,96,128]{3,2,1,0:T(8,128)S(1)} %slice_add_fusion.18), channel_id=1, source_target_pairs={{0,8},{2,10},{4,12},{6,14},{8,0},{10,2},{12,4},{14,6},{16,24},{18,... | collective-permute-start | bytes 589832 | tf_op jit(solution)/shard_map/ppermute | solution.py:286
  137.1 28.0 %collective-permute-start.38 = (f32[4,80,128]{2,1,0:T(8,128)S(1)}, f32[4,80,128]{2,1,0:T(8,128)S(1)}, u32[]{:S(2)}, u32[]{:S(2)}) collective-permute-start(f32[4,80,128]{2,1,0:T(8,128)S(1)} %pad_maximum_fusion.18), channel_id=1, source_target_pairs={{0,8},{2,10},{4,12},{6,14},{8,0},{10,2},{12,4},{14,6},{16,24},{18,... | collective-permute-start | bytes 491528 | tf_op jit(solution)/shard_map/ppermute | solution.py:286
  138.8 39.9 %collective-permute-start.14 = (f32[4,80,128]{2,1,0:T(8,128)S(1)}, f32[4,80,128]{2,1,0:T(8,128)S(1)}, u32[]{:S(2)}, u32[]{:S(2)}) collective-permute-start(f32[4,80,128]{2,1,0:T(8,128)S(1)} %pad_maximum_fusion.17), channel_id=1, source_target_pairs={{0,8},{2,10},{4,12},{6,14},{8,0},{10,2},{12,4},{14,6},{16,24},{18,... | collective-permute-start | bytes 491528 | tf_op jit(solution)/shard_map/ppermute | solution.py:286
  156.5 7.0 %collective-permute-start.29 = (f32[2,96,128]{2,1,0:T(8,128)S(1)}, f32[2,96,128]{2,1,0:T(8,128)S(1)}, u32[]{:S(2)}, u32[]{:S(2)}) collective-permute-start(f32[2,96,128]{2,1,0:T(8,128)S(1)} %pad_maximum_fusion.26), channel_id=1, source_target_pairs={{0,8},{2,10},{4,12},{6,14},{8,0},{10,2},{12,4},{14,6},{16,24},{18,... | collective-permute-start | bytes 294920 | tf_op jit(solution)/shard_map/ppermute | solution.py:286
  168.5 16.6 %collective-permute-start.39 = (f32[8,80,128]{2,1,0:T(8,128)S(1)}, f32[8,80,128]{2,1,0:T(8,128)S(1)}, u32[]{:S(2)}, u32[]{:S(2)}) collective-permute-start(f32[8,80,128]{2,1,0:T(8,128)S(1)} %pad_maximum_fusion.6), channel_id=1, source_target_pairs={{0,4},{2,6},{4,0},{6,2},{8,12},{10,14},{12,8},{14,10},{16,20},{18,... | collective-permute-start | bytes 983048 | tf_op jit(solution)/shard_map/ppermute | solution.py:286
  175.5 9.6 %collective-permute-start.31 = (f32[8,96,128]{2,1,0:T(8,128)S(1)}, f32[8,96,128]{2,1,0:T(8,128)S(1)}, u32[]{:S(2)}, u32[]{:S(2)}) collective-permute-start(f32[8,96,128]{2,1,0:T(8,128)S(1)} %pad_maximum_fusion.2), channel_id=1, source_target_pairs={{0,2},{2,0},{4,6},{6,4},{8,10},{10,8},{12,14},{14,12},{16,18},{18,... | collective-permute-start | bytes 1179656 | tf_op jit(solution)/shard_map/ppermute | solution.py:286
  182.3 15.3 %collective-permute-start.15 = (f32[8,80,128]{2,1,0:T(8,128)S(1)}, f32[8,80,128]{2,1,0:T(8,128)S(1)}, u32[]{:S(2)}, u32[]{:S(2)}) collective-permute-start(f32[8,80,128]{2,1,0:T(8,128)S(1)} %pad_maximum_fusion.5), channel_id=1, source_target_pairs={{0,4},{2,6},{4,0},{6,2},{8,12},{10,14},{12,8},{14,10},{16,20},{18,... | collective-permute-start | bytes 983048 | tf_op jit(solution)/shard_map/ppermute | solution.py:286
  184.8 12.8 %collective-permute-start.7 = (f32[8,96,128]{2,1,0:T(8,128)S(1)}, f32[8,96,128]{2,1,0:T(8,128)S(1)}, u32[]{:S(2)}, u32[]{:S(2)}) collective-permute-start(f32[8,96,128]{2,1,0:T(8,128)S(1)} %pad_maximum_fusion.1), channel_id=1, source_target_pairs={{0,2},{2,0},{4,6},{6,4},{8,10},{10,8},{12,14},{14,12},{16,18},{18,... | collective-permute-start | bytes 1179656 | tf_op jit(solution)/shard_map/ppermute | solution.py:286
  217.8 13.4 %collective-permute-start.89 = (f32[8,2,56,128]{3,2,1,0:T(8,128)S(1)}, f32[8,2,56,128]{3,2,1,0:T(8,128)S(1)}, u32[]{:S(2)}, u32[]{:S(2)}) collective-permute-start(f32[8,2,56,128]{3,2,1,0:T(8,128)S(1)} %bitcast.204), channel_id=1, source_target_pairs={{0,8},{2,10},{4,12},{6,14},{8,0},{10,2},{12,4},{14,6},{16,24},{18,... | collective-permute-start | bytes 1376264 | tf_op jit(solution)/shard_map/ppermute | solution.py:286
  224.7 15.5 %collective-permute-start.65 = (f32[8,2,56,128]{3,2,1,0:T(8,128)S(1)}, f32[8,2,56,128]{3,2,1,0:T(8,128)S(1)}, u32[]{:S(2)}, u32[]{:S(2)}) collective-permute-start(f32[8,2,56,128]{3,2,1,0:T(8,128)S(1)} %bitcast.205), channel_id=1, source_target_pairs={{0,8},{2,10},{4,12},{6,14},{8,0},{10,2},{12,4},{14,6},{16,24},{18,... | collective-permute-start | bytes 1376264 | tf_op jit(solution)/shard_map/ppermute | solution.py:286
  225.2 17.6 %collective-permute-start.81 = (f32[8,2,80,128]{3,2,1,0:T(8,128)S(1)}, f32[8,2,80,128]{3,2,1,0:T(8,128)S(1)}, u32[]{:S(2)}, u32[]{:S(2)}) collective-permute-start(f32[8,2,80,128]{3,2,1,0:T(8,128)S(1)} %bitcast.202), channel_id=1, source_target_pairs={{0,4},{2,6},{4,0},{6,2},{8,12},{10,14},{12,8},{14,10},{16,20},{18,... | collective-permute-start | bytes 1966088 | tf_op jit(solution)/shard_map/ppermute | solution.py:286
  225.8 47.2 %collective-permute-start.73 = (f32[8,2,96,128]{3,2,1,0:T(8,128)S(1)}, f32[8,2,96,128]{3,2,1,0:T(8,128)S(1)}, u32[]{:S(2)}, u32[]{:S(2)}) collective-permute-start(f32[8,2,96,128]{3,2,1,0:T(8,128)S(1)} %bitcast.200), channel_id=1, source_target_pairs={{0,2},{2,0},{4,6},{6,4},{8,10},{10,8},{12,14},{14,12},{16,18},{18,... | collective-permute-start | bytes 2359304 | tf_op jit(solution)/shard_map/ppermute | solution.py:286
  228.1 27.4 %collective-permute-start.57 = (f32[8,2,80,128]{3,2,1,0:T(8,128)S(1)}, f32[8,2,80,128]{3,2,1,0:T(8,128)S(1)}, u32[]{:S(2)}, u32[]{:S(2)}) collective-permute-start(f32[8,2,80,128]{3,2,1,0:T(8,128)S(1)} %bitcast.203), channel_id=1, source_target_pairs={{0,4},{2,6},{4,0},{6,2},{8,12},{10,14},{12,8},{14,10},{16,20},{18,... | collective-permute-start | bytes 1966088 | tf_op jit(solution)/shard_map/ppermute | solution.py:286
  231.1 42.4 %collective-permute-start.49 = (f32[8,2,96,128]{3,2,1,0:T(8,128)S(1)}, f32[8,2,96,128]{3,2,1,0:T(8,128)S(1)}, u32[]{:S(2)}, u32[]{:S(2)}) collective-permute-start(f32[8,2,96,128]{3,2,1,0:T(8,128)S(1)} %bitcast.201), channel_id=1, source_target_pairs={{0,2},{2,0},{4,6},{6,4},{8,10},{10,8},{12,14},{14,12},{16,18},{18,... | collective-permute-start | bytes 2359304 | tf_op jit(solution)/shard_map/ppermute | solution.py:286
  240.2 28.0 %collective-permute-start.90 = (f32[4,2,56,128]{3,2,1,0:T(8,128)S(1)}, f32[4,2,56,128]{3,2,1,0:T(8,128)S(1)}, u32[]{:S(2)}, u32[]{:S(2)}) collective-permute-start(f32[4,2,56,128]{3,2,1,0:T(8,128)S(1)} %slice_add_fusion.8), channel_id=1, source_target_pairs={{0,2},{2,0},{4,6},{6,4},{8,10},{10,8},{12,14},{14,12},{16,18},{18,... | collective-permute-start | bytes 688136 | tf_op jit(solution)/shard_map/ppermute | solution.py:286
  242.8 28.5 %collective-permute-start.66 = (f32[4,2,56,128]{3,2,1,0:T(8,128)S(1)}, f32[4,2,56,128]{3,2,1,0:T(8,128)S(1)}, u32[]{:S(2)}, u32[]{:S(2)}) collective-permute-start(f32[4,2,56,128]{3,2,1,0:T(8,128)S(1)} %slice_add_fusion.9), channel_id=1, source_target_pairs={{0,2},{2,0},{4,6},{6,4},{8,10},{10,8},{12,14},{14,12},{16,18},{18,... | collective-permute-start | bytes 688136 | tf_op jit(solution)/shard_map/ppermute | solution.py:286
  255.5 56.2 %collective-permute-start.82 = (f32[4,2,80,128]{3,2,1,0:T(8,128)S(1)}, f32[4,2,80,128]{3,2,1,0:T(8,128)S(1)}, u32[]{:S(2)}, u32[]{:S(2)}) collective-permute-start(f32[4,2,80,128]{3,2,1,0:T(8,128)S(1)} %slice_add_fusion.4), channel_id=1, source_target_pairs={{0,8},{2,10},{4,12},{6,14},{8,0},{10,2},{12,4},{14,6},{16,24},{18,... | collective-permute-start | bytes 983048 | tf_op jit(solution)/shard_map/ppermute | solution.py:286
  268.2 43.8 %collective-permute-start.58 = (f32[4,2,80,128]{3,2,1,0:T(8,128)S(1)}, f32[4,2,80,128]{3,2,1,0:T(8,128)S(1)}, u32[]{:S(2)}, u32[]{:S(2)}) collective-permute-start(f32[4,2,80,128]{3,2,1,0:T(8,128)S(1)} %slice_add_fusion.5), channel_id=1, source_target_pairs={{0,8},{2,10},{4,12},{6,14},{8,0},{10,2},{12,4},{14,6},{16,24},{18,... | collective-permute-start | bytes 983048 | tf_op jit(solution)/shard_map/ppermute | solution.py:286
  273.5 46.7 %collective-permute-start.74 = (f32[4,2,96,128]{3,2,1,0:T(8,128)S(1)}, f32[4,2,96,128]{3,2,1,0:T(8,128)S(1)}, u32[]{:S(2)}, u32[]{:S(2)}) collective-permute-start(f32[4,2,96,128]{3,2,1,0:T(8,128)S(1)} %slice_add_fusion), channel_id=1, source_target_pairs={{0,4},{2,6},{4,0},{6,2},{8,12},{10,14},{12,8},{14,10},{16,20},{18,... | collective-permute-start | bytes 1179656 | tf_op jit(solution)/shard_map/ppermute | solution.py:286
  277.3 45.8 %collective-permute-start.50 = (f32[4,2,96,128]{3,2,1,0:T(8,128)S(1)}, f32[4,2,96,128]{3,2,1,0:T(8,128)S(1)}, u32[]{:S(2)}, u32[]{:S(2)}) collective-permute-start(f32[4,2,96,128]{3,2,1,0:T(8,128)S(1)} %slice_add_fusion.1), channel_id=1, source_target_pairs={{0,4},{2,6},{4,0},{6,2},{8,12},{10,14},{12,8},{14,10},{16,20},{18,... | collective-permute-start | bytes 1179656 | tf_op jit(solution)/shard_map/ppermute | solution.py:286
  311.7 73.1 %collective-permute-start.71 = (f32[4,56,128]{2,1,0:T(8,128)S(1)}, f32[4,56,128]{2,1,0:T(8,128)S(1)}, u32[]{:S(2)}, u32[]{:S(2)}) collective-permute-start(f32[4,56,128]{2,1,0:T(8,128)S(1)} %pad_maximum_fusion.23), channel_id=1, source_target_pairs={{0,2},{2,0},{4,6},{6,4},{8,10},{10,8},{12,14},{14,12},{16,18},{18,... | collective-permute-start | bytes 344072 | tf_op jit(solution)/shard_map/ppermute | solution.py:286
  318.3 73.3 %collective-permute-start.96 = (f32[8,56,128]{2,1,0:T(8,128)S(1)}, f32[8,56,128]{2,1,0:T(8,128)S(1)}, u32[]{:S(2)}, u32[]{:S(2)}) collective-permute-start(f32[8,56,128]{2,1,0:T(8,128)S(1)} %pad_maximum_fusion.12), channel_id=1, source_target_pairs={{0,8},{2,10},{4,12},{6,14},{8,0},{10,2},{12,4},{14,6},{16,24},{18,... | collective-permute-start | bytes 688136 | tf_op jit(solution)/shard_map/ppermute | solution.py:286
  320.1 7.0 %collective-permute-start.84 = (f32[1,2,80,128]{3,2,1,0:T(8,128)S(1)}, f32[1,2,80,128]{3,2,1,0:T(8,128)S(1)}, u32[]{:S(2)}, u32[]{:S(2)}) collective-permute-start(f32[1,2,80,128]{3,2,1,0:T(8,128)S(1)} %slice_add_fusion.60), channel_id=1, source_target_pairs={{0,16},{2,18},{4,20},{6,22},{8,24},{10,26},{12,28},{14,30},{16,0},... | collective-permute-start | bytes 245768 | tf_op jit(solution)/shard_map/ppermute | solution.py:286
  320.2 7.7 %collective-permute-start.60 = (f32[1,2,80,128]{3,2,1,0:T(8,128)S(1)}, f32[1,2,80,128]{3,2,1,0:T(8,128)S(1)}, u32[]{:S(2)}, u32[]{:S(2)}) collective-permute-start(f32[1,2,80,128]{3,2,1,0:T(8,128)S(1)} %slice_add_fusion.66), channel_id=1, source_target_pairs={{0,16},{2,18},{4,20},{6,22},{8,24},{10,26},{12,28},{14,30},{16,0},... | collective-permute-start | bytes 245768 | tf_op jit(solution)/shard_map/ppermute | solution.py:286
  323.1 25.1 %collective-permute-start.75 = (f32[2,2,96,128]{3,2,1,0:T(8,128)S(1)}, f32[2,2,96,128]{3,2,1,0:T(8,128)S(1)}, u32[]{:S(2)}, u32[]{:S(2)}) collective-permute-start(f32[2,2,96,128]{3,2,1,0:T(8,128)S(1)} %slice_add_fusion.12), channel_id=1, source_target_pairs={{0,8},{2,10},{4,12},{6,14},{8,0},{10,2},{12,4},{14,6},{16,24},{18,... | collective-permute-start | bytes 589832 | tf_op jit(solution)/shard_map/ppermute | solution.py:286
  327.1 23.1 %collective-permute-start.51 = (f32[2,2,96,128]{3,2,1,0:T(8,128)S(1)}, f32[2,2,96,128]{3,2,1,0:T(8,128)S(1)}, u32[]{:S(2)}, u32[]{:S(2)}) collective-permute-start(f32[2,2,96,128]{3,2,1,0:T(8,128)S(1)} %slice_add_fusion.14), channel_id=1, source_target_pairs={{0,8},{2,10},{4,12},{6,14},{8,0},{10,2},{12,4},{14,6},{16,24},{18,... | collective-permute-start | bytes 589832 | tf_op jit(solution)/shard_map/ppermute | solution.py:286
  348.0 25.2 %collective-permute-start.87 = (f32[4,80,128]{2,1,0:T(8,128)S(1)}, f32[4,80,128]{2,1,0:T(8,128)S(1)}, u32[]{:S(2)}, u32[]{:S(2)}) collective-permute-start(f32[4,80,128]{2,1,0:T(8,128)S(1)} %pad_maximum_fusion.20), channel_id=1, source_target_pairs={{0,8},{2,10},{4,12},{6,14},{8,0},{10,2},{12,4},{14,6},{16,24},{18,... | collective-permute-start | bytes 491528 | tf_op jit(solution)/shard_map/ppermute | solution.py:286
  348.3 37.7 %collective-permute-start.63 = (f32[4,80,128]{2,1,0:T(8,128)S(1)}, f32[4,80,128]{2,1,0:T(8,128)S(1)}, u32[]{:S(2)}, u32[]{:S(2)}) collective-permute-start(f32[4,80,128]{2,1,0:T(8,128)S(1)} %pad_maximum_fusion.19), channel_id=1, source_target_pairs={{0,8},{2,10},{4,12},{6,14},{8,0},{10,2},{12,4},{14,6},{16,24},{18,... | collective-permute-start | bytes 491528 | tf_op jit(solution)/shard_map/ppermute | solution.py:286
  377.8 14.6 %collective-permute-start.88 = (f32[8,80,128]{2,1,0:T(8,128)S(1)}, f32[8,80,128]{2,1,0:T(8,128)S(1)}, u32[]{:S(2)}, u32[]{:S(2)}) collective-permute-start(f32[8,80,128]{2,1,0:T(8,128)S(1)} %pad_maximum_fusion.8), channel_id=1, source_target_pairs={{0,4},{2,6},{4,0},{6,2},{8,12},{10,14},{12,8},{14,10},{16,20},{18,... | collective-permute-start | bytes 983048 | tf_op jit(solution)/shard_map/ppermute | solution.py:286
  383.6 8.8 %collective-permute-start.80 = (f32[8,96,128]{2,1,0:T(8,128)S(1)}, f32[8,96,128]{2,1,0:T(8,128)S(1)}, u32[]{:S(2)}, u32[]{:S(2)}) collective-permute-start(f32[8,96,128]{2,1,0:T(8,128)S(1)} %pad_maximum_fusion.4), channel_id=1, source_target_pairs={{0,2},{2,0},{4,6},{6,4},{8,10},{10,8},{12,14},{14,12},{16,18},{18,... | collective-permute-start | bytes 1179656 | tf_op jit(solution)/shard_map/ppermute | solution.py:286
  386.0 19.4 %collective-permute-start.72 = (f32[8,56,128]{2,1,0:T(8,128)S(1)}, f32[8,56,128]{2,1,0:T(8,128)S(1)}, u32[]{:S(2)}, u32[]{:S(2)}) collective-permute-start(f32[8,56,128]{2,1,0:T(8,128)S(1)} %pad_maximum_fusion.11), channel_id=1, source_target_pairs={{0,8},{2,10},{4,12},{6,14},{8,0},{10,2},{12,4},{14,6},{16,24},{18,... | collective-permute-start | bytes 688136 | tf_op jit(solution)/shard_map/ppermute | solution.py:286
  390.5 14.9 %collective-permute-start.64 = (f32[8,80,128]{2,1,0:T(8,128)S(1)}, f32[8,80,128]{2,1,0:T(8,128)S(1)}, u32[]{:S(2)}, u32[]{:S(2)}) collective-permute-start(f32[8,80,128]{2,1,0:T(8,128)S(1)} %pad_maximum_fusion.7), channel_id=1, source_target_pairs={{0,4},{2,6},{4,0},{6,2},{8,12},{10,14},{12,8},{14,10},{16,20},{18,... | collective-permute-start | bytes 983048 | tf_op jit(solution)/shard_map/ppermute | solution.py:286
  391.7 13.8 %collective-permute-start.56 = (f32[8,96,128]{2,1,0:T(8,128)S(1)}, f32[8,96,128]{2,1,0:T(8,128)S(1)}, u32[]{:S(2)}, u32[]{:S(2)}) collective-permute-start(f32[8,96,128]{2,1,0:T(8,128)S(1)} %pad_maximum_fusion.3), channel_id=1, source_target_pairs={{0,2},{2,0},{4,6},{6,4},{8,10},{10,8},{12,14},{14,12},{16,18},{18,... | collective-permute-start | bytes 1179656 | tf_op jit(solution)/shard_map/ppermute | solution.py:286
  (64 other events, 531.2 us)

commit v2 on v1

--- a/solution.py
+++ b/solution.py
@@ -9,7 +9,7 @@
 from jax.sharding import PartitionSpec as P
 
 ALTS = 2
-WAVES = 2
+WAVES = 1
 LANES = 128
 VMEM_LIMIT = 48 * 1024 * 1024
 
@@ -148,14 +148,6 @@
     write_features(lab, left_ref, right_ref, *outs)
 
 
-def theta_pair(refs, spans, first, second):
-    columns = []
-    for piece in (first, second):
-        rows = [ref[piece] for ref in refs]
-        columns.append(jnp.concatenate(rows, axis=0))
-    return jnp.concatenate(columns, axis=1)
-
-
 def grad_kernel(plan, from_coeffs, me_ref, *refs):
     n, half, parts = plan["n"], plan["half"], plan["parts"]
     flux_ref, ivar_ref, feat_ref, featt_ref, sqt_ref = refs[:5]
@@ -167,43 +159,25 @@
     sends, keeps = refs[: len(parts)], refs[len(parts) :]
     low = me_ref[0] & (half - 1)
     feat = feat_ref[...]
-    for pair in range(half // 2):
-        spots = [pl.multiple_of((r ^ low) * LANES, LANES) for r in (2 * pair, 2 * pair + 1)]
-
-        def wide(ref):
-            return jnp.concatenate([ref[:, pl.ds(spot, LANES)] for spot in spots], axis=1)
-
-        flux = wide(flux_ref)
-        ivar = wide(ivar_ref)
+    width = plan["lanes"]
+    for r in range(half):
+        lanes = pl.ds(pl.multiple_of((r ^ low) * width, width), width)
+        flux = flux_ref[:, lanes]
+        ivar = ivar_ref[:, lanes]
         if from_coeffs:
-            theta = wide(coeffs_ref).astype(jnp.bfloat16)
-            model = mm(feat[:, : theta.shape[0]], theta)
+            theta = coeffs_ref[:, lanes].astype(jnp.bfloat16)
         else:
-            theta = jnp.concatenate(
-                [
-                    jnp.concatenate(
-                        [
-                            theta_piece(plan, thetas, part, r)
-                            for part in range(len(parts))
-                        ],
-                        axis=0,
-                    )
-                    for r in (2 * pair, 2 * pair + 1)
-                ],
-                axis=1,
-            ).astype(jnp.bfloat16)
-            model = mm(feat[:, : theta.shape[0]], theta)
+            theta = theta_piece(plan, thetas, r).astype(jnp.bfloat16)
+        model = mm(feat[:, : theta.shape[0]], theta)
         weighted = (ivar.astype(jnp.float32) * (flux.astype(jnp.float32) - model)).astype(jnp.bfloat16)
         grad = mm(featt_ref[...], weighted)
         curv = mm(sqt_ref[...], ivar)
-        for side, r in enumerate((2 * pair, 2 * pair + 1)):
-            lanes = slice(side * LANES, (side + 1) * LANES)
-            for index, part in enumerate(parts):
-                upper, spot = place(part["order"], r)
-                target = sends[index] if upper else keeps[index]
-                rows = slice(part["start"], part["start"] + part["rows"])
-                target[spot, 0, 0] = grad[rows, lanes]
-                target[spot, 0, 1] = curv[rows, lanes]
+        for index, part in enumerate(parts):
+            upper, spot = place(part["order"], r)
+            target = sends[index] if upper else keeps[index]
+            rows = slice(part["start"], part["start"] + part["rows"])
+            target[spot, 0, 0] = grad[rows]
+            target[spot, 0, 1] = curv[rows]
 
 
 def place(order, r):
@@ -214,9 +188,12 @@
     return bits[0], spot
 
 
-def theta_piece(plan, thetas, part, r):
-    upper, spot = place(plan["parts"][part]["order"], r)
-    return thetas[2 * part + upper][spot, 0]
+def theta_piece(plan, thetas, r):
+    rows = []
+    for index, part in enumerate(plan["parts"]):
+        upper, spot = place(part["order"], r)
+        rows.append(thetas[2 * index + upper][spot, 0])
+    return jnp.concatenate(rows, axis=0)
 
 
 def label_kernel(plan, count, last, me_ref, *refs):
@@ -239,25 +216,17 @@
         squares_ref[...] = jnp.zeros_like(squares_ref)
 
     feat = feat_ref[...]
-    for pair in range(half // 2):
-        spots = [pl.multiple_of((r ^ low) * LANES, LANES) for r in (2 * pair, 2 * pair + 1)]
-
-        def wide(ref):
-            return jnp.concatenate([ref[:, pl.ds(spot, LANES)] for spot in spots], axis=1)
-
-        columns = []
-        for r, spot in zip((2 * pair, 2 * pair + 1), spots):
-            column = jnp.concatenate(
-                [theta_piece(plan, thetas, part, r) for part in range(len(parts))], axis=0
-            )
-            if last:
-                new_ref[:, pl.ds(spot, LANES)] = column[: new_ref.shape[0]]
-            columns.append(column)
-        theta = jnp.concatenate(columns, axis=1).astype(jnp.bfloat16)
-        ivar = wide(ivar_ref).astype(jnp.float32)
+    width = plan["lanes"]
+    for r in range(half):
+        lanes = pl.ds(pl.multiple_of((r ^ low) * width, width), width)
+        column = theta_piece(plan, thetas, r)
+        if last:
+            new_ref[:, lanes] = column[: new_ref.shape[0]]
+        theta = column.astype(jnp.bfloat16)
+        ivar = ivar_ref[:, lanes].astype(jnp.float32)
         iv_ref[...] = ivar
         model = mm(feat[:, : theta.shape[0]], theta)
-        weighted = (ivar * (wide(flux_ref).astype(jnp.float32) - model)).astype(jnp.bfloat16)
+        weighted = (ivar * (flux_ref[:, lanes].astype(jnp.float32) - model)).astype(jnp.bfloat16)
         dots_ref[...] += lax.dot_general(
             weighted, theta, (((1,), (1,)), ((), ())), preferred_element_type=jnp.float32
         )
@@ -265,7 +234,7 @@
         for label in range(count):
             jac = mm(lab1_ref[...], blocks[label * rows : (label + 1) * rows])
             term = jac * jac * iv_ref[...]
-            squares_ref[label] += term[:, :LANES] + term[:, LANES:]
+            squares_ref[label] += sum(term[:, at : at + LANES] for at in range(0, width, LANES))
 
     @pl.when(step == pl.num_programs(0) - 1)
     def _():
@@ -300,7 +269,8 @@
     select = jnp.asarray(select, jnp.bfloat16)
     me = lax.axis_index("star")
     me_vec = me.astype(jnp.int32).reshape(1)
-    block = half * LANES
+    width = plan["lanes"]
+    block = half * width
     params = pltpu.CompilerParams(vmem_limit_bytes=VMEM_LIMIT)
     whole = pl.BlockSpec(memory_space=pltpu.VMEM)
 
@@ -332,10 +302,10 @@
         return pl.BlockSpec(array.shape, lambda step, me: (0,) * array.ndim)
 
     def theta_spec(part):
-        return pl.BlockSpec((half // 2, 1, part["rows"], LANES), lambda step, me: (0, step, 0, 0))
+        return pl.BlockSpec((half // 2, 1, part["rows"], width), lambda step, me: (0, step, 0, 0))
 
     def grad_call(wave, thetas):
-        specs = [pixel_spec(stars, wave)] * 2 + [fixed(feat), fixed(featt[:height]), fixed(sqt[:height])]
+        specs = [pixel_spec(stars, wave)] * 2 + [fixed(feat), fixed(featt), fixed(sqt)]
         operands = [flux, inv_var, feat, featt, sqt]
         if thetas is None:
             specs.append(pixel_spec(features, wave))
@@ -345,10 +315,10 @@
                 specs += [theta_spec(part)] * 2
                 operands += list(arrays)
         shapes = [
-            jax.ShapeDtypeStruct((half // 2, 2, 2, part["rows"], LANES), jnp.float32) for part in parts
+            jax.ShapeDtypeStruct((half // 2, 2, 2, part["rows"], width), jnp.float32) for part in parts
         ] * 2
         out_specs = [
-            pl.BlockSpec((half // 2, 1, 2, part["rows"], LANES), lambda step, me: (0, step, 0, 0, 0))
+            pl.BlockSpec((half // 2, 1, 2, part["rows"], width), lambda step, me: (0, step, 0, 0, 0))
             for part in parts
         ] * 2
         outs = pl.pallas_call(
@@ -392,7 +362,7 @@
                 scratch_shapes=[
                     pltpu.VMEM((stars, height), jnp.float32),
                     pltpu.VMEM((count, stars, LANES), jnp.float32),
-                    pltpu.VMEM((stars, 2 * LANES), jnp.float32),
+                    pltpu.VMEM((stars, width), jnp.float32),
                 ],
             ),
             compiler_params=params,
@@ -408,7 +378,7 @@
     base = jnp.pad(
         jnp.stack(
             [
-                lax.dynamic_slice(coeffs, (0, (wave * n + me) * LANES), (features, LANES))
+                lax.dynamic_slice(coeffs, (0, (wave * n + me) * width), (features, width))
                 for wave in range(WAVES)
             ]
         ),
@@ -462,7 +432,7 @@
             name="update",
         )(lab, sums, there, left, right)
         lab = new_lab
-    return jnp.concatenate(news, axis=1), lab[:, 1 : 1 + count]
+    return jnp.concatenate(news, axis=1) if WAVES > 1 else news[0], lab[:, 1 : 1 + count]
 
 
 def make_plan(mesh, flux, coeffs):
@@ -472,11 +442,10 @@
     pixels = flux.shape[1] // mesh.shape["pix"]
     if n != 1 << bits or bits < 4 or mesh.shape["pix"] != 2:
         return None
-    if pixels != WAVES * n * LANES or stars % 16:
+    if pixels % (WAVES * n * LANES) or stars % 16:
         return None
     height = round_up(coeffs.shape[0], 8)
-    first = round_up(int(0.4 * height), 16)
-    second = round_up(int(0.34 * height), 16)
+    first = second = round_up(height // 3, 16)
     cuts = [0, first, first + second, height]
     rest = list(range(3, bits))
     orders = [[0, 1, 2] + rest, [1, 2, 0] + rest, [2, 0, 1] + rest]
@@ -487,6 +456,7 @@
         "n": n,
         "bits": bits,
         "half": n // 2,
+        "lanes": pixels // (WAVES * n),
         "parts": parts,
         "padded": round_up(coeffs.shape[0], 256),
         "swap": [(0, 1), (1, 0)],

time: 431 us -> 316 us (0.73); the launches traced: 423 us -> 315 us
  starting transfers between devices: 117 us -> 51.2 us
  waiting for transfers between devices: 197 us -> 176 us
  Pallas kernels: 75.1 us -> 65.3 us
  other arithmetic: 22.6 us -> 13.6 us
    ppermute x96 -> x48, starting transfers between devices: 117 us -> 51.1 us  [exchange(): return lax.ppermute(value, 'star', [(d, d ^ 1 << bit) for d in range(n)])]
    ppermute x96 -> x48, waiting for transfers between devices: 196 us -> 173 us  [exchange(): return lax.ppermute(value, 'star', [(d, d ^ 1 << bit) for d in range(n)])]
    pallas_call x4 -> x2, Pallas kernels: 51.2 us -> 44.3 us  [label_call(): pl.pallas_call(functools.partial(label_kernel, plan, count, last), out_sh...]
    add x36 -> x18, other arithmetic: 14.7 us -> 9.73 us  [pieces_device(): outgoing = sum((array[size:2 * size] for array in kept))]
    pallas_call x4 -> x2, Pallas kernels: 21.6 us -> 18.7 us  [grad_call(): pl.pallas_call(functools.partial(grad_kernel, plan, thetas is None), out_...]
  transfers between devices with their start and end apart: 98 -> 50, of which waited for: 61 -> 38; matrix products, arithmetic and copies ran while one was open for 6% -> 6% of each run, Pallas kernels for 9% -> 0%
where the time goes in v2:
time: 316 us; the launch traced here: 315 us
  waiting for transfers between devices  176 us (56%)
  Pallas kernels  65.3 us (21%)
  starting transfers between devices  51.2 us (16%)
  other arithmetic  13.6 us (4%)
  local copies, waits for them, and re-layouts  8.04 us (3%)
    ppermute x48, waiting for transfers between devices, exchange(): return lax.ppermute(value, 'star', [(d, d ^ 1 << bit) for d in range(n)])  173 us
    ppermute x48, starting transfers between devices, exchange(): return lax.ppermute(value, 'star', [(d, d ^ 1 << bit) for d in range(n)])  51.1 us
    pallas_call x2, Pallas kernels, label_call(): pl.pallas_call(functools.partial(label_kernel, plan, count, last), out_sh...  44.3 us
    pallas_call x2, Pallas kernels, grad_call(): pl.pallas_call(functools.partial(grad_kernel, plan, thetas is None), out_...  18.7 us
    add x18, other arithmetic, pieces_device(): outgoing = sum((array[size:2 * size] for array in kept))  9.73 us
  transfers between devices with their start and end apart: 50, of which 38 were waited for; matrix products, arithmetic and copies ran while one was open for 6% of the time, Pallas kernels for 0%

profile of v2, /device:TPU:0, one launch (start us, length us, event | category | flops | bytes accessed | tf_op | source)
XLA Modules:
  0.0 315.4 jit_solution(2401241423467189940)
XLA Ops:
  3.6 9.3 %gradient.2 = (f32[4,2,2,80,256]{4,3,2,1,0:T(8,128)S(1)}, f32[4,2,2,80,256]{4,3,2,1,0:T(8,128)S(1)}, f32[4,2,2,72,256]{4,3,2,1,0:T(8,128)S(1)}, f32[4,2,2,80,256...) custom-call(s32[1]{0:T(128)} %bitcast.me_ref, bf16[320,4096]{1,0:T(8,128)(2,1)} %refs_0_.7, ...), custom_call_target="tpu_custom_call" | custom-call | flops 1824522240 | bytes 16646144 | tf_op jit(solution)/shard_map/gradient/pallas_call | solution.py:324
  12.9 3.0 collective-permute-start.16
  20.1 21.7 %collective-permute-done.16 = f32[8,2,72,256]{3,2,1,0:T(8,128)S(1)} collective-permute-done((f32[8,2,72,256]{3,2,1,0:T(8,128)S(1)}, f32[8,2,72,256]{3,2,1,0:T(8,128)S(1)}, u32[]{:S(2)}, u32[]{:S(2)}) %collective-permute-start.16) | collective-permute-done | bytes 1179680 | tf_op jit(solution)/shard_map/ppermute | solution.py:255
  42.8 1.7 collective-permute-start.17
  44.5 1.6 collective-permute-done.8
  47.5 1.6 collective-permute-done
  51.8 8.4 %collective-permute-done.17 = f32[4,2,72,256]{3,2,1,0:T(8,128)} collective-permute-done((f32[4,2,72,256]{3,2,1,0:T(8,128)}, f32[4,2,72,256]{3,2,1,0:T(8,128)}, u32[]{:S(2)}, u32[]{:S(2)}) %collective-permute-start.17) | collective-permute-done | bytes 589856 | tf_op jit(solution)/shard_map/ppermute | solution.py:255
  63.7 1.6 collective-permute-start.10
  67.5 2.0 collective-permute-start.2
  71.7 2.4 collective-permute-start.19
  77.1 3.7 %collective-permute-start.3 = (f32[1,2,80,256]{3,2,1,0:T(8,128)S(1)}, f32[1,2,80,256]{3,2,1,0:T(8,128)S(1)}, u32[]{:S(2)}, u32[]{:S(2)}) collective-permute-start(f32[1,2,80,256]{3,2,1,0:T(8,128)S(1)} %slice_add_fusion.36), channel_id=1, source_target_pairs={{0,16},{2,18},{4,20},{6,22},{8,24},{10,26},{12,28},{14,30},{16,0},... | collective-permute-start | bytes 491528 | tf_op jit(solution)/shard_map/ppermute | solution.py:255
  80.9 10.7 %collective-permute-done.11 = f32[1,2,80,256]{3,2,1,0:T(8,128)S(1)} collective-permute-done((f32[1,2,80,256]{3,2,1,0:T(8,128)S(1)}, f32[1,2,80,256]{3,2,1,0:T(8,128)S(1)}, u32[]{:S(2)}, u32[]{:S(2)}) %collective-permute-start.11) | collective-permute-done | bytes 163872 | tf_op jit(solution)/shard_map/ppermute | solution.py:255
  95.8 3.0 collective-permute-start.12
  98.8 3.1 collective-permute-done.4
  102.0 2.6 collective-permute-start.20
  105.2 1.6 collective-permute-start.13
  108.1 1.6 collective-permute-start.6
  111.0 6.4 %collective-permute-done.21 = f32[2,72,256]{2,1,0:T(8,128)S(1)} collective-permute-done((f32[2,72,256]{2,1,0:T(8,128)S(1)}, f32[2,72,256]{2,1,0:T(8,128)S(1)}, u32[]{:S(2)}, u32[]{:S(2)}) %collective-permute-start.21) | collective-permute-done | bytes 147488 | tf_op jit(solution)/shard_map/ppermute | solution.py:255
  117.5 1.6 collective-permute-start.22
  119.8 1.8 collective-permute-start.15
  121.6 5.9 %collective-permute-done.22 = f32[4,72,256]{2,1,0:T(8,128)S(1)} collective-permute-done((f32[4,72,256]{2,1,0:T(8,128)S(1)}, f32[4,72,256]{2,1,0:T(8,128)S(1)}, u32[]{:S(2)}, u32[]{:S(2)}) %collective-permute-start.22) | collective-permute-done | bytes 294944 | tf_op jit(solution)/shard_map/ppermute | solution.py:255
  127.6 9.9 %collective-permute-done.23 = f32[8,72,256]{2,1,0:T(8,128)S(1)} collective-permute-done((f32[8,72,256]{2,1,0:T(8,128)S(1)}, f32[8,72,256]{2,1,0:T(8,128)S(1)}, u32[]{:S(2)}, u32[]{:S(2)}) %collective-permute-start.23) | collective-permute-done | bytes 589856 | tf_op jit(solution)/shard_map/ppermute | solution.py:255
  137.5 21.1 %labels.2.here_ref = f32[320,256]{1,0:T(8,128)S(1)} custom-call(s32[1]{0:T(128)} %bitcast.me_ref, bf16[320,4096]{1,0:T(8,128)(2,1)} %refs_0_.7, bf16[320,4096]{1,0:T(8,128)(2,1)} %refs_1_.7, bf16[320,256]{1,0:T(8,128)(2,1)S(1)} %get-tuple-element.26.refs_2_, bf16[320,32]{1,0:T(8,128)(2,1)S(1)} %get-tuple-element.27.refs_3_, bf16[640,256]{1,0:T(8,128)(2,1)S(1)} %copy-done.4, ...), custom_call_target="tpu_custom_call" | custom-call | flops 14763950080 | bytes 9043968 | tf_op jit(solution)/shard_map/labels/pallas_call | solution.py:354
  158.8 1.6 collective-permute-done.24.there_ref
  160.9 9.4 %gradient.3 = (f32[4,2,2,80,256]{4,3,2,1,0:T(8,128)}, f32[4,2,2,80,256]{4,3,2,1,0:T(8,128)}, f32[4,2,2,72,256]{4,3,2,1,0:T(8,128)S(1)}, f32[4,2,2,80,256]{4,3,2,...) custom-call(s32[1]{0:T(128)} %bitcast.me_ref, bf16[320,4096]{1,0:T(8,128)(2,1)} %refs_0_.7, ...), custom_call_target="tpu_custom_call" | custom-call | flops 1824522240 | bytes 16646144 | tf_op jit(solution)/shard_map/gradient/pallas_call | solution.py:324
  170.3 1.8 collective-permute-start.33
  175.9 22.5 %collective-permute-done.41 = f32[8,2,72,256]{3,2,1,0:T(8,128)S(1)} collective-permute-done((f32[8,2,72,256]{3,2,1,0:T(8,128)S(1)}, f32[8,2,72,256]{3,2,1,0:T(8,128)S(1)}, u32[]{:S(2)}, u32[]{:S(2)}) %collective-permute-start.41) | collective-permute-done | bytes 1179680 | tf_op jit(solution)/shard_map/ppermute | solution.py:255
  198.4 1.5 collective-permute-start.42
  201.5 1.7 collective-permute-start.34
  205.2 10.3 %collective-permute-done.42 = f32[4,2,72,256]{3,2,1,0:T(8,128)S(1)} collective-permute-done((f32[4,2,72,256]{3,2,1,0:T(8,128)S(1)}, f32[4,2,72,256]{3,2,1,0:T(8,128)S(1)}, u32[]{:S(2)}, u32[]{:S(2)}) %collective-permute-start.42) | collective-permute-done | bytes 589856 | tf_op jit(solution)/shard_map/ppermute | solution.py:255
  216.0 1.6 collective-permute-done.34
  217.6 1.5 collective-permute-start.35
  219.1 6.0 %collective-permute-done.43 = f32[2,2,72,256]{3,2,1,0:T(8,128)S(1)} collective-permute-done((f32[2,2,72,256]{3,2,1,0:T(8,128)S(1)}, f32[2,2,72,256]{3,2,1,0:T(8,128)S(1)}, u32[]{:S(2)}, u32[]{:S(2)}) %collective-permute-start.43) | collective-permute-done | bytes 294944 | tf_op jit(solution)/shard_map/ppermute | solution.py:255
  227.6 6.0 %collective-permute-done.44 = f32[1,2,72,256]{3,2,1,0:T(8,128)S(1)} collective-permute-done((f32[1,2,72,256]{3,2,1,0:T(8,128)S(1)}, f32[1,2,72,256]{3,2,1,0:T(8,128)S(1)}, u32[]{:S(2)}, u32[]{:S(2)}) %collective-permute-start.44) | collective-permute-done | bytes 147488 | tf_op jit(solution)/shard_map/ppermute | solution.py:255
  234.4 5.5 %collective-permute-done.27 = f32[2,2,80,256]{3,2,1,0:T(8,128)S(1)} collective-permute-done((f32[2,2,80,256]{3,2,1,0:T(8,128)S(1)}, f32[2,2,80,256]{3,2,1,0:T(8,128)S(1)}, u32[]{:S(2)}, u32[]{:S(2)}) %collective-permute-start.27) | collective-permute-done | bytes 327712 | tf_op jit(solution)/shard_map/ppermute | solution.py:255
  241.2 6.7 %collective-permute-done.36 = f32[1,2,80,256]{3,2,1,0:T(8,128)S(1)} collective-permute-done((f32[1,2,80,256]{3,2,1,0:T(8,128)S(1)}, f32[1,2,80,256]{3,2,1,0:T(8,128)S(1)}, u32[]{:S(2)}, u32[]{:S(2)}) %collective-permute-start.36) | collective-permute-done | bytes 163872 | tf_op jit(solution)/shard_map/ppermute | solution.py:255
  248.1 4.2 %collective-permute-done.28 = f32[1,2,80,256]{3,2,1,0:T(8,128)S(1)} collective-permute-done((f32[1,2,80,256]{3,2,1,0:T(8,128)S(1)}, f32[1,2,80,256]{3,2,1,0:T(8,128)S(1)}, u32[]{:S(2)}, u32[]{:S(2)}) %collective-permute-start.28) | collective-permute-done | bytes 163872 | tf_op jit(solution)/shard_map/ppermute | solution.py:255
  252.4 3.3 %collective-permute-done.37 = f32[1,80,256]{2,1,0:T(8,128)S(1)} collective-permute-done((f32[1,80,256]{2,1,0:T(8,128)S(1)}, f32[1,80,256]{2,1,0:T(8,128)S(1)}, u32[]{:S(2)}, u32[]{:S(2)}) %collective-permute-start.37) | collective-permute-done | bytes 81952 | tf_op jit(solution)/shard_map/ppermute | solution.py:255
  257.0 1.9 collective-permute-done.29
  259.0 2.2 collective-permute-done.38
  262.4 3.7 %collective-permute-done.30 = f32[2,80,256]{2,1,0:T(8,128)S(1)} collective-permute-done((f32[2,80,256]{2,1,0:T(8,128)S(1)}, f32[2,80,256]{2,1,0:T(8,128)S(1)}, u32[]{:S(2)}, u32[]{:S(2)}) %collective-permute-start.30) | collective-permute-done | bytes 163872 | tf_op jit(solution)/shard_map/ppermute | solution.py:255
  266.2 2.3 collective-permute-done.46
  268.5 1.6 collective-permute-start.47
  270.4 6.1 %collective-permute-done.31 = f32[4,80,256]{2,1,0:T(8,128)S(1)} collective-permute-done((f32[4,80,256]{2,1,0:T(8,128)S(1)}, f32[4,80,256]{2,1,0:T(8,128)S(1)}, u32[]{:S(2)}, u32[]{:S(2)}) %collective-permute-start.31) | collective-permute-done | bytes 327712 | tf_op jit(solution)/shard_map/ppermute | solution.py:255
  276.6 1.9 collective-permute-done.47
  279.0 9.5 %collective-permute-done.48 = f32[8,72,256]{2,1,0:T(8,128)S(1)} collective-permute-done((f32[8,72,256]{2,1,0:T(8,128)S(1)}, f32[8,72,256]{2,1,0:T(8,128)S(1)}, u32[]{:S(2)}, u32[]{:S(2)}) %collective-permute-start.48) | collective-permute-done | bytes 589856 | tf_op jit(solution)/shard_map/ppermute | solution.py:255
  288.5 23.1 %labels.3 = (f32[320,256]{1,0:T(8,128)S(1)}, f32[231,4096]{1,0:T(8,128)}) custom-call(s32[1]{0:T(128)} %bitcast.me_ref, bf16[320,4096]{1,0:T(8,128)(2,1)} %refs_0_.7, bf16[320,4096]{1,0:T(8,128)(2,1)} %refs_1_.7, bf16[320,256]{1,0:T(8,128)(2,1)S(1)} %get-tuple-element.36.refs_2_, bf16[320,32]{1,0:T(8,128)(2,1)S(1)} %get-tuple-element.37.refs_3_, ...), custom_call_target="tpu_custom_call" | custom-call | flops 14763950080 | bytes 9043968 | tf_op jit(solution)/shard_map/labels/pallas_call | solution.py:354
  311.6 1.6 collective-permute-done.49.there_ref
  (145 shorter events, 50.6 us)
Async XLA Ops:
  12.9 29.0 %collective-permute-start.16 = (f32[8,2,72,256]{3,2,1,0:T(8,128)S(1)}, f32[8,2,72,256]{3,2,1,0:T(8,128)S(1)}, u32[]{:S(2)}, u32[]{:S(2)}) collective-permute-start(f32[8,2,72,256]{3,2,1,0:T(8,128)S(1)} %bitcast.95), channel_id=1, source_target_pairs={{0,8},{2,10},{4,12},{6,14},{8,0},{10,2},{12,4},{14,6},{16,24},{18,... | collective-permute-start | bytes 3538952 | tf_op jit(solution)/shard_map/ppermute | solution.py:255
  15.9 30.2 %collective-permute-start.8 = (f32[8,2,80,256]{3,2,1,0:T(8,128)S(1)}, f32[8,2,80,256]{3,2,1,0:T(8,128)S(1)}, u32[]{:S(2)}, u32[]{:S(2)}) collective-permute-start(f32[8,2,80,256]{3,2,1,0:T(8,128)S(1)} %bitcast.93), channel_id=1, source_target_pairs={{0,4},{2,6},{4,0},{6,2},{8,12},{10,14},{12,8},{14,10},{16,20},{18,... | collective-permute-start | bytes 3932168 | tf_op jit(solution)/shard_map/ppermute | solution.py:255
  17.4 31.7 %collective-permute-start = (f32[8,2,80,256]{3,2,1,0:T(8,128)S(1)}, f32[8,2,80,256]{3,2,1,0:T(8,128)S(1)}, u32[]{:S(2)}, u32[]{:S(2)}) collective-permute-start(f32[8,2,80,256]{3,2,1,0:T(8,128)S(1)} %bitcast.92), channel_id=1, source_target_pairs={{0,2},{2,0},{4,6},{6,4},{8,10},{10,8},{12,14},{14,12},{16,18},{18,... | collective-permute-start | bytes 3932168 | tf_op jit(solution)/shard_map/ppermute | solution.py:255
  42.8 17.3 %collective-permute-start.17 = (f32[4,2,72,256]{3,2,1,0:T(8,128)}, f32[4,2,72,256]{3,2,1,0:T(8,128)}, u32[]{:S(2)}, u32[]{:S(2)}) collective-permute-start(f32[4,2,72,256]{3,2,1,0:T(8,128)} %slice_add_fusion.5), channel_id=1, source_target_pairs={{0,2},{2,0},{4,6},{6,4},{8,10},{10,8},{12,14},{14,12},{16,18},{18,... | collective-permute-start | bytes 1769480 | tf_op jit(solution)/shard_map/ppermute | solution.py:255
  47.1 15.5 %collective-permute-start.9 = (f32[4,2,80,256]{3,2,1,0:T(8,128)}, f32[4,2,80,256]{3,2,1,0:T(8,128)S(1)}, u32[]{:S(2)}, u32[]{:S(2)}) collective-permute-start(f32[4,2,80,256]{3,2,1,0:T(8,128)} %slice_add_fusion.2), channel_id=1, source_target_pairs={{0,8},{2,10},{4,12},{6,14},{8,0},{10,2},{12,4},{14,6},{16,24},{18,... | collective-permute-start | bytes 1966088 | tf_op jit(solution)/shard_map/ppermute | solution.py:255
  50.4 16.0 %collective-permute-start.1 = (f32[4,2,80,256]{3,2,1,0:T(8,128)}, f32[4,2,80,256]{3,2,1,0:T(8,128)}, u32[]{:S(2)}, u32[]{:S(2)}) collective-permute-start(f32[4,2,80,256]{3,2,1,0:T(8,128)} %slice_add_fusion.3), channel_id=1, source_target_pairs={{0,4},{2,6},{4,0},{6,2},{8,12},{10,14},{12,8},{14,10},{16,20},{18,... | collective-permute-start | bytes 1966088 | tf_op jit(solution)/shard_map/ppermute | solution.py:255
  61.2 9.4 %collective-permute-start.18 = (f32[2,2,72,256]{3,2,1,0:T(8,128)S(1)}, f32[2,2,72,256]{3,2,1,0:T(8,128)S(1)}, u32[]{:S(2)}, u32[]{:S(2)}) collective-permute-start(f32[2,2,72,256]{3,2,1,0:T(8,128)S(1)} %slice_add_fusion.16), channel_id=1, source_target_pairs={{0,4},{2,6},{4,0},{6,2},{8,12},{10,14},{12,8},{14,10},{16,20},{18,... | collective-permute-start | bytes 884744 | tf_op jit(solution)/shard_map/ppermute | solution.py:255
  63.7 10.4 %collective-permute-start.10 = (f32[2,2,80,256]{3,2,1,0:T(8,128)S(1)}, f32[2,2,80,256]{3,2,1,0:T(8,128)S(1)}, u32[]{:S(2)}, u32[]{:S(2)}) collective-permute-start(f32[2,2,80,256]{3,2,1,0:T(8,128)S(1)} %slice_add_fusion.10), channel_id=1, source_target_pairs={{0,2},{2,0},{4,6},{6,4},{8,10},{10,8},{12,14},{14,12},{16,18},{18,... | collective-permute-start | bytes 983048 | tf_op jit(solution)/shard_map/ppermute | solution.py:255
  67.5 8.6 %collective-permute-start.2 = (f32[2,2,80,256]{3,2,1,0:T(8,128)S(1)}, f32[2,2,80,256]{3,2,1,0:T(8,128)S(1)}, u32[]{:S(2)}, u32[]{:S(2)}) collective-permute-start(f32[2,2,80,256]{3,2,1,0:T(8,128)S(1)} %slice_add_fusion.12), channel_id=1, source_target_pairs={{0,8},{2,10},{4,12},{6,14},{8,0},{10,2},{12,4},{14,6},{16,24},{18,... | collective-permute-start | bytes 983048 | tf_op jit(solution)/shard_map/ppermute | solution.py:255
  71.7 23.1 %collective-permute-start.19 = (f32[1,2,72,256]{3,2,1,0:T(8,128)S(1)}, f32[1,2,72,256]{3,2,1,0:T(8,128)S(1)}, u32[]{:S(2)}, u32[]{:S(2)}) collective-permute-start(f32[1,2,72,256]{3,2,1,0:T(8,128)S(1)} %slice_add_fusion.48), channel_id=1, source_target_pairs={{0,16},{2,18},{4,20},{6,22},{8,24},{10,26},{12,28},{14,30},{16,0},... | collective-permute-start | bytes 442376 | tf_op jit(solution)/shard_map/ppermute | solution.py:255
  75.1 16.5 %collective-permute-start.11 = (f32[1,2,80,256]{3,2,1,0:T(8,128)S(1)}, f32[1,2,80,256]{3,2,1,0:T(8,128)S(1)}, u32[]{:S(2)}, u32[]{:S(2)}) collective-permute-start(f32[1,2,80,256]{3,2,1,0:T(8,128)S(1)} %slice_add_fusion.30), channel_id=1, source_target_pairs={{0,16},{2,18},{4,20},{6,22},{8,24},{10,26},{12,28},{14,30},{16,0},... | collective-permute-start | bytes 491528 | tf_op jit(solution)/shard_map/ppermute | solution.py:255
  77.1 16.6 %collective-permute-start.3 = (f32[1,2,80,256]{3,2,1,0:T(8,128)S(1)}, f32[1,2,80,256]{3,2,1,0:T(8,128)S(1)}, u32[]{:S(2)}, u32[]{:S(2)}) collective-permute-start(f32[1,2,80,256]{3,2,1,0:T(8,128)S(1)} %slice_add_fusion.36), channel_id=1, source_target_pairs={{0,16},{2,18},{4,20},{6,22},{8,24},{10,26},{12,28},{14,30},{16,0},... | collective-permute-start | bytes 491528 | tf_op jit(solution)/shard_map/ppermute | solution.py:255
  94.7 7.2 %collective-permute-start.4 = (f32[1,80,256]{2,1,0:T(8,128)S(1)}, f32[1,80,256]{2,1,0:T(8,128)S(1)}, u32[]{:S(2)}, u32[]{:S(2)}) collective-permute-start(f32[1,80,256]{2,1,0:T(8,128)S(1)} %get-tuple-element.53), channel_id=1, source_target_pairs={{0,16},{2,18},{4,20},{6,22},{8,24},{10,26},{12,28},{14,30},{16,0},... | collective-permute-start | bytes 245768 | tf_op jit(solution)/shard_map/ppermute | solution.py:255
  95.8 9.3 %collective-permute-start.12 = (f32[1,80,256]{2,1,0:T(8,128)S(1)}, f32[1,80,256]{2,1,0:T(8,128)S(1)}, u32[]{:S(2)}, u32[]{:S(2)}) collective-permute-start(f32[1,80,256]{2,1,0:T(8,128)S(1)} %get-tuple-element.52), channel_id=1, source_target_pairs={{0,16},{2,18},{4,20},{6,22},{8,24},{10,26},{12,28},{14,30},{16,0},... | collective-permute-start | bytes 245768 | tf_op jit(solution)/shard_map/ppermute | solution.py:255
  101.9 6.2 %collective-permute-start.5 = (f32[2,80,256]{2,1,0:T(8,128)S(1)}, f32[2,80,256]{2,1,0:T(8,128)S(1)}, u32[]{:S(2)}, u32[]{:S(2)}) collective-permute-start(f32[2,80,256]{2,1,0:T(8,128)S(1)} %pad_maximum_fusion.12), channel_id=1, source_target_pairs={{0,8},{2,10},{4,12},{6,14},{8,0},{10,2},{12,4},{14,6},{16,24},{18,... | collective-permute-start | bytes 491528 | tf_op jit(solution)/shard_map/ppermute | solution.py:255
  102.0 7.7 %collective-permute-start.20 = (f32[1,72,256]{2,1,0:T(8,128)S(1)}, f32[1,72,256]{2,1,0:T(8,128)S(1)}, u32[]{:S(2)}, u32[]{:S(2)}) collective-permute-start(f32[1,72,256]{2,1,0:T(8,128)S(1)} %fusion.18), channel_id=1, source_target_pairs={{0,16},{2,18},{4,20},{6,22},{8,24},{10,26},{12,28},{14,30},{16,0},... | collective-permute-start | bytes 221192 | tf_op jit(solution)/shard_map/ppermute | solution.py:255
  105.2 5.4 %collective-permute-start.13 = (f32[2,80,256]{2,1,0:T(8,128)S(1)}, f32[2,80,256]{2,1,0:T(8,128)S(1)}, u32[]{:S(2)}, u32[]{:S(2)}) collective-permute-start(f32[2,80,256]{2,1,0:T(8,128)S(1)} %pad_maximum_fusion.13), channel_id=1, source_target_pairs={{0,2},{2,0},{4,6},{6,4},{8,10},{10,8},{12,14},{14,12},{16,18},{18,... | collective-permute-start | bytes 491528 | tf_op jit(solution)/shard_map/ppermute | solution.py:255
  108.1 10.9 %collective-permute-start.6 = (f32[4,80,256]{2,1,0:T(8,128)S(1)}, f32[4,80,256]{2,1,0:T(8,128)S(1)}, u32[]{:S(2)}, u32[]{:S(2)}) collective-permute-start(f32[4,80,256]{2,1,0:T(8,128)S(1)} %pad_maximum_fusion.6), channel_id=1, source_target_pairs={{0,4},{2,6},{4,0},{6,2},{8,12},{10,14},{12,8},{14,10},{16,20},{18,... | collective-permute-start | bytes 983048 | tf_op jit(solution)/shard_map/ppermute | solution.py:255
  109.7 7.7 %collective-permute-start.21 = (f32[2,72,256]{2,1,0:T(8,128)S(1)}, f32[2,72,256]{2,1,0:T(8,128)S(1)}, u32[]{:S(2)}, u32[]{:S(2)}) collective-permute-start(f32[2,72,256]{2,1,0:T(8,128)S(1)} %pad_maximum_fusion.16), channel_id=1, source_target_pairs={{0,4},{2,6},{4,0},{6,2},{8,12},{10,14},{12,8},{14,10},{16,20},{18,... | collective-permute-start | bytes 442376 | tf_op jit(solution)/shard_map/ppermute | solution.py:255
  110.6 9.1 %collective-permute-start.14 = (f32[4,80,256]{2,1,0:T(8,128)S(1)}, f32[4,80,256]{2,1,0:T(8,128)S(1)}, u32[]{:S(2)}, u32[]{:S(2)}) collective-permute-start(f32[4,80,256]{2,1,0:T(8,128)S(1)} %pad_maximum_fusion.7), channel_id=1, source_target_pairs={{0,8},{2,10},{4,12},{6,14},{8,0},{10,2},{12,4},{14,6},{16,24},{18,... | collective-permute-start | bytes 983048 | tf_op jit(solution)/shard_map/ppermute | solution.py:255
  117.5 10.0 %collective-permute-start.22 = (f32[4,72,256]{2,1,0:T(8,128)S(1)}, f32[4,72,256]{2,1,0:T(8,128)S(1)}, u32[]{:S(2)}, u32[]{:S(2)}) collective-permute-start(f32[4,72,256]{2,1,0:T(8,128)S(1)} %pad_maximum_fusion.10), channel_id=1, source_target_pairs={{0,2},{2,0},{4,6},{6,4},{8,10},{10,8},{12,14},{14,12},{16,18},{18,... | collective-permute-start | bytes 884744 | tf_op jit(solution)/shard_map/ppermute | solution.py:255
  119.1 18.4 %collective-permute-start.7 = (f32[8,80,256]{2,1,0:T(8,128)S(1)}, f32[8,80,256]{2,1,0:T(8,128)S(1)}, u32[]{:S(2)}, u32[]{:S(2)}) collective-permute-start(f32[8,80,256]{2,1,0:T(8,128)S(1)} %pad_maximum_fusion), channel_id=1, source_target_pairs={{0,2},{2,0},{4,6},{6,4},{8,10},{10,8},{12,14},{14,12},{16,18},{18,... | collective-permute-start | bytes 1966088 | tf_op jit(solution)/shard_map/ppermute | solution.py:255
  119.8 17.7 %collective-permute-start.15 = (f32[8,80,256]{2,1,0:T(8,128)S(1)}, f32[8,80,256]{2,1,0:T(8,128)S(1)}, u32[]{:S(2)}, u32[]{:S(2)}) collective-permute-start(f32[8,80,256]{2,1,0:T(8,128)S(1)} %pad_maximum_fusion.1), channel_id=1, source_target_pairs={{0,4},{2,6},{4,0},{6,2},{8,12},{10,14},{12,8},{14,10},{16,20},{18,... | collective-permute-start | bytes 1966088 | tf_op jit(solution)/shard_map/ppermute | solution.py:255
  127.5 9.9 %collective-permute-start.23 = (f32[8,72,256]{2,1,0:T(8,128)S(1)}, f32[8,72,256]{2,1,0:T(8,128)S(1)}, u32[]{:S(2)}, u32[]{:S(2)}) collective-permute-start(f32[8,72,256]{2,1,0:T(8,128)S(1)} %pad_maximum_fusion.4), channel_id=1, source_target_pairs={{0,8},{2,10},{4,12},{6,14},{8,0},{10,2},{12,4},{14,6},{16,24},{18,... | collective-permute-start | bytes 1769480 | tf_op jit(solution)/shard_map/ppermute | solution.py:255
  170.3 28.0 %collective-permute-start.41 = (f32[8,2,72,256]{3,2,1,0:T(8,128)S(1)}, f32[8,2,72,256]{3,2,1,0:T(8,128)S(1)}, u32[]{:S(2)}, u32[]{:S(2)}) collective-permute-start(f32[8,2,72,256]{3,2,1,0:T(8,128)S(1)} %bitcast.94), channel_id=1, source_target_pairs={{0,8},{2,10},{4,12},{6,14},{8,0},{10,2},{12,4},{14,6},{16,24},{18,... | collective-permute-start | bytes 3538952 | tf_op jit(solution)/shard_map/ppermute | solution.py:255
  170.3 31.1 %collective-permute-start.33 = (f32[8,2,80,256]{3,2,1,0:T(8,128)}, f32[8,2,80,256]{3,2,1,0:T(8,128)S(1)}, u32[]{:S(2)}, u32[]{:S(2)}) collective-permute-start(f32[8,2,80,256]{3,2,1,0:T(8,128)} %bitcast.110), channel_id=1, source_target_pairs={{0,4},{2,6},{4,0},{6,2},{8,12},{10,14},{12,8},{14,10},{16,20},{18,... | collective-permute-start | bytes 3932168 | tf_op jit(solution)/shard_map/ppermute | solution.py:255
  172.1 31.9 %collective-permute-start.25 = (f32[8,2,80,256]{3,2,1,0:T(8,128)}, f32[8,2,80,256]{3,2,1,0:T(8,128)S(1)}, u32[]{:S(2)}, u32[]{:S(2)}) collective-permute-start(f32[8,2,80,256]{3,2,1,0:T(8,128)} %bitcast.109), channel_id=1, source_target_pairs={{0,2},{2,0},{4,6},{6,4},{8,10},{10,8},{12,14},{14,12},{16,18},{18,... | collective-permute-start | bytes 3932168 | tf_op jit(solution)/shard_map/ppermute | solution.py:255
  198.4 17.1 %collective-permute-start.42 = (f32[4,2,72,256]{3,2,1,0:T(8,128)S(1)}, f32[4,2,72,256]{3,2,1,0:T(8,128)S(1)}, u32[]{:S(2)}, u32[]{:S(2)}) collective-permute-start(f32[4,2,72,256]{3,2,1,0:T(8,128)S(1)} %slice_add_fusion.4), channel_id=1, source_target_pairs={{0,2},{2,0},{4,6},{6,4},{8,10},{10,8},{12,14},{14,12},{16,18},{18,... | collective-permute-start | bytes 1769480 | tf_op jit(solution)/shard_map/ppermute | solution.py:255
  201.5 16.0 %collective-permute-start.34 = (f32[4,2,80,256]{3,2,1,0:T(8,128)S(1)}, f32[4,2,80,256]{3,2,1,0:T(8,128)S(1)}, u32[]{:S(2)}, u32[]{:S(2)}) collective-permute-start(f32[4,2,80,256]{3,2,1,0:T(8,128)S(1)} %slice_add_fusion), channel_id=1, source_target_pairs={{0,8},{2,10},{4,12},{6,14},{8,0},{10,2},{12,4},{14,6},{16,24},{18,... | collective-permute-start | bytes 1966088 | tf_op jit(solution)/shard_map/ppermute | solution.py:255
  204.1 22.5 %collective-permute-start.26 = (f32[4,2,80,256]{3,2,1,0:T(8,128)S(1)}, f32[4,2,80,256]{3,2,1,0:T(8,128)S(1)}, u32[]{:S(2)}, u32[]{:S(2)}) collective-permute-start(f32[4,2,80,256]{3,2,1,0:T(8,128)S(1)} %slice_add_fusion.1), channel_id=1, source_target_pairs={{0,4},{2,6},{4,0},{6,2},{8,12},{10,14},{12,8},{14,10},{16,20},{18,... | collective-permute-start | bytes 1966088 | tf_op jit(solution)/shard_map/ppermute | solution.py:255
  215.6 9.6 %collective-permute-start.43 = (f32[2,2,72,256]{3,2,1,0:T(8,128)S(1)}, f32[2,2,72,256]{3,2,1,0:T(8,128)S(1)}, u32[]{:S(2)}, u32[]{:S(2)}) collective-permute-start(f32[2,2,72,256]{3,2,1,0:T(8,128)S(1)} %slice_add_fusion.14), channel_id=1, source_target_pairs={{0,4},{2,6},{4,0},{6,2},{8,12},{10,14},{12,8},{14,10},{16,20},{18,... | collective-permute-start | bytes 884744 | tf_op jit(solution)/shard_map/ppermute | solution.py:255
  217.6 16.1 %collective-permute-start.35 = (f32[2,2,80,256]{3,2,1,0:T(8,128)S(1)}, f32[2,2,80,256]{3,2,1,0:T(8,128)S(1)}, u32[]{:S(2)}, u32[]{:S(2)}) collective-permute-start(f32[2,2,80,256]{3,2,1,0:T(8,128)S(1)} %slice_add_fusion.6), channel_id=1, source_target_pairs={{0,2},{2,0},{4,6},{6,4},{8,10},{10,8},{12,14},{14,12},{16,18},{18,... | collective-permute-start | bytes 983048 | tf_op jit(solution)/shard_map/ppermute | solution.py:255
  225.2 8.4 %collective-permute-start.44 = (f32[1,2,72,256]{3,2,1,0:T(8,128)S(1)}, f32[1,2,72,256]{3,2,1,0:T(8,128)S(1)}, u32[]{:S(2)}, u32[]{:S(2)}) collective-permute-start(f32[1,2,72,256]{3,2,1,0:T(8,128)S(1)} %slice_add_fusion.42), channel_id=1, source_target_pairs={{0,16},{2,18},{4,20},{6,22},{8,24},{10,26},{12,28},{14,30},{16,0},... | collective-permute-start | bytes 442376 | tf_op jit(solution)/shard_map/ppermute | solution.py:255
  226.6 13.3 %collective-permute-start.27 = (f32[2,2,80,256]{3,2,1,0:T(8,128)S(1)}, f32[2,2,80,256]{3,2,1,0:T(8,128)S(1)}, u32[]{:S(2)}, u32[]{:S(2)}) collective-permute-start(f32[2,2,80,256]{3,2,1,0:T(8,128)S(1)} %slice_add_fusion.8), channel_id=1, source_target_pairs={{0,8},{2,10},{4,12},{6,14},{8,0},{10,2},{12,4},{14,6},{16,24},{18,... | collective-permute-start | bytes 983048 | tf_op jit(solution)/shard_map/ppermute | solution.py:255
  233.8 14.1 %collective-permute-start.36 = (f32[1,2,80,256]{3,2,1,0:T(8,128)S(1)}, f32[1,2,80,256]{3,2,1,0:T(8,128)S(1)}, u32[]{:S(2)}, u32[]{:S(2)}) collective-permute-start(f32[1,2,80,256]{3,2,1,0:T(8,128)S(1)} %slice_add_fusion.18), channel_id=1, source_target_pairs={{0,16},{2,18},{4,20},{6,22},{8,24},{10,26},{12,28},{14,30},{16,0},... | collective-permute-start | bytes 491528 | tf_op jit(solution)/shard_map/ppermute | solution.py:255
  240.0 12.3 %collective-permute-start.28 = (f32[1,2,80,256]{3,2,1,0:T(8,128)S(1)}, f32[1,2,80,256]{3,2,1,0:T(8,128)S(1)}, u32[]{:S(2)}, u32[]{:S(2)}) collective-permute-start(f32[1,2,80,256]{3,2,1,0:T(8,128)S(1)} %slice_add_fusion.24), channel_id=1, source_target_pairs={{0,16},{2,18},{4,20},{6,22},{8,24},{10,26},{12,28},{14,30},{16,0},... | collective-permute-start | bytes 491528 | tf_op jit(solution)/shard_map/ppermute | solution.py:255
  248.0 7.8 %collective-permute-start.37 = (f32[1,80,256]{2,1,0:T(8,128)S(1)}, f32[1,80,256]{2,1,0:T(8,128)S(1)}, u32[]{:S(2)}, u32[]{:S(2)}) collective-permute-start(f32[1,80,256]{2,1,0:T(8,128)S(1)} %fusion.8), channel_id=1, source_target_pairs={{0,16},{2,18},{4,20},{6,22},{8,24},{10,26},{12,28},{14,30},{16,0},... | collective-permute-start | bytes 245768 | tf_op jit(solution)/shard_map/ppermute | solution.py:255
  252.3 6.5 %collective-permute-start.29 = (f32[1,80,256]{2,1,0:T(8,128)S(1)}, f32[1,80,256]{2,1,0:T(8,128)S(1)}, u32[]{:S(2)}, u32[]{:S(2)}) collective-permute-start(f32[1,80,256]{2,1,0:T(8,128)S(1)} %fusion.11), channel_id=1, source_target_pairs={{0,16},{2,18},{4,20},{6,22},{8,24},{10,26},{12,28},{14,30},{16,0},... | collective-permute-start | bytes 245768 | tf_op jit(solution)/shard_map/ppermute | solution.py:255
  255.8 5.4 %collective-permute-start.38 = (f32[2,80,256]{2,1,0:T(8,128)S(1)}, f32[2,80,256]{2,1,0:T(8,128)S(1)}, u32[]{:S(2)}, u32[]{:S(2)}) collective-permute-start(f32[2,80,256]{2,1,0:T(8,128)S(1)} %pad_maximum_fusion.15), channel_id=1, source_target_pairs={{0,2},{2,0},{4,6},{6,4},{8,10},{10,8},{12,14},{14,12},{16,18},{18,... | collective-permute-start | bytes 491528 | tf_op jit(solution)/shard_map/ppermute | solution.py:255
  256.9 5.4 %collective-permute-start.45 = (f32[1,72,256]{2,1,0:T(8,128)S(1)}, f32[1,72,256]{2,1,0:T(8,128)S(1)}, u32[]{:S(2)}, u32[]{:S(2)}) collective-permute-start(f32[1,72,256]{2,1,0:T(8,128)S(1)} %fusion.21), channel_id=1, source_target_pairs={{0,16},{2,18},{4,20},{6,22},{8,24},{10,26},{12,28},{14,30},{16,0},... | collective-permute-start | bytes 221192 | tf_op jit(solution)/shard_map/ppermute | solution.py:255
  258.9 7.2 %collective-permute-start.30 = (f32[2,80,256]{2,1,0:T(8,128)S(1)}, f32[2,80,256]{2,1,0:T(8,128)S(1)}, u32[]{:S(2)}, u32[]{:S(2)}) collective-permute-start(f32[2,80,256]{2,1,0:T(8,128)S(1)} %pad_maximum_fusion.14), channel_id=1, source_target_pairs={{0,8},{2,10},{4,12},{6,14},{8,0},{10,2},{12,4},{14,6},{16,24},{18,... | collective-permute-start | bytes 491528 | tf_op jit(solution)/shard_map/ppermute | solution.py:255
  261.2 9.0 %collective-permute-start.39 = (f32[4,80,256]{2,1,0:T(8,128)S(1)}, f32[4,80,256]{2,1,0:T(8,128)S(1)}, u32[]{:S(2)}, u32[]{:S(2)}) collective-permute-start(f32[4,80,256]{2,1,0:T(8,128)S(1)} %pad_maximum_fusion.9), channel_id=1, source_target_pairs={{0,8},{2,10},{4,12},{6,14},{8,0},{10,2},{12,4},{14,6},{16,24},{18,... | collective-permute-start | bytes 983048 | tf_op jit(solution)/shard_map/ppermute | solution.py:255
  262.3 6.2 %collective-permute-start.46 = (f32[2,72,256]{2,1,0:T(8,128)S(1)}, f32[2,72,256]{2,1,0:T(8,128)S(1)}, u32[]{:S(2)}, u32[]{:S(2)}) collective-permute-start(f32[2,72,256]{2,1,0:T(8,128)S(1)} %pad_maximum_fusion.17), channel_id=1, source_target_pairs={{0,4},{2,6},{4,0},{6,2},{8,12},{10,14},{12,8},{14,10},{16,20},{18,... | collective-permute-start | bytes 442376 | tf_op jit(solution)/shard_map/ppermute | solution.py:255
  266.1 10.3 %collective-permute-start.31 = (f32[4,80,256]{2,1,0:T(8,128)S(1)}, f32[4,80,256]{2,1,0:T(8,128)S(1)}, u32[]{:S(2)}, u32[]{:S(2)}) collective-permute-start(f32[4,80,256]{2,1,0:T(8,128)S(1)} %pad_maximum_fusion.8), channel_id=1, source_target_pairs={{0,4},{2,6},{4,0},{6,2},{8,12},{10,14},{12,8},{14,10},{16,20},{18,... | collective-permute-start | bytes 983048 | tf_op jit(solution)/shard_map/ppermute | solution.py:255
  268.5 10.0 %collective-permute-start.47 = (f32[4,72,256]{2,1,0:T(8,128)S(1)}, f32[4,72,256]{2,1,0:T(8,128)S(1)}, u32[]{:S(2)}, u32[]{:S(2)}) collective-permute-start(f32[4,72,256]{2,1,0:T(8,128)S(1)} %pad_maximum_fusion.11), channel_id=1, source_target_pairs={{0,2},{2,0},{4,6},{6,4},{8,10},{10,8},{12,14},{14,12},{16,18},{18,... | collective-permute-start | bytes 884744 | tf_op jit(solution)/shard_map/ppermute | solution.py:255
  270.2 18.3 %collective-permute-start.40 = (f32[8,80,256]{2,1,0:T(8,128)S(1)}, f32[8,80,256]{2,1,0:T(8,128)S(1)}, u32[]{:S(2)}, u32[]{:S(2)}) collective-permute-start(f32[8,80,256]{2,1,0:T(8,128)S(1)} %pad_maximum_fusion.3), channel_id=1, source_target_pairs={{0,4},{2,6},{4,0},{6,2},{8,12},{10,14},{12,8},{14,10},{16,20},{18,... | collective-permute-start | bytes 1966088 | tf_op jit(solution)/shard_map/ppermute | solution.py:255
  276.5 12.0 %collective-permute-start.32 = (f32[8,80,256]{2,1,0:T(8,128)S(1)}, f32[8,80,256]{2,1,0:T(8,128)S(1)}, u32[]{:S(2)}, u32[]{:S(2)}) collective-permute-start(f32[8,80,256]{2,1,0:T(8,128)S(1)} %pad_maximum_fusion.2), channel_id=1, source_target_pairs={{0,2},{2,0},{4,6},{6,4},{8,10},{10,8},{12,14},{14,12},{16,18},{18,... | collective-permute-start | bytes 1966088 | tf_op jit(solution)/shard_map/ppermute | solution.py:255
  278.5 9.9 %collective-permute-start.48 = (f32[8,72,256]{2,1,0:T(8,128)S(1)}, f32[8,72,256]{2,1,0:T(8,128)S(1)}, u32[]{:S(2)}, u32[]{:S(2)}) collective-permute-start(f32[8,72,256]{2,1,0:T(8,128)S(1)} %pad_maximum_fusion.5), channel_id=1, source_target_pairs={{0,8},{2,10},{4,12},{6,14},{8,0},{10,2},{12,4},{14,6},{16,24},{18,... | collective-permute-start | bytes 1769480 | tf_op jit(solution)/shard_map/ppermute | solution.py:255
  (16 other events, 148.5 us)

commit v3 on v0

--- a/solution.py
+++ b/solution.py
@@ -1,11 +1,16 @@
+import functools
+
 import jax
 import jax.numpy as jnp
 import numpy as np
 from jax import lax
+from jax.experimental import pallas as pl
+from jax.experimental.pallas import tpu as pltpu
 from jax.sharding import PartitionSpec as P
 
 ALTS = 2
-
+LANES = 128
+VMEM_LIMIT = 16 * 1024 * 1024
 
 step_size = 0.25
 
@@ -27,13 +32,17 @@
     return (np.array(left_index, np.int32), np.array(right_index, np.int32), pair_table, doubling)
 
 
+def round_up(value, unit):
+    return -(-value // unit) * unit
+
+
 def contract_rows(left, right):
     return lax.dot_general(
         left, right, (((0,), (0,)), ((), ())), preferred_element_type=jnp.float32
     )
 
 
-def per_device(flux, inv_var, coeffs, labels):
+def plain_device(flux, inv_var, coeffs, labels):
     count = labels.shape[1]
     left_index, right_index, pair_table, doubling = pair_tables(count)
     flux_f = flux.astype(jnp.float32)
@@ -78,9 +87,366 @@
     return (theta, lab)
 
 
+def feature_maps(count, padded):
+    left_index, right_index, pair_table, doubling = pair_tables(count)
+    rows = round_up(1 + count, 32)
+    left = np.zeros((rows, padded), np.float32)
+    right = np.zeros((rows, padded), np.float32)
+    left[0, 0] = 1.0
+    right[0, : 1 + count] = 1.0
+    for label in range(count):
+        left[1 + label, 1 + label] = 1.0
+    for position in range(len(left_index)):
+        left[1 + left_index[position], 1 + count + position] = 1.0
+        right[1 + right_index[position], 1 + count + position] = 1.0
+    select = np.zeros((count, rows, padded), np.float32)
+    for label in range(count):
+        select[label, 0, 1 + label] = 1.0
+        for other in range(count):
+            select[label, 1 + other, pair_table[label, other]] = doubling[label, other]
+    return left, right, select.reshape(count * rows, padded)
+
+
+def split_exact(value):
+    high = value.astype(jnp.bfloat16)
+    rest = value - high.astype(jnp.float32)
+    middle = rest.astype(jnp.bfloat16)
+    low = (rest - middle.astype(jnp.float32)).astype(jnp.bfloat16)
+    return high, middle, low
+
+
+def mm(left, right):
+    return jnp.dot(left, right, preferred_element_type=jnp.float32)
+
+
+def write_features(lab, left_ref, right_ref, feat_ref, featt_ref, sqt_ref, lab1_ref):
+    parts = split_exact(lab)
+    first = sum(mm(part, left_ref[...]) for part in parts[::-1])
+    second = sum(mm(part, right_ref[...]) for part in parts[::-1])
+    feat = first * second
+    feat_ref[...] = feat.astype(jnp.bfloat16)
+    featt_ref[...] = feat.T.astype(jnp.bfloat16)
+    sqt_ref[...] = (feat * feat).T.astype(jnp.bfloat16)
+    lab1_ref[...] = lab.astype(jnp.bfloat16)
+
+
+def features_kernel(lab_ref, left_ref, right_ref, *outs):
+    write_features(lab_ref[...], left_ref, right_ref, *outs)
+
+
+def update_kernel(count, lab_ref, here_ref, there_ref, left_ref, right_ref, new_ref, *outs):
+    lab = lab_ref[...]
+    stars, rows = lab.shape
+    total = here_ref[...] + there_ref[...]
+    lgrad = total[:, :rows]
+    lcurv = total[:, LANES : LANES + rows]
+    column = lax.broadcasted_iota(jnp.int32, lab.shape, 1)
+    inside = (column >= 1) & (column <= count)
+    lab = jnp.where(inside, lab + (lgrad - lab) / (1.0 + lcurv), lab)
+    new_ref[...] = lab
+    write_features(lab, left_ref, right_ref, *outs)
+
+
+def place(order, r):
+    bits = [(r >> bit) & 1 for bit in order]
+    spot = 0
+    for bit in bits[1:]:
+        spot = 2 * spot + bit
+    return bits[0], spot
+
+
+def load_chains(chains, refs, r):
+    rows = []
+    for index, chain in enumerate(chains):
+        upper, spot = place(chain["order"], r)
+        rows.append(refs[2 * index + upper][spot])
+    return jnp.concatenate(rows, axis=0)
+
+
+def swapped(bits):
+    return (bits & ~12) | ((bits & 4) << 1) | ((bits >> 1) & 4)
+
+
+def lanes_of(me_ref, r, width):
+    piece = (r + me_ref[1] * (swapped(r) - r)) ^ me_ref[0]
+    return pl.ds(pl.multiple_of(piece * width, width), width)
+
+
+def gradient_kernel(plan, from_coeffs, me_ref, flux_ref, ivar_ref, feat_ref, featt_ref, sqt_ref, *refs):
+    height = plan["height"]
+    if from_coeffs:
+        coeffs_ref, outs = refs[0], refs[1:]
+    else:
+        thetas, outs = refs[: 2 * len(plan["parts"])], refs[2 * len(plan["parts"]) :]
+    for r in range(plan["n"]):
+        lanes = lanes_of(me_ref, r, plan["lanes"])
+        if from_coeffs:
+            theta = coeffs_ref[:, lanes].astype(jnp.bfloat16)
+        else:
+            theta = load_chains(plan["parts"], thetas, r).astype(jnp.bfloat16)
+        ivar = ivar_ref[:, lanes]
+        model = mm(feat_ref[:, : theta.shape[0]], theta)
+        weighted = (
+            ivar.astype(jnp.float32) * (flux_ref[:, lanes].astype(jnp.float32) - model)
+        ).astype(jnp.bfloat16)
+        curv = mm(sqt_ref[...], ivar)
+        grad = mm(featt_ref[...], weighted)
+        for index, chain in enumerate(plan["sums"]):
+            upper, spot = place(chain["order"], r)
+            target = outs[2 * index + upper]
+            at = 0
+            for value, (first, stop) in ((curv, chain["curv"]), (grad, chain["grad"])):
+                if stop > first:
+                    target[spot, at : at + stop - first] = value[first:stop]
+                    at += stop - first
+
+
+def label_kernel(plan, count, last, me_ref, flux_ref, ivar_ref, feat_ref, lab1_ref, select_ref, *refs):
+    parts, width, group = plan["parts"], plan["lanes"], plan["group"]
+    thetas, refs = refs[: 2 * len(parts)], refs[2 * len(parts) :]
+    sums_ref, refs = refs[0], refs[1:]
+    if last:
+        new_ref, refs = refs[0], refs[1:]
+    theta_ref, blocks_ref, dots_ref, squares_ref, iv_ref = refs
+    stars = flux_ref.shape[0]
+    rows = lab1_ref.shape[1]
+    chunk = plan["chunk"]
+    height = theta_ref.shape[1]
+
+    for r in range(plan["n"]):
+        column = load_chains(parts, thetas, r)
+        if last:
+            new_ref[:, lanes_of(me_ref, r, width)] = column[: new_ref.shape[0]]
+        fill = jnp.zeros((height - column.shape[0], width), jnp.float32)
+        theta_ref[r] = jnp.concatenate([column, fill], axis=0).astype(jnp.bfloat16)
+    dots_ref[...] = jnp.zeros_like(dots_ref)
+    squares_ref[...] = jnp.zeros_like(squares_ref)
+
+    def some(step, carry):
+        for k in range(group):
+            r = step * group + k
+            lanes = lanes_of(me_ref, r, width)
+            theta = theta_ref[r]
+            ivar = ivar_ref[:, lanes].astype(jnp.float32)
+            iv_ref[k] = ivar
+            model = mm(feat_ref[...], theta)
+            weighted = (ivar * (flux_ref[:, lanes].astype(jnp.float32) - model)).astype(jnp.bfloat16)
+            dots_ref[...] += lax.dot_general(
+                weighted, theta, (((1,), (1,)), ((), ())), preferred_element_type=jnp.float32
+            )
+            blocks_ref[k] = mm(select_ref[...], theta).astype(jnp.bfloat16)
+        for label in range(count):
+            for at in range(0, stars, chunk):
+                total = squares_ref[label, at : at + chunk]
+                for k in range(group):
+                    jac = mm(lab1_ref[at : at + chunk], blocks_ref[k, label * rows : (label + 1) * rows])
+                    term = jac * jac * iv_ref[k, at : at + chunk]
+                    total += sum(term[:, lane : lane + LANES] for lane in range(0, width, LANES))
+                squares_ref[label, at : at + chunk] = total
+        return carry
+
+    lax.fori_loop(0, plan["n"] // group, some, 0)
+
+    dots = dots_ref[...]
+    column = lax.broadcasted_iota(jnp.int32, (stars, LANES), 1)
+    lgrad = jnp.zeros((stars, LANES), jnp.float32)
+    lcurv = jnp.zeros((stars, LANES), jnp.float32)
+    for label in range(count):
+        slopes = mm(lab1_ref[...], select_ref[label * rows : (label + 1) * rows])
+        here = column == 1 + label
+        lgrad = jnp.where(here, jnp.sum(slopes * dots, axis=1, keepdims=True), lgrad)
+        lcurv = jnp.where(here, jnp.sum(squares_ref[label], axis=1, keepdims=True), lcurv)
+    sums_ref[:, :LANES] = lgrad
+    sums_ref[:, LANES:] = lcurv
+
+
+def exchange(value, bit, n):
+    pairs = []
+    for device in range(n):
+        for side in range(2):
+            step = 1 << bit if side == 0 else swapped(1 << bit)
+            pairs.append((2 * device + side, 2 * (device ^ step) + side))
+    return lax.ppermute(value, ("star", "pix"), pairs)
+
+
+def pieces_device(plan, flux, inv_var, coeffs, labels):
+    n, parts, sums_of, width = plan["n"], plan["parts"], plan["sums"], plan["lanes"]
+    stars, pixels = flux.shape
+    count = labels.shape[1]
+    features = coeffs.shape[0]
+    padded = plan["padded"]
+    height = plan["height"]
+    left, right, select = feature_maps(count, padded)
+    rows = left.shape[0]
+    left = jnp.asarray(left, jnp.bfloat16)
+    right = jnp.asarray(right, jnp.bfloat16)
+    select = jnp.asarray(select, jnp.bfloat16)
+    me = lax.axis_index("star").astype(jnp.int32)
+    me_vec = jnp.stack([me, lax.axis_index("pix").astype(jnp.int32)])
+    params = pltpu.CompilerParams(vmem_limit_bytes=VMEM_LIMIT)
+    whole = pl.BlockSpec(memory_space=pltpu.VMEM)
+    scalar = pl.BlockSpec(memory_space=pltpu.SMEM)
+
+    feature_shapes = [
+        jax.ShapeDtypeStruct((stars, padded), jnp.bfloat16),
+        jax.ShapeDtypeStruct((padded, stars), jnp.bfloat16),
+        jax.ShapeDtypeStruct((padded, stars), jnp.bfloat16),
+        jax.ShapeDtypeStruct((stars, rows), jnp.bfloat16),
+    ]
+    lab = jnp.pad(
+        jnp.concatenate([jnp.ones((stars, 1), jnp.float32), labels], axis=1),
+        ((0, 0), (0, rows - 1 - count)),
+    )
+    feat, featt, sqt, lab1 = pl.pallas_call(
+        features_kernel,
+        out_shape=feature_shapes,
+        in_specs=[whole] * 3,
+        out_specs=[whole] * 4,
+        compiler_params=params,
+        name="features",
+    )(lab, left, right)
+
+    def call(kernel, name, shapes, flops, operands, scratch=()):
+        moved = sum(int(np.prod(a.shape)) * a.dtype.itemsize for a in list(operands) + list(shapes))
+        return pl.pallas_call(
+            kernel,
+            out_shape=shapes,
+            in_specs=[scalar] + [whole] * len(operands),
+            out_specs=[whole] * len(shapes),
+            scratch_shapes=list(scratch),
+            compiler_params=params,
+            cost_estimate=pl.CostEstimate(flops=flops, bytes_accessed=moved, transcendentals=0),
+            name=name,
+        )(me_vec, *operands)
+
+    halves = [
+        jax.ShapeDtypeStruct((n // 2, chain["rows"], width), jnp.float32)
+        for chain in sums_of
+        for _ in range(2)
+    ]
+
+    def reduced(keeps, sends, orders):
+        kept = [[keep] for keep in keeps]
+        outgoing = sends
+        size = n // 2
+        for step in range(len(orders[0])):
+            if step > 0:
+                size //= 2
+                outgoing = [sum(array[size : 2 * size] for array in arrays) for arrays in kept]
+            arrived = [exchange(value, order[step], n) for value, order in zip(outgoing, orders)]
+            for arrays, value in zip(kept, arrived):
+                arrays.append(value)
+        return [sum(array[0] for array in arrays) for arrays in kept]
+
+    def gathered(pieces, orders):
+        held = [piece[None] for piece in pieces]
+        for step in range(len(orders[0]) - 1, 0, -1):
+            arrived = [exchange(value, order[step], n) for value, order in zip(held, orders)]
+            held = [jnp.concatenate(both, axis=0) for both in zip(held, arrived)]
+        others = [exchange(value, order[0], n) for value, order in zip(held, orders)]
+        return [half for both in zip(held, others) for half in both]
+
+    base = lax.dynamic_slice(coeffs, (0, me * width), (features, width))
+    base = jnp.pad(base, ((0, height - features), (0, 0)))
+    own = [base[part["start"] : part["start"] + part["rows"]] for part in parts]
+    thetas = None
+    for turn in range(ALTS):
+        last = turn == ALTS - 1
+        known = [coeffs] if thetas is None else thetas
+        sums = call(
+            functools.partial(gradient_kernel, plan, thetas is None),
+            "gradient",
+            halves,
+            6 * stars * height * pixels,
+            [flux, inv_var, feat, featt, sqt] + known,
+        )
+        totals = reduced(sums[0::2], sums[1::2], [chain["order"] for chain in sums_of])
+
+        def rows_of(key, start, stop):
+            for chain, total in zip(sums_of, totals):
+                first, end = chain[key]
+                if first <= start and stop <= end:
+                    at = start - first + (chain["curv"][1] - chain["curv"][0] if key == "grad" else 0)
+                    return total[at : at + stop - start]
+
+        for index, part in enumerate(parts):
+            start, stop = part["start"], part["start"] + part["rows"]
+            own[index] = own[index] + step_size * rows_of("grad", start, stop) / (
+                1.0 + rows_of("curv", start, stop)
+            )
+        thetas = gathered(own, [part["order"] for part in parts])
+        shapes = [jax.ShapeDtypeStruct((stars, 2 * LANES), jnp.float32)]
+        if last:
+            shapes.append(jax.ShapeDtypeStruct((features, pixels), jnp.float32))
+        outs = call(
+            functools.partial(label_kernel, plan, count, last),
+            "labels",
+            shapes,
+            2 * stars * 256 * pixels * (count + 2),
+            [flux, inv_var, feat, lab1, select] + thetas,
+            [
+                pltpu.VMEM((n, padded, width), jnp.bfloat16),
+                pltpu.VMEM((plan["group"], count * rows, width), jnp.bfloat16),
+                pltpu.VMEM((stars, padded), jnp.float32),
+                pltpu.VMEM((count, stars, LANES), jnp.float32),
+                pltpu.VMEM((plan["group"], stars, width), jnp.float32),
+            ],
+        )
+        there = lax.ppermute(outs[0], "pix", plan["swap"])
+        lab, feat, featt, sqt, lab1 = pl.pallas_call(
+            functools.partial(update_kernel, count),
+            out_shape=[jax.ShapeDtypeStruct((stars, rows), jnp.float32)] + feature_shapes,
+            in_specs=[whole] * 5,
+            out_specs=[whole] * 5,
+            compiler_params=params,
+            name="update",
+        )(lab, outs[0], there, left, right)
+    return outs[1], lab[:, 1 : 1 + count]
+
+
+def make_plan(mesh, flux, coeffs):
+    n = mesh.shape["star"]
+    bits = n.bit_length() - 1
+    stars = flux.shape[0] // n
+    pixels = flux.shape[1] // mesh.shape["pix"]
+    if n != 1 << bits or bits < 4 or mesh.shape["pix"] != 2:
+        return None
+    if pixels % (n * LANES) or stars % 32:
+        return None
+    height = round_up(coeffs.shape[0], 8)
+    third = round_up(height // 3, 16)
+    cuts = [0, third, 2 * third, height]
+    rest = list(range(3, bits))
+    orders = [[0, 1, 2] + rest, [1, 2, 0] + rest, [2, 0, 1] + rest]
+    parts = [
+        {"start": cuts[i], "rows": cuts[i + 1] - cuts[i], "order": orders[i]} for i in range(3)
+    ]
+    sums = [
+        {"curv": (cuts[i], cuts[i + 1]), "grad": (cuts[i], cuts[i + 1]), "rows": 2 * parts[i]["rows"], "order": orders[i]}
+        for i in range(3)
+    ]
+    return {
+        "n": n,
+        "lanes": pixels // n,
+        "parts": parts,
+        "sums": sums,
+        "height": height,
+        "padded": round_up(coeffs.shape[0], 256),
+        "group": 4,
+        "chunk": stars // 2,
+        "swap": [(0, 1), (1, 0)],
+    }
+
+
 def solution(mesh):
     in_specs = (P("star", "pix"), P("star", "pix"), P(None, "pix"), P("star", None))
     out_specs = (P(None, "pix"), P("star", None))
-    return jax.shard_map(
-        per_device, mesh=mesh, in_specs=in_specs, out_specs=out_specs, check_vma=False
-    )
+
+    def run(flux, inv_var, coeffs, labels):
+        plan = make_plan(mesh, flux, coeffs)
+        body = plain_device if plan is None else functools.partial(pieces_device, plan)
+        return jax.shard_map(
+            body, mesh=mesh, in_specs=in_specs, out_specs=out_specs, check_vma=False
+        )(flux, inv_var, coeffs, labels)
+
+    return run

time: 827 us -> 310 us (0.37)
  waiting for transfers between devices: 477 us -> 174 us
  matrix products: 256 us -> 0 us
  Pallas kernels: 0 us -> 54 us
  starting transfers between devices: 0.08 us -> 54 us
  other arithmetic: 39.5 us -> 15.5 us
  local copies, waits for them, and re-layouts: 30.2 us -> 9.99 us
  between operations: 14.2 us -> 1.12 us
    psum x2 -> x0, waiting for transfers between devices: 477 us -> none  [per_device(): grad, curv = lax.psum((grad, curv), 'star')]
    dot_general x46 -> x0, matrix products: 256 us -> none  [the longest x40 226 us: per_label(): jnp.dot(lab_b, block, preferred_element_type=jnp.float32)]
    ppermute x0 -> x50, waiting for transfers between devices: none -> 174 us  [the longest x48 171 us: exchange(): return lax.ppermute(value, ('star', 'pix'), pairs)]
    ppermute x0 -> x50, starting transfers between devices: none -> 54 us  [the longest x48 53.9 us: exchange(): return lax.ppermute(value, ('star', 'pix'), pairs)]
    pallas_call x0 -> x7, Pallas kernels: none -> 54 us  [the longest x4 51.6 us: call(): pl.pallas_call(kernel, out_shape=shapes, in_specs=[scalar] + [whole] * le...]
    convert_element_type x9 -> x0, other arithmetic: 35.4 us -> none  [the longest x2 15.2 us: per_device(): theta_b = theta.astype(jnp.bfloat16)]
    gather x6 -> x0, local copies, waits for them, and re-layouts: 13.5 us -> none  [the longest x2 8.21 us: per_device(): theta_b[pair_table.reshape(-1)].astype(jnp.float32)]
    add x41 -> x26, other arithmetic: 1.5 us -> 14.8 us  [the longest x18 10.4 us: reduced(): sum((array[size:2 * size] for array in arrays))]
  transfers between devices with their start and end apart: 2 -> 50, of which waited for: 2 -> 33; matrix products, arithmetic and copies ran while one was open for 0% -> 5% of each run, Pallas kernels for 0% -> 0%
where the time goes in v3:
time: 310 us; the launch traced here: 309 us
  waiting for transfers between devices  174 us (56%)
  Pallas kernels  54 us (17%)
  starting transfers between devices  54 us (17%)
  other arithmetic  15.5 us (5%)
  local copies, waits for them, and re-layouts  9.99 us (3%)
    ppermute x48, waiting for transfers between devices, exchange(): return lax.ppermute(value, ('star', 'pix'), pairs)  171 us
    ppermute x48, starting transfers between devices, exchange(): return lax.ppermute(value, ('star', 'pix'), pairs)  53.9 us
    pallas_call x4, Pallas kernels, call(): pl.pallas_call(kernel, out_shape=shapes, in_specs=[scalar] + [whole] * le...  51.6 us
    add x18, other arithmetic, reduced(): sum((array[size:2 * size] for array in arrays))  10.4 us
    unnamed x38, local copies, waits for them, and re-layouts  8.83 us
  transfers between devices with their start and end apart: 50, of which 33 were waited for; matrix products, arithmetic and copies ran while one was open for 5% of the time, Pallas kernels for 0%

profile of v3, /device:TPU:0, one launch (start us, length us, event | category | flops | bytes accessed | tf_op | source)
XLA Modules:
  0.0 308.9 jit_solution(13448518944025293666)
XLA Ops:
  3.7 1.7 copy-done
  5.4 1.7 copy-done.2
  7.2 2.1 copy-done.4
  9.2 4.4 %gradient.2 = (f32[8,160,256]{2,1,0:T(8,128)S(1)}, f32[8,160,256]{2,1,0:T(8,128)S(1)}, f32[8,160,256]{2,1,0:T(8,128)S(1)}, f32[8,160,256]{2,1,0:T(8,128)S(1)}, f...) custom-call(s32[2]{0:T(128)S(1)} %pad_add_fusion.me_ref, bf16[320,4096]{1,0:T(8,128)(2,1)S(1)} %copy-done, ...), custom_call_target="tpu_custom_call" | custom-call | flops 1824522240 | bytes 17121280 | tf_op jit(solution)/shard_map/gradient/pallas_call | solution.py:311
  13.7 3.1 %collective-permute-start.16 = (f32[8,144,256]{2,1,0:T(8,128)S(1)}, f32[8,144,256]{2,1,0:T(8,128)S(1)}, u32[]{:S(2)}, u32[]{:S(2)}) collective-permute-start(f32[8,144,256]{2,1,0:T(8,128)S(1)} %get-tuple-element.35), channel_id=1, source_target_pairs={{0,8},{1,17},{2,10},{3,19},{4,12},{5,21},{6,14},{7,23},{8,0},{9,25... | collective-permute-start | bytes 3538952 | tf_op jit(solution)/shard_map/ppermute | solution.py:269
  19.8 23.4 %collective-permute-done.16 = f32[8,144,256]{2,1,0:T(8,128)S(1)} collective-permute-done((f32[8,144,256]{2,1,0:T(8,128)S(1)}, f32[8,144,256]{2,1,0:T(8,128)S(1)}, u32[]{:S(2)}, u32[]{:S(2)}) %collective-permute-start.16) | collective-permute-done | bytes 1179680 | tf_op jit(solution)/shard_map/ppermute | solution.py:269
  44.2 1.9 collective-permute-start.17
  46.1 2.2 collective-permute-done
  53.2 7.5 %collective-permute-done.17 = f32[4,144,256]{2,1,0:T(8,128)} collective-permute-done((f32[4,144,256]{2,1,0:T(8,128)}, f32[4,144,256]{2,1,0:T(8,128)}, u32[]{:S(2)}, u32[]{:S(2)}) %collective-permute-start.17) | collective-permute-done | bytes 589856 | tf_op jit(solution)/shard_map/ppermute | solution.py:269
  62.0 1.6 collective-permute-start.18
  63.6 3.5 %collective-permute-done.1 = f32[4,160,256]{2,1,0:T(8,128)} collective-permute-done((f32[4,160,256]{2,1,0:T(8,128)}, f32[4,160,256]{2,1,0:T(8,128)}, u32[]{:S(2)}, u32[]{:S(2)}) %collective-permute-start.1) | collective-permute-done | bytes 655392 | tf_op jit(solution)/shard_map/ppermute | solution.py:269
  73.8 6.2 %collective-permute-done.2 = f32[2,160,256]{2,1,0:T(8,128)S(1)} collective-permute-done((f32[2,160,256]{2,1,0:T(8,128)S(1)}, f32[2,160,256]{2,1,0:T(8,128)S(1)}, u32[]{:S(2)}, u32[]{:S(2)}) %collective-permute-start.2) | collective-permute-done | bytes 327712 | tf_op jit(solution)/shard_map/ppermute | solution.py:269
  81.0 1.6 collective-permute-start.3
  85.1 4.0 %collective-permute-done.3 = f32[1,160,256]{2,1,0:T(8,128)S(1)} collective-permute-done((f32[1,160,256]{2,1,0:T(8,128)S(1)}, f32[1,160,256]{2,1,0:T(8,128)S(1)}, u32[]{:S(2)}, u32[]{:S(2)}) %collective-permute-start.3) | collective-permute-done | bytes 163872 | tf_op jit(solution)/shard_map/ppermute | solution.py:269
  90.1 2.4 collective-permute-done.11
  95.7 3.0 collective-permute-start.4
  98.7 8.2 %collective-permute-done.12 = f32[1,80,256]{2,1,0:T(8,128)S(1)} collective-permute-done((f32[1,80,256]{2,1,0:T(8,128)S(1)}, f32[1,80,256]{2,1,0:T(8,128)S(1)}, u32[]{:S(2)}, u32[]{:S(2)}) %collective-permute-start.12) | collective-permute-done | bytes 81952 | tf_op jit(solution)/shard_map/ppermute | solution.py:269
  109.6 4.1 %collective-permute-done.13 = f32[2,80,256]{2,1,0:T(8,128)S(1)} collective-permute-done((f32[2,80,256]{2,1,0:T(8,128)S(1)}, f32[2,80,256]{2,1,0:T(8,128)S(1)}, u32[]{:S(2)}, u32[]{:S(2)}) %collective-permute-start.13) | collective-permute-done | bytes 163872 | tf_op jit(solution)/shard_map/ppermute | solution.py:269
  114.2 1.9 collective-permute-start.6
  116.1 4.7 %collective-permute-done.21 = f32[2,72,256]{2,1,0:T(8,128)S(1)} collective-permute-done((f32[2,72,256]{2,1,0:T(8,128)S(1)}, f32[2,72,256]{2,1,0:T(8,128)S(1)}, u32[]{:S(2)}, u32[]{:S(2)}) %collective-permute-start.21) | collective-permute-done | bytes 147488 | tf_op jit(solution)/shard_map/ppermute | solution.py:269
  122.9 3.8 %collective-permute-done.6 = f32[4,80,256]{2,1,0:T(8,128)S(1)} collective-permute-done((f32[4,80,256]{2,1,0:T(8,128)S(1)}, f32[4,80,256]{2,1,0:T(8,128)S(1)}, u32[]{:S(2)}, u32[]{:S(2)}) %collective-permute-start.6) | collective-permute-done | bytes 327712 | tf_op jit(solution)/shard_map/ppermute | solution.py:269
  129.4 8.5 %collective-permute-done.23.refs_5_ = f32[8,72,256]{2,1,0:T(8,128)S(1)} collective-permute-done((f32[8,72,256]{2,1,0:T(8,128)S(1)}, f32[8,72,256]{2,1,0:T(8,128)S(1)}, u32[]{:S(2)}, u32[]{:S(2)}) %collective-permute-start.23) | collective-permute-done | bytes 589856 | tf_op jit(solution)/shard_map/ppermute | solution.py:269
  138.0 21.1 %labels.2.here_ref = f32[320,256]{1,0:T(8,128)S(1)} custom-call(s32[2]{0:T(128)S(1)} %pad_add_fusion.me_ref, bf16[320,4096]{1,0:T(8,128)(2,1)S(1)} %copy-done.1, bf16[320,4096]{1,0:T(8,128)(2,1)S(1)} %copy-done.3, bf16[320,256]{1,0:T(8,128)(2,1)S(1)} %get-tuple-element.26.feat_ref, bf16[320,32]{1,0:T(8,128)(2,1)S(1)} %get-tuple-element.27.lab1_ref, ...), custom_call_target="tpu_custom_call" | custom-call | flops 14763950080 | bytes 9883648 | tf_op jit(solution)/shard_map/labels/pallas_call | solution.py:311
  159.2 1.6 collective-permute-done.24.there_ref
  161.3 4.4 %gradient.3 = (f32[8,160,256]{2,1,0:T(8,128)S(1)}, f32[8,160,256]{2,1,0:T(8,128)S(1)}, f32[8,160,256]{2,1,0:T(8,128)S(1)}, f32[8,160,256]{2,1,0:T(8,128)S(1)}, f...) custom-call(s32[2]{0:T(128)S(1)} %pad_add_fusion.me_ref, bf16[320,4096]{1,0:T(8,128)(2,1)S(1)} %copy-done.1, ...), custom_call_target="tpu_custom_call" | custom-call | flops 1824522240 | bytes 17137664 | tf_op jit(solution)/shard_map/gradient/pallas_call | solution.py:311
  168.6 26.1 %collective-permute-done.41 = f32[8,144,256]{2,1,0:T(8,128)S(1)} collective-permute-done((f32[8,144,256]{2,1,0:T(8,128)S(1)}, f32[8,144,256]{2,1,0:T(8,128)S(1)}, u32[]{:S(2)}, u32[]{:S(2)}) %collective-permute-start.41) | collective-permute-done | bytes 1179680 | tf_op jit(solution)/shard_map/ppermute | solution.py:269
  195.6 2.3 collective-permute-done.25
  199.5 1.7 collective-permute-start.34
  201.2 8.8 %collective-permute-done.42 = f32[4,144,256]{2,1,0:T(8,128)S(1)} collective-permute-done((f32[4,144,256]{2,1,0:T(8,128)S(1)}, f32[4,144,256]{2,1,0:T(8,128)S(1)}, u32[]{:S(2)}, u32[]{:S(2)}) %collective-permute-start.42) | collective-permute-done | bytes 589856 | tf_op jit(solution)/shard_map/ppermute | solution.py:269
  210.0 1.9 collective-permute-start.43
  211.9 3.6 %collective-permute-done.26 = f32[4,160,256]{2,1,0:T(8,128)S(1)} collective-permute-done((f32[4,160,256]{2,1,0:T(8,128)S(1)}, f32[4,160,256]{2,1,0:T(8,128)S(1)}, u32[]{:S(2)}, u32[]{:S(2)}) %collective-permute-start.26) | collective-permute-done | bytes 655392 | tf_op jit(solution)/shard_map/ppermute | solution.py:269
  216.3 4.2 %collective-permute-done.43 = f32[2,144,256]{2,1,0:T(8,128)S(1)} collective-permute-done((f32[2,144,256]{2,1,0:T(8,128)S(1)}, f32[2,144,256]{2,1,0:T(8,128)S(1)}, u32[]{:S(2)}, u32[]{:S(2)}) %collective-permute-start.43) | collective-permute-done | bytes 294944 | tf_op jit(solution)/shard_map/ppermute | solution.py:269
  220.6 2.0 collective-permute-start.44
  223.0 5.3 %collective-permute-done.44 = f32[1,144,256]{2,1,0:T(8,128)S(1)} collective-permute-done((f32[1,144,256]{2,1,0:T(8,128)S(1)}, f32[1,144,256]{2,1,0:T(8,128)S(1)}, u32[]{:S(2)}, u32[]{:S(2)}) %collective-permute-start.44) | collective-permute-done | bytes 147488 | tf_op jit(solution)/shard_map/ppermute | solution.py:269
  230.3 3.1 %collective-permute-start.36 = (f32[1,160,256]{2,1,0:T(8,128)S(1)}, f32[1,160,256]{2,1,0:T(8,128)S(1)}, u32[]{:S(2)}, u32[]{:S(2)}) collective-permute-start(f32[1,160,256]{2,1,0:T(8,128)S(1)} %slice_add_fusion.18), channel_id=1, source_target_pairs={{0,16},{1,9},{2,18},{3,11},{4,20},{5,13},{6,22},{7,15},{8,24},{9,1... | collective-permute-start | bytes 491528 | tf_op jit(solution)/shard_map/ppermute | solution.py:269
  233.4 3.5 %collective-permute-done.28 = f32[1,160,256]{2,1,0:T(8,128)S(1)} collective-permute-done((f32[1,160,256]{2,1,0:T(8,128)S(1)}, f32[1,160,256]{2,1,0:T(8,128)S(1)}, u32[]{:S(2)}, u32[]{:S(2)}) %collective-permute-start.28) | collective-permute-done | bytes 163872 | tf_op jit(solution)/shard_map/ppermute | solution.py:269
  237.5 2.6 collective-permute-done.36
  240.5 5.4 %collective-permute-done.29 = f32[1,80,256]{2,1,0:T(8,128)S(1)} collective-permute-done((f32[1,80,256]{2,1,0:T(8,128)S(1)}, f32[1,80,256]{2,1,0:T(8,128)S(1)}, u32[]{:S(2)}, u32[]{:S(2)}) %collective-permute-start.29) | collective-permute-done | bytes 81952 | tf_op jit(solution)/shard_map/ppermute | solution.py:269
  246.0 2.8 collective-permute-start.45
  250.3 1.8 collective-permute-done.30
  252.1 1.7 collective-permute-start.31
  255.6 5.2 %collective-permute-done.46 = f32[2,72,256]{2,1,0:T(8,128)S(1)} collective-permute-done((f32[2,72,256]{2,1,0:T(8,128)S(1)}, f32[2,72,256]{2,1,0:T(8,128)S(1)}, u32[]{:S(2)}, u32[]{:S(2)}) %collective-permute-start.46) | collective-permute-done | bytes 147488 | tf_op jit(solution)/shard_map/ppermute | solution.py:269
  261.2 1.9 collective-permute-start.32
  263.3 1.7 collective-permute-start.40
  265.0 5.8 %collective-permute-done.47 = f32[4,72,256]{2,1,0:T(8,128)S(1)} collective-permute-done((f32[4,72,256]{2,1,0:T(8,128)S(1)}, f32[4,72,256]{2,1,0:T(8,128)S(1)}, u32[]{:S(2)}, u32[]{:S(2)}) %collective-permute-start.47) | collective-permute-done | bytes 294944 | tf_op jit(solution)/shard_map/ppermute | solution.py:269
  271.0 12.5 %collective-permute-done.48.refs_5_ = f32[8,72,256]{2,1,0:T(8,128)S(1)} collective-permute-done((f32[8,72,256]{2,1,0:T(8,128)S(1)}, f32[8,72,256]{2,1,0:T(8,128)S(1)}, u32[]{:S(2)}, u32[]{:S(2)}) %collective-permute-start.48) | collective-permute-done | bytes 589856 | tf_op jit(solution)/shard_map/ppermute | solution.py:269
  283.5 21.7 %labels.3 = (f32[320,256]{1,0:T(8,128)S(1)}, f32[231,4096]{1,0:T(8,128)}) custom-call(s32[2]{0:T(128)S(1)} %pad_add_fusion.me_ref, bf16[320,4096]{1,0:T(8,128)(2,1)S(1)} %copy-done.1, bf16[320,4096]{1,0:T(8,128)(2,1)S(1)} %copy-done.3, bf16[320,256]{1,0:T(8,128)(2,1)S(1)} %get-tuple-element.36.feat_ref, bf16[320,32]{1,0:T(8,128)(2,1)S(1)} %get-tuple-element.37.lab1_ref, ...), custom_call_target="tpu_custom_call" | custom-call | flops 14763950080 | bytes 13668352 | tf_op jit(solution)/shard_map/labels/pallas_call | solution.py:311
  305.2 1.6 collective-permute-done.49.there_ref
  (148 shorter events, 52.1 us)
Async XLA Ops:
  13.7 29.5 %collective-permute-start.16 = (f32[8,144,256]{2,1,0:T(8,128)S(1)}, f32[8,144,256]{2,1,0:T(8,128)S(1)}, u32[]{:S(2)}, u32[]{:S(2)}) collective-permute-start(f32[8,144,256]{2,1,0:T(8,128)S(1)} %get-tuple-element.35), channel_id=1, source_target_pairs={{0,8},{1,17},{2,10},{3,19},{4,12},{5,21},{6,14},{7,23},{8,0},{9,25... | collective-permute-start | bytes 3538952 | tf_op jit(solution)/shard_map/ppermute | solution.py:269
  16.8 31.6 %collective-permute-start = (f32[8,160,256]{2,1,0:T(8,128)S(1)}, f32[8,160,256]{2,1,0:T(8,128)S(1)}, u32[]{:S(2)}, u32[]{:S(2)}) collective-permute-start(f32[8,160,256]{2,1,0:T(8,128)S(1)} %get-tuple-element.31), channel_id=1, source_target_pairs={{0,2},{1,3},{2,0},{3,1},{4,6},{5,7},{6,4},{7,5},{8,10},{9,11},{10,... | collective-permute-start | bytes 3932168 | tf_op jit(solution)/shard_map/ppermute | solution.py:269
  18.3 32.6 %collective-permute-start.8 = (f32[8,160,256]{2,1,0:T(8,128)S(1)}, f32[8,160,256]{2,1,0:T(8,128)S(1)}, u32[]{:S(2)}, u32[]{:S(2)}) collective-permute-start(f32[8,160,256]{2,1,0:T(8,128)S(1)} %get-tuple-element.33), channel_id=1, source_target_pairs={{0,4},{1,5},{2,6},{3,7},{4,0},{5,1},{6,2},{7,3},{8,12},{9,13},{10,... | collective-permute-start | bytes 3932168 | tf_op jit(solution)/shard_map/ppermute | solution.py:269
  44.2 16.6 %collective-permute-start.17 = (f32[4,144,256]{2,1,0:T(8,128)}, f32[4,144,256]{2,1,0:T(8,128)}, u32[]{:S(2)}, u32[]{:S(2)}) collective-permute-start(f32[4,144,256]{2,1,0:T(8,128)} %slice_add_fusion.5), channel_id=1, source_target_pairs={{0,2},{1,3},{2,0},{3,1},{4,6},{5,7},{6,4},{7,5},{8,10},{9,11},{10,... | collective-permute-start | bytes 1769480 | tf_op jit(solution)/shard_map/ppermute | solution.py:269
  49.4 17.6 %collective-permute-start.1 = (f32[4,160,256]{2,1,0:T(8,128)}, f32[4,160,256]{2,1,0:T(8,128)}, u32[]{:S(2)}, u32[]{:S(2)}) collective-permute-start(f32[4,160,256]{2,1,0:T(8,128)} %slice_add_fusion.3), channel_id=1, source_target_pairs={{0,4},{1,5},{2,6},{3,7},{4,0},{5,1},{6,2},{7,3},{8,12},{9,13},{10,... | collective-permute-start | bytes 1966088 | tf_op jit(solution)/shard_map/ppermute | solution.py:269
  52.2 17.3 %collective-permute-start.9 = (f32[4,160,256]{2,1,0:T(8,128)}, f32[4,160,256]{2,1,0:T(8,128)}, u32[]{:S(2)}, u32[]{:S(2)}) collective-permute-start(f32[4,160,256]{2,1,0:T(8,128)} %slice_add_fusion.2), channel_id=1, source_target_pairs={{0,8},{1,17},{2,10},{3,19},{4,12},{5,21},{6,14},{7,23},{8,0},{9,25... | collective-permute-start | bytes 1966088 | tf_op jit(solution)/shard_map/ppermute | solution.py:269
  62.0 10.2 %collective-permute-start.18 = (f32[2,144,256]{2,1,0:T(8,128)S(1)}, f32[2,144,256]{2,1,0:T(8,128)S(1)}, u32[]{:S(2)}, u32[]{:S(2)}) collective-permute-start(f32[2,144,256]{2,1,0:T(8,128)S(1)} %slice_add_fusion.16), channel_id=1, source_target_pairs={{0,4},{1,5},{2,6},{3,7},{4,0},{5,1},{6,2},{7,3},{8,12},{9,13},{10,... | collective-permute-start | bytes 884744 | tf_op jit(solution)/shard_map/ppermute | solution.py:269
  68.2 11.8 %collective-permute-start.2 = (f32[2,160,256]{2,1,0:T(8,128)S(1)}, f32[2,160,256]{2,1,0:T(8,128)S(1)}, u32[]{:S(2)}, u32[]{:S(2)}) collective-permute-start(f32[2,160,256]{2,1,0:T(8,128)S(1)} %slice_add_fusion.12), channel_id=1, source_target_pairs={{0,8},{1,17},{2,10},{3,19},{4,12},{5,21},{6,14},{7,23},{8,0},{9,25... | collective-permute-start | bytes 983048 | tf_op jit(solution)/shard_map/ppermute | solution.py:269
  70.7 11.9 %collective-permute-start.10 = (f32[2,160,256]{2,1,0:T(8,128)S(1)}, f32[2,160,256]{2,1,0:T(8,128)S(1)}, u32[]{:S(2)}, u32[]{:S(2)}) collective-permute-start(f32[2,160,256]{2,1,0:T(8,128)S(1)} %slice_add_fusion.10), channel_id=1, source_target_pairs={{0,2},{1,3},{2,0},{3,1},{4,6},{5,7},{6,4},{7,5},{8,10},{9,11},{10,... | collective-permute-start | bytes 983048 | tf_op jit(solution)/shard_map/ppermute | solution.py:269
  73.3 21.4 %collective-permute-start.19 = (f32[1,144,256]{2,1,0:T(8,128)S(1)}, f32[1,144,256]{2,1,0:T(8,128)S(1)}, u32[]{:S(2)}, u32[]{:S(2)}) collective-permute-start(f32[1,144,256]{2,1,0:T(8,128)S(1)} %slice_add_fusion.48), channel_id=1, source_target_pairs={{0,16},{1,9},{2,18},{3,11},{4,20},{5,13},{6,22},{7,15},{8,24},{9,1... | collective-permute-start | bytes 442376 | tf_op jit(solution)/shard_map/ppermute | solution.py:269
  81.0 8.1 %collective-permute-start.3 = (f32[1,160,256]{2,1,0:T(8,128)S(1)}, f32[1,160,256]{2,1,0:T(8,128)S(1)}, u32[]{:S(2)}, u32[]{:S(2)}) collective-permute-start(f32[1,160,256]{2,1,0:T(8,128)S(1)} %slice_add_fusion.36), channel_id=1, source_target_pairs={{0,16},{1,9},{2,18},{3,11},{4,20},{5,13},{6,22},{7,15},{8,24},{9,1... | collective-permute-start | bytes 491528 | tf_op jit(solution)/shard_map/ppermute | solution.py:269
  83.6 8.9 %collective-permute-start.11 = (f32[1,160,256]{2,1,0:T(8,128)S(1)}, f32[1,160,256]{2,1,0:T(8,128)S(1)}, u32[]{:S(2)}, u32[]{:S(2)}) collective-permute-start(f32[1,160,256]{2,1,0:T(8,128)S(1)} %slice_add_fusion.30), channel_id=1, source_target_pairs={{0,16},{1,9},{2,18},{3,11},{4,20},{5,13},{6,22},{7,15},{8,24},{9,1... | collective-permute-start | bytes 491528 | tf_op jit(solution)/shard_map/ppermute | solution.py:269
  94.6 12.4 %collective-permute-start.12 = (f32[1,80,256]{2,1,0:T(8,128)S(1)}, f32[1,80,256]{2,1,0:T(8,128)S(1)}, u32[]{:S(2)}, u32[]{:S(2)}) collective-permute-start(f32[1,80,256]{2,1,0:T(8,128)S(1)} %bitcast.41), channel_id=1, source_target_pairs={{0,16},{1,9},{2,18},{3,11},{4,20},{5,13},{6,22},{7,15},{8,24},{9,1... | collective-permute-start | bytes 245768 | tf_op jit(solution)/shard_map/ppermute | solution.py:269
  95.7 12.9 %collective-permute-start.4 = (f32[1,80,256]{2,1,0:T(8,128)S(1)}, f32[1,80,256]{2,1,0:T(8,128)S(1)}, u32[]{:S(2)}, u32[]{:S(2)}) collective-permute-start(f32[1,80,256]{2,1,0:T(8,128)S(1)} %bitcast.45), channel_id=1, source_target_pairs={{0,16},{1,9},{2,18},{3,11},{4,20},{5,13},{6,22},{7,15},{8,24},{9,1... | collective-permute-start | bytes 245768 | tf_op jit(solution)/shard_map/ppermute | solution.py:269
  106.9 6.8 %collective-permute-start.13 = (f32[2,80,256]{2,1,0:T(8,128)S(1)}, f32[2,80,256]{2,1,0:T(8,128)S(1)}, u32[]{:S(2)}, u32[]{:S(2)}) collective-permute-start(f32[2,80,256]{2,1,0:T(8,128)S(1)} %pad_maximum_fusion.13), channel_id=1, source_target_pairs={{0,2},{1,3},{2,0},{3,1},{4,6},{5,7},{6,4},{7,5},{8,10},{9,11},{10,... | collective-permute-start | bytes 491528 | tf_op jit(solution)/shard_map/ppermute | solution.py:269
  107.0 6.8 %collective-permute-start.20 = (f32[1,72,256]{2,1,0:T(8,128)S(1)}, f32[1,72,256]{2,1,0:T(8,128)S(1)}, u32[]{:S(2)}, u32[]{:S(2)}) collective-permute-start(f32[1,72,256]{2,1,0:T(8,128)S(1)} %bitcast.49), channel_id=1, source_target_pairs={{0,16},{1,9},{2,18},{3,11},{4,20},{5,13},{6,22},{7,15},{8,24},{9,1... | collective-permute-start | bytes 221192 | tf_op jit(solution)/shard_map/ppermute | solution.py:269
  108.7 5.5 %collective-permute-start.5 = (f32[2,80,256]{2,1,0:T(8,128)S(1)}, f32[2,80,256]{2,1,0:T(8,128)S(1)}, u32[]{:S(2)}, u32[]{:S(2)}) collective-permute-start(f32[2,80,256]{2,1,0:T(8,128)S(1)} %pad_maximum_fusion.12), channel_id=1, source_target_pairs={{0,8},{1,17},{2,10},{3,19},{4,12},{5,21},{6,14},{7,23},{8,0},{9,25... | collective-permute-start | bytes 491528 | tf_op jit(solution)/shard_map/ppermute | solution.py:269
  113.8 8.9 %collective-permute-start.14 = (f32[4,80,256]{2,1,0:T(8,128)S(1)}, f32[4,80,256]{2,1,0:T(8,128)S(1)}, u32[]{:S(2)}, u32[]{:S(2)}) collective-permute-start(f32[4,80,256]{2,1,0:T(8,128)S(1)} %pad_maximum_fusion.7), channel_id=1, source_target_pairs={{0,8},{1,17},{2,10},{3,19},{4,12},{5,21},{6,14},{7,23},{8,0},{9,25... | collective-permute-start | bytes 983048 | tf_op jit(solution)/shard_map/ppermute | solution.py:269
  113.9 6.9 %collective-permute-start.21 = (f32[2,72,256]{2,1,0:T(8,128)S(1)}, f32[2,72,256]{2,1,0:T(8,128)S(1)}, u32[]{:S(2)}, u32[]{:S(2)}) collective-permute-start(f32[2,72,256]{2,1,0:T(8,128)S(1)} %pad_maximum_fusion.16), channel_id=1, source_target_pairs={{0,4},{1,5},{2,6},{3,7},{4,0},{5,1},{6,2},{7,3},{8,12},{9,13},{10,... | collective-permute-start | bytes 442376 | tf_op jit(solution)/shard_map/ppermute | solution.py:269
  114.2 12.4 %collective-permute-start.6 = (f32[4,80,256]{2,1,0:T(8,128)S(1)}, f32[4,80,256]{2,1,0:T(8,128)S(1)}, u32[]{:S(2)}, u32[]{:S(2)}) collective-permute-start(f32[4,80,256]{2,1,0:T(8,128)S(1)} %pad_maximum_fusion.6), channel_id=1, source_target_pairs={{0,4},{1,5},{2,6},{3,7},{4,0},{5,1},{6,2},{7,3},{8,12},{9,13},{10,... | collective-permute-start | bytes 983048 | tf_op jit(solution)/shard_map/ppermute | solution.py:269
  120.8 7.1 %collective-permute-start.22 = (f32[4,72,256]{2,1,0:T(8,128)S(1)}, f32[4,72,256]{2,1,0:T(8,128)S(1)}, u32[]{:S(2)}, u32[]{:S(2)}) collective-permute-start(f32[4,72,256]{2,1,0:T(8,128)S(1)} %pad_maximum_fusion.10), channel_id=1, source_target_pairs={{0,2},{1,3},{2,0},{3,1},{4,6},{5,7},{6,4},{7,5},{8,10},{9,11},{10,... | collective-permute-start | bytes 884744 | tf_op jit(solution)/shard_map/ppermute | solution.py:269
  122.8 15.1 %collective-permute-start.15 = (f32[8,80,256]{2,1,0:T(8,128)S(1)}, f32[8,80,256]{2,1,0:T(8,128)S(1)}, u32[]{:S(2)}, u32[]{:S(2)}) collective-permute-start(f32[8,80,256]{2,1,0:T(8,128)S(1)} %pad_maximum_fusion.1.refs_2_), channel_id=1, source_target_pairs={{0,4},{1,5},{2,6},{3,7},{4,0},{5,1},{6,2},{7,3},{8,12},{9,13},{10,... | collective-permute-start | bytes 1966088 | tf_op jit(solution)/shard_map/ppermute | solution.py:269
  126.7 11.2 %collective-permute-start.7 = (f32[8,80,256]{2,1,0:T(8,128)S(1)}, f32[8,80,256]{2,1,0:T(8,128)S(1)}, u32[]{:S(2)}, u32[]{:S(2)}) collective-permute-start(f32[8,80,256]{2,1,0:T(8,128)S(1)} %pad_maximum_fusion.refs_0_), channel_id=1, source_target_pairs={{0,2},{1,3},{2,0},{3,1},{4,6},{5,7},{6,4},{7,5},{8,10},{9,11},{10,... | collective-permute-start | bytes 1966088 | tf_op jit(solution)/shard_map/ppermute | solution.py:269
  128.0 9.9 %collective-permute-start.23 = (f32[8,72,256]{2,1,0:T(8,128)S(1)}, f32[8,72,256]{2,1,0:T(8,128)S(1)}, u32[]{:S(2)}, u32[]{:S(2)}) collective-permute-start(f32[8,72,256]{2,1,0:T(8,128)S(1)} %pad_maximum_fusion.4.refs_4_), channel_id=1, source_target_pairs={{0,8},{1,17},{2,10},{3,19},{4,12},{5,21},{6,14},{7,23},{8,0},{9,25... | collective-permute-start | bytes 1769480 | tf_op jit(solution)/shard_map/ppermute | solution.py:269
  165.8 28.9 %collective-permute-start.41 = (f32[8,144,256]{2,1,0:T(8,128)S(1)}, f32[8,144,256]{2,1,0:T(8,128)S(1)}, u32[]{:S(2)}, u32[]{:S(2)}) collective-permute-start(f32[8,144,256]{2,1,0:T(8,128)S(1)} %get-tuple-element.45), channel_id=1, source_target_pairs={{0,8},{1,17},{2,10},{3,19},{4,12},{5,21},{6,14},{7,23},{8,0},{9,25... | collective-permute-start | bytes 3538952 | tf_op jit(solution)/shard_map/ppermute | solution.py:269
  167.3 30.7 %collective-permute-start.25 = (f32[8,160,256]{2,1,0:T(8,128)S(1)}, f32[8,160,256]{2,1,0:T(8,128)S(1)}, u32[]{:S(2)}, u32[]{:S(2)}) collective-permute-start(f32[8,160,256]{2,1,0:T(8,128)S(1)} %get-tuple-element.41), channel_id=1, source_target_pairs={{0,2},{1,3},{2,0},{3,1},{4,6},{5,7},{6,4},{7,5},{8,10},{9,11},{10,... | collective-permute-start | bytes 3932168 | tf_op jit(solution)/shard_map/ppermute | solution.py:269
  167.3 32.1 %collective-permute-start.33 = (f32[8,160,256]{2,1,0:T(8,128)S(1)}, f32[8,160,256]{2,1,0:T(8,128)S(1)}, u32[]{:S(2)}, u32[]{:S(2)}) collective-permute-start(f32[8,160,256]{2,1,0:T(8,128)S(1)} %get-tuple-element.43), channel_id=1, source_target_pairs={{0,4},{1,5},{2,6},{3,7},{4,0},{5,1},{6,2},{7,3},{8,12},{9,13},{10,... | collective-permute-start | bytes 3932168 | tf_op jit(solution)/shard_map/ppermute | solution.py:269
  194.8 15.1 %collective-permute-start.42 = (f32[4,144,256]{2,1,0:T(8,128)S(1)}, f32[4,144,256]{2,1,0:T(8,128)S(1)}, u32[]{:S(2)}, u32[]{:S(2)}) collective-permute-start(f32[4,144,256]{2,1,0:T(8,128)S(1)} %slice_add_fusion.4), channel_id=1, source_target_pairs={{0,2},{1,3},{2,0},{3,1},{4,6},{5,7},{6,4},{7,5},{8,10},{9,11},{10,... | collective-permute-start | bytes 1769480 | tf_op jit(solution)/shard_map/ppermute | solution.py:269
  198.1 17.5 %collective-permute-start.26 = (f32[4,160,256]{2,1,0:T(8,128)S(1)}, f32[4,160,256]{2,1,0:T(8,128)S(1)}, u32[]{:S(2)}, u32[]{:S(2)}) collective-permute-start(f32[4,160,256]{2,1,0:T(8,128)S(1)} %slice_add_fusion.1), channel_id=1, source_target_pairs={{0,4},{1,5},{2,6},{3,7},{4,0},{5,1},{6,2},{7,3},{8,12},{9,13},{10,... | collective-permute-start | bytes 1966088 | tf_op jit(solution)/shard_map/ppermute | solution.py:269
  199.5 23.0 %collective-permute-start.34 = (f32[4,160,256]{2,1,0:T(8,128)S(1)}, f32[4,160,256]{2,1,0:T(8,128)S(1)}, u32[]{:S(2)}, u32[]{:S(2)}) collective-permute-start(f32[4,160,256]{2,1,0:T(8,128)S(1)} %slice_add_fusion), channel_id=1, source_target_pairs={{0,8},{1,17},{2,10},{3,19},{4,12},{5,21},{6,14},{7,23},{8,0},{9,25... | collective-permute-start | bytes 1966088 | tf_op jit(solution)/shard_map/ppermute | solution.py:269
  210.0 10.5 %collective-permute-start.43 = (f32[2,144,256]{2,1,0:T(8,128)S(1)}, f32[2,144,256]{2,1,0:T(8,128)S(1)}, u32[]{:S(2)}, u32[]{:S(2)}) collective-permute-start(f32[2,144,256]{2,1,0:T(8,128)S(1)} %slice_add_fusion.14), channel_id=1, source_target_pairs={{0,4},{1,5},{2,6},{3,7},{4,0},{5,1},{6,2},{7,3},{8,12},{9,13},{10,... | collective-permute-start | bytes 884744 | tf_op jit(solution)/shard_map/ppermute | solution.py:269
  215.6 12.8 %collective-permute-start.27 = (f32[2,160,256]{2,1,0:T(8,128)S(1)}, f32[2,160,256]{2,1,0:T(8,128)S(1)}, u32[]{:S(2)}, u32[]{:S(2)}) collective-permute-start(f32[2,160,256]{2,1,0:T(8,128)S(1)} %slice_add_fusion.8), channel_id=1, source_target_pairs={{0,8},{1,17},{2,10},{3,19},{4,12},{5,21},{6,14},{7,23},{8,0},{9,25... | collective-permute-start | bytes 983048 | tf_op jit(solution)/shard_map/ppermute | solution.py:269
  220.6 7.8 %collective-permute-start.44 = (f32[1,144,256]{2,1,0:T(8,128)S(1)}, f32[1,144,256]{2,1,0:T(8,128)S(1)}, u32[]{:S(2)}, u32[]{:S(2)}) collective-permute-start(f32[1,144,256]{2,1,0:T(8,128)S(1)} %slice_add_fusion.42), channel_id=1, source_target_pairs={{0,16},{1,9},{2,18},{3,11},{4,20},{5,13},{6,22},{7,15},{8,24},{9,1... | collective-permute-start | bytes 442376 | tf_op jit(solution)/shard_map/ppermute | solution.py:269
  222.6 7.6 %collective-permute-start.35 = (f32[2,160,256]{2,1,0:T(8,128)S(1)}, f32[2,160,256]{2,1,0:T(8,128)S(1)}, u32[]{:S(2)}, u32[]{:S(2)}) collective-permute-start(f32[2,160,256]{2,1,0:T(8,128)S(1)} %slice_add_fusion.6), channel_id=1, source_target_pairs={{0,2},{1,3},{2,0},{3,1},{4,6},{5,7},{6,4},{7,5},{8,10},{9,11},{10,... | collective-permute-start | bytes 983048 | tf_op jit(solution)/shard_map/ppermute | solution.py:269
  228.5 8.5 %collective-permute-start.28 = (f32[1,160,256]{2,1,0:T(8,128)S(1)}, f32[1,160,256]{2,1,0:T(8,128)S(1)}, u32[]{:S(2)}, u32[]{:S(2)}) collective-permute-start(f32[1,160,256]{2,1,0:T(8,128)S(1)} %slice_add_fusion.24), channel_id=1, source_target_pairs={{0,16},{1,9},{2,18},{3,11},{4,20},{5,13},{6,22},{7,15},{8,24},{9,1... | collective-permute-start | bytes 491528 | tf_op jit(solution)/shard_map/ppermute | solution.py:269
  230.3 9.7 %collective-permute-start.36 = (f32[1,160,256]{2,1,0:T(8,128)S(1)}, f32[1,160,256]{2,1,0:T(8,128)S(1)}, u32[]{:S(2)}, u32[]{:S(2)}) collective-permute-start(f32[1,160,256]{2,1,0:T(8,128)S(1)} %slice_add_fusion.18), channel_id=1, source_target_pairs={{0,16},{1,9},{2,18},{3,11},{4,20},{5,13},{6,22},{7,15},{8,24},{9,1... | collective-permute-start | bytes 491528 | tf_op jit(solution)/shard_map/ppermute | solution.py:269
  237.1 8.8 %collective-permute-start.29 = (f32[1,80,256]{2,1,0:T(8,128)S(1)}, f32[1,80,256]{2,1,0:T(8,128)S(1)}, u32[]{:S(2)}, u32[]{:S(2)}) collective-permute-start(f32[1,80,256]{2,1,0:T(8,128)S(1)} %fusion.13), channel_id=1, source_target_pairs={{0,16},{1,9},{2,18},{3,11},{4,20},{5,13},{6,22},{7,15},{8,24},{9,1... | collective-permute-start | bytes 245768 | tf_op jit(solution)/shard_map/ppermute | solution.py:269
  240.1 8.7 %collective-permute-start.37 = (f32[1,80,256]{2,1,0:T(8,128)S(1)}, f32[1,80,256]{2,1,0:T(8,128)S(1)}, u32[]{:S(2)}, u32[]{:S(2)}) collective-permute-start(f32[1,80,256]{2,1,0:T(8,128)S(1)} %fusion.9), channel_id=1, source_target_pairs={{0,16},{1,9},{2,18},{3,11},{4,20},{5,13},{6,22},{7,15},{8,24},{9,1... | collective-permute-start | bytes 245768 | tf_op jit(solution)/shard_map/ppermute | solution.py:269
  245.9 6.2 %collective-permute-start.30 = (f32[2,80,256]{2,1,0:T(8,128)S(1)}, f32[2,80,256]{2,1,0:T(8,128)S(1)}, u32[]{:S(2)}, u32[]{:S(2)}) collective-permute-start(f32[2,80,256]{2,1,0:T(8,128)S(1)} %pad_maximum_fusion.14), channel_id=1, source_target_pairs={{0,8},{1,17},{2,10},{3,19},{4,12},{5,21},{6,14},{7,23},{8,0},{9,25... | collective-permute-start | bytes 491528 | tf_op jit(solution)/shard_map/ppermute | solution.py:269
  246.0 7.8 %collective-permute-start.45 = (f32[1,72,256]{2,1,0:T(8,128)S(1)}, f32[1,72,256]{2,1,0:T(8,128)S(1)}, u32[]{:S(2)}, u32[]{:S(2)}) collective-permute-start(f32[1,72,256]{2,1,0:T(8,128)S(1)} %fusion.24), channel_id=1, source_target_pairs={{0,16},{1,9},{2,18},{3,11},{4,20},{5,13},{6,22},{7,15},{8,24},{9,1... | collective-permute-start | bytes 221192 | tf_op jit(solution)/shard_map/ppermute | solution.py:269
  248.9 5.4 %collective-permute-start.38 = (f32[2,80,256]{2,1,0:T(8,128)S(1)}, f32[2,80,256]{2,1,0:T(8,128)S(1)}, u32[]{:S(2)}, u32[]{:S(2)}) collective-permute-start(f32[2,80,256]{2,1,0:T(8,128)S(1)} %pad_maximum_fusion.15), channel_id=1, source_target_pairs={{0,2},{1,3},{2,0},{3,1},{4,6},{5,7},{6,4},{7,5},{8,10},{9,11},{10,... | collective-permute-start | bytes 491528 | tf_op jit(solution)/shard_map/ppermute | solution.py:269
  252.1 9.0 %collective-permute-start.31 = (f32[4,80,256]{2,1,0:T(8,128)S(1)}, f32[4,80,256]{2,1,0:T(8,128)S(1)}, u32[]{:S(2)}, u32[]{:S(2)}) collective-permute-start(f32[4,80,256]{2,1,0:T(8,128)S(1)} %pad_maximum_fusion.8), channel_id=1, source_target_pairs={{0,4},{1,5},{2,6},{3,7},{4,0},{5,1},{6,2},{7,3},{8,12},{9,13},{10,... | collective-permute-start | bytes 983048 | tf_op jit(solution)/shard_map/ppermute | solution.py:269
  253.8 7.0 %collective-permute-start.46 = (f32[2,72,256]{2,1,0:T(8,128)S(1)}, f32[2,72,256]{2,1,0:T(8,128)S(1)}, u32[]{:S(2)}, u32[]{:S(2)}) collective-permute-start(f32[2,72,256]{2,1,0:T(8,128)S(1)} %pad_maximum_fusion.17), channel_id=1, source_target_pairs={{0,4},{1,5},{2,6},{3,7},{4,0},{5,1},{6,2},{7,3},{8,12},{9,13},{10,... | collective-permute-start | bytes 442376 | tf_op jit(solution)/shard_map/ppermute | solution.py:269
  254.3 9.0 %collective-permute-start.39 = (f32[4,80,256]{2,1,0:T(8,128)S(1)}, f32[4,80,256]{2,1,0:T(8,128)S(1)}, u32[]{:S(2)}, u32[]{:S(2)}) collective-permute-start(f32[4,80,256]{2,1,0:T(8,128)S(1)} %pad_maximum_fusion.9), channel_id=1, source_target_pairs={{0,8},{1,17},{2,10},{3,19},{4,12},{5,21},{6,14},{7,23},{8,0},{9,25... | collective-permute-start | bytes 983048 | tf_op jit(solution)/shard_map/ppermute | solution.py:269
  260.8 10.0 %collective-permute-start.47 = (f32[4,72,256]{2,1,0:T(8,128)S(1)}, f32[4,72,256]{2,1,0:T(8,128)S(1)}, u32[]{:S(2)}, u32[]{:S(2)}) collective-permute-start(f32[4,72,256]{2,1,0:T(8,128)S(1)} %pad_maximum_fusion.11), channel_id=1, source_target_pairs={{0,2},{1,3},{2,0},{3,1},{4,6},{5,7},{6,4},{7,5},{8,10},{9,11},{10,... | collective-permute-start | bytes 884744 | tf_op jit(solution)/shard_map/ppermute | solution.py:269
  261.2 22.3 %collective-permute-start.32 = (f32[8,80,256]{2,1,0:T(8,128)S(1)}, f32[8,80,256]{2,1,0:T(8,128)S(1)}, u32[]{:S(2)}, u32[]{:S(2)}) collective-permute-start(f32[8,80,256]{2,1,0:T(8,128)S(1)} %pad_maximum_fusion.2.refs_0_), channel_id=1, source_target_pairs={{0,2},{1,3},{2,0},{3,1},{4,6},{5,7},{6,4},{7,5},{8,10},{9,11},{10,... | collective-permute-start | bytes 1966088 | tf_op jit(solution)/shard_map/ppermute | solution.py:269
  263.3 20.1 %collective-permute-start.40 = (f32[8,80,256]{2,1,0:T(8,128)S(1)}, f32[8,80,256]{2,1,0:T(8,128)S(1)}, u32[]{:S(2)}, u32[]{:S(2)}) collective-permute-start(f32[8,80,256]{2,1,0:T(8,128)S(1)} %pad_maximum_fusion.3.refs_2_), channel_id=1, source_target_pairs={{0,4},{1,5},{2,6},{3,7},{4,0},{5,1},{6,2},{7,3},{8,12},{9,13},{10,... | collective-permute-start | bytes 1966088 | tf_op jit(solution)/shard_map/ppermute | solution.py:269
  270.9 12.6 %collective-permute-start.48 = (f32[8,72,256]{2,1,0:T(8,128)S(1)}, f32[8,72,256]{2,1,0:T(8,128)S(1)}, u32[]{:S(2)}, u32[]{:S(2)}) collective-permute-start(f32[8,72,256]{2,1,0:T(8,128)S(1)} %pad_maximum_fusion.5.refs_4_), channel_id=1, source_target_pairs={{0,8},{1,17},{2,10},{3,19},{4,12},{5,21},{6,14},{7,23},{8,0},{9,25... | collective-permute-start | bytes 1769480 | tf_op jit(solution)/shard_map/ppermute | solution.py:269
  (20 other events, 266.6 us)

commit v4 on v3

--- a/solution.py
+++ b/solution.py
@@ -11,6 +11,8 @@
 ALTS = 2
 LANES = 128
 VMEM_LIMIT = 16 * 1024 * 1024
+BLOCKS = 4
+FIRST_LIMIT = 46 * 1024 * 1024
 
 step_size = 0.25
 
@@ -92,18 +94,18 @@
     rows = round_up(1 + count, 32)
     left = np.zeros((rows, padded), np.float32)
     right = np.zeros((rows, padded), np.float32)
-    left[0, 0] = 1.0
-    right[0, : 1 + count] = 1.0
+    left[count, 0] = 1.0
+    right[count, : 1 + count] = 1.0
     for label in range(count):
-        left[1 + label, 1 + label] = 1.0
+        left[label, 1 + label] = 1.0
     for position in range(len(left_index)):
-        left[1 + left_index[position], 1 + count + position] = 1.0
-        right[1 + right_index[position], 1 + count + position] = 1.0
+        left[left_index[position], 1 + count + position] = 1.0
+        right[right_index[position], 1 + count + position] = 1.0
     select = np.zeros((count, rows, padded), np.float32)
     for label in range(count):
-        select[label, 0, 1 + label] = 1.0
+        select[label, count, 1 + label] = 1.0
         for other in range(count):
-            select[label, 1 + other, pair_table[label, other]] = doubling[label, other]
+            select[label, other, pair_table[label, other]] = doubling[label, other]
     return left, right, select.reshape(count * rows, padded)
 
 
@@ -130,21 +132,24 @@
     lab1_ref[...] = lab.astype(jnp.bfloat16)
 
 
-def features_kernel(lab_ref, left_ref, right_ref, *outs):
-    write_features(lab_ref[...], left_ref, right_ref, *outs)
-
-
-def update_kernel(count, lab_ref, here_ref, there_ref, left_ref, right_ref, new_ref, *outs):
+def updated(count, lab_ref, here_ref, there_ref):
     lab = lab_ref[...]
-    stars, rows = lab.shape
+    rows = lab.shape[1]
     total = here_ref[...] + there_ref[...]
     lgrad = total[:, :rows]
     lcurv = total[:, LANES : LANES + rows]
     column = lax.broadcasted_iota(jnp.int32, lab.shape, 1)
-    inside = (column >= 1) & (column <= count)
-    lab = jnp.where(inside, lab + (lgrad - lab) / (1.0 + lcurv), lab)
+    return jnp.where(column < count, lab + (lgrad - lab) / (1.0 + lcurv), lab)
+
+
+def update_kernel(count, lab_ref, here_ref, there_ref, left_ref, right_ref, new_ref, *outs):
+    lab = updated(count, lab_ref, here_ref, there_ref)
     new_ref[...] = lab
     write_features(lab, left_ref, right_ref, *outs)
+
+
+def final_kernel(count, lab_ref, here_ref, there_ref, new_ref):
+    new_ref[...] = updated(count, lab_ref, here_ref, there_ref).T[:count]
 
 
 def place(order, r):
@@ -172,33 +177,79 @@
     return pl.ds(pl.multiple_of(piece * width, width), width)
 
 
-def gradient_kernel(plan, from_coeffs, me_ref, flux_ref, ivar_ref, feat_ref, featt_ref, sqt_ref, *refs):
-    height = plan["height"]
-    if from_coeffs:
-        coeffs_ref, outs = refs[0], refs[1:]
-    else:
-        thetas, outs = refs[: 2 * len(plan["parts"])], refs[2 * len(plan["parts"]) :]
+def store_sums(plan, outs, r, key, value):
+    for index, chain in enumerate(plan["sums"]):
+        upper, spot = place(chain["order"], r)
+        first, stop = chain["curv"]
+        at = stop - first if key == "grad" else 0
+        first, stop = chain[key]
+        outs[2 * index + upper][spot, at : at + stop - first] = value[first:stop]
+
+
+def weighted_rest(flux, ivar, theta, feat_ref):
+    model = mm(feat_ref[:, : theta.shape[0]], theta.astype(jnp.bfloat16))
+    return (ivar.astype(jnp.float32) * (flux.astype(jnp.float32) - model)).astype(jnp.bfloat16)
+
+
+def row_copies(source, target, sems, first, blocks):
+    rows = source.shape[0]
+    size = round_up(rows // blocks, 16)
+    copies = []
+    for at in range(0, rows, size):
+        span = pl.ds(at, min(size, rows - at))
+        copies.append(pltpu.make_async_copy(source.at[span], target.at[span], sems.at[first + len(copies)]))
+    return copies
+
+
+def first_kernel(plan, count, me_ref, labels_ref, flux_ref, ivar_ref, coeffs_ref, left_ref, right_ref, *refs):
+    lab_ref, feat_ref, featt_ref, sqt_ref, lab1_ref = refs[:5]
+    outs, refs = refs[5 : 5 + 2 * len(plan["sums"])], refs[5 + 2 * len(plan["sums"]) :]
+    flux_here, ivar_here, coeffs_here, left_here, right_here, rows_ref, sems = refs
+    pairs = (
+        (left_ref, left_here, 1),
+        (right_ref, right_here, 1),
+        (ivar_ref, ivar_here, BLOCKS),
+        (coeffs_ref, coeffs_here, BLOCKS),
+        (flux_ref, flux_here, BLOCKS),
+    )
+    copies = [
+        row_copies(source, target, sems, (BLOCKS + 1) * index, blocks)
+        for index, (source, target, blocks) in enumerate(pairs)
+    ]
+    for group in copies:
+        for copy in group:
+            copy.start()
+    rows_ref[...] = jnp.where(
+        lax.broadcasted_iota(jnp.int32, rows_ref.shape, 0) == count, 1.0, 0.0
+    )
+    rows_ref[:count] = labels_ref[...]
+    lab = rows_ref[...].T
+    lab_ref[...] = lab
+    for copy in copies[0] + copies[1]:
+        copy.wait()
+    write_features(lab, left_here, right_here, feat_ref, featt_ref, sqt_ref, lab1_ref)
+    for copy in copies[2]:
+        copy.wait()
     for r in range(plan["n"]):
         lanes = lanes_of(me_ref, r, plan["lanes"])
-        if from_coeffs:
-            theta = coeffs_ref[:, lanes].astype(jnp.bfloat16)
-        else:
-            theta = load_chains(plan["parts"], thetas, r).astype(jnp.bfloat16)
+        store_sums(plan, outs, r, "curv", mm(sqt_ref[...], ivar_here[:, lanes]))
+    for copy in copies[3] + copies[4]:
+        copy.wait()
+    for r in range(plan["n"]):
+        lanes = lanes_of(me_ref, r, plan["lanes"])
+        rest = weighted_rest(flux_here[:, lanes], ivar_here[:, lanes], coeffs_here[:, lanes], feat_ref)
+        store_sums(plan, outs, r, "grad", mm(featt_ref[...], rest))
+
+
+def gradient_kernel(plan, me_ref, flux_ref, ivar_ref, feat_ref, featt_ref, sqt_ref, *refs):
+    thetas, outs = refs[: 2 * len(plan["parts"])], refs[2 * len(plan["parts"]) :]
+    for r in range(plan["n"]):
+        lanes = lanes_of(me_ref, r, plan["lanes"])
+        theta = load_chains(plan["parts"], thetas, r)
         ivar = ivar_ref[:, lanes]
-        model = mm(feat_ref[:, : theta.shape[0]], theta)
-        weighted = (
-            ivar.astype(jnp.float32) * (flux_ref[:, lanes].astype(jnp.float32) - model)
-        ).astype(jnp.bfloat16)
-        curv = mm(sqt_ref[...], ivar)
-        grad = mm(featt_ref[...], weighted)
-        for index, chain in enumerate(plan["sums"]):
-            upper, spot = place(chain["order"], r)
-            target = outs[2 * index + upper]
-            at = 0
-            for value, (first, stop) in ((curv, chain["curv"]), (grad, chain["grad"])):
-                if stop > first:
-                    target[spot, at : at + stop - first] = value[first:stop]
-                    at += stop - first
+        rest = weighted_rest(flux_ref[:, lanes], ivar, theta, feat_ref)
+        store_sums(plan, outs, r, "curv", mm(sqt_ref[...], ivar))
+        store_sums(plan, outs, r, "grad", mm(featt_ref[...], rest))
 
 
 def label_kernel(plan, count, last, me_ref, flux_ref, ivar_ref, feat_ref, lab1_ref, select_ref, *refs):
@@ -253,7 +304,7 @@
     lcurv = jnp.zeros((stars, LANES), jnp.float32)
     for label in range(count):
         slopes = mm(lab1_ref[...], select_ref[label * rows : (label + 1) * rows])
-        here = column == 1 + label
+        here = column == label
         lgrad = jnp.where(here, jnp.sum(slopes * dots, axis=1, keepdims=True), lgrad)
         lcurv = jnp.where(here, jnp.sum(squares_ref[label], axis=1, keepdims=True), lcurv)
     sums_ref[:, :LANES] = lgrad
@@ -293,28 +344,15 @@
         jax.ShapeDtypeStruct((padded, stars), jnp.bfloat16),
         jax.ShapeDtypeStruct((stars, rows), jnp.bfloat16),
     ]
-    lab = jnp.pad(
-        jnp.concatenate([jnp.ones((stars, 1), jnp.float32), labels], axis=1),
-        ((0, 0), (0, rows - 1 - count)),
-    )
-    feat, featt, sqt, lab1 = pl.pallas_call(
-        features_kernel,
-        out_shape=feature_shapes,
-        in_specs=[whole] * 3,
-        out_specs=[whole] * 4,
-        compiler_params=params,
-        name="features",
-    )(lab, left, right)
-
-    def call(kernel, name, shapes, flops, operands, scratch=()):
+    def call(kernel, name, shapes, flops, operands, scratch=(), specs=None, limit=VMEM_LIMIT):
         moved = sum(int(np.prod(a.shape)) * a.dtype.itemsize for a in list(operands) + list(shapes))
         return pl.pallas_call(
             kernel,
             out_shape=shapes,
-            in_specs=[scalar] + [whole] * len(operands),
+            in_specs=[scalar] + (specs or [whole] * len(operands)),
             out_specs=[whole] * len(shapes),
             scratch_shapes=list(scratch),
-            compiler_params=params,
+            compiler_params=pltpu.CompilerParams(vmem_limit_bytes=limit),
             cost_estimate=pl.CostEstimate(flops=flops, bytes_accessed=moved, transcendentals=0),
             name=name,
         )(me_vec, *operands)
@@ -326,17 +364,17 @@
     ]
 
     def reduced(keeps, sends, orders):
-        kept = [[keep] for keep in keeps]
-        outgoing = sends
-        size = n // 2
-        for step in range(len(orders[0])):
-            if step > 0:
-                size //= 2
-                outgoing = [sum(array[size : 2 * size] for array in arrays) for arrays in kept]
-            arrived = [exchange(value, order[step], n) for value, order in zip(outgoing, orders)]
-            for arrays, value in zip(kept, arrived):
-                arrays.append(value)
-        return [sum(array[0] for array in arrays) for arrays in kept]
+        totals = []
+        for kept, outgoing, order in zip(keeps, sends, orders):
+            for bit in order:
+                arrived = exchange(outgoing, bit, n)
+                size = kept.shape[0] // 2
+                if size == 0:
+                    totals.append(kept[0] + arrived[0])
+                else:
+                    outgoing = kept[size:] + arrived[size:]
+                    kept = kept[:size] + arrived[:size]
+        return totals
 
     def gathered(pieces, orders):
         held = [piece[None] for piece in pieces]
@@ -352,14 +390,36 @@
     thetas = None
     for turn in range(ALTS):
         last = turn == ALTS - 1
-        known = [coeffs] if thetas is None else thetas
-        sums = call(
-            functools.partial(gradient_kernel, plan, thetas is None),
-            "gradient",
-            halves,
-            6 * stars * height * pixels,
-            [flux, inv_var, feat, featt, sqt] + known,
-        )
+        if turn == 0:
+            hbm = pl.BlockSpec(memory_space=pltpu.HBM)
+            outs = call(
+                functools.partial(first_kernel, plan, count),
+                "first",
+                [jax.ShapeDtypeStruct((stars, rows), jnp.float32)] + feature_shapes + halves,
+                6 * stars * height * pixels,
+                [labels.T, flux, inv_var, coeffs, left, right],
+                [
+                    pltpu.VMEM(flux.shape, flux.dtype),
+                    pltpu.VMEM(inv_var.shape, inv_var.dtype),
+                    pltpu.VMEM(coeffs.shape, coeffs.dtype),
+                    pltpu.VMEM(left.shape, left.dtype),
+                    pltpu.VMEM(right.shape, right.dtype),
+                    pltpu.VMEM((rows, stars), jnp.float32),
+                    pltpu.SemaphoreType.DMA((5 * (BLOCKS + 1),)),
+                ],
+                [whole] + [hbm] * 5,
+                FIRST_LIMIT,
+            )
+            lab, feat, featt, sqt, lab1 = outs[:5]
+            sums = outs[5:]
+        else:
+            sums = call(
+                functools.partial(gradient_kernel, plan),
+                "gradient",
+                halves,
+                6 * stars * height * pixels,
+                [flux, inv_var, feat, featt, sqt] + thetas,
+            )
         totals = reduced(sums[0::2], sums[1::2], [chain["order"] for chain in sums_of])
 
         def rows_of(key, start, stop):
@@ -393,15 +453,25 @@
             ],
         )
         there = lax.ppermute(outs[0], "pix", plan["swap"])
-        lab, feat, featt, sqt, lab1 = pl.pallas_call(
-            functools.partial(update_kernel, count),
-            out_shape=[jax.ShapeDtypeStruct((stars, rows), jnp.float32)] + feature_shapes,
-            in_specs=[whole] * 5,
-            out_specs=[whole] * 5,
-            compiler_params=params,
-            name="update",
-        )(lab, outs[0], there, left, right)
-    return outs[1], lab[:, 1 : 1 + count]
+        if last:
+            new_labels = pl.pallas_call(
+                functools.partial(final_kernel, count),
+                out_shape=jax.ShapeDtypeStruct((count, stars), jnp.float32),
+                in_specs=[whole] * 3,
+                out_specs=whole,
+                compiler_params=params,
+                name="final",
+            )(lab, outs[0], there)
+        else:
+            lab, feat, featt, sqt, lab1 = pl.pallas_call(
+                functools.partial(update_kernel, count),
+                out_shape=[jax.ShapeDtypeStruct((stars, rows), jnp.float32)] + feature_shapes,
+                in_specs=[whole] * 5,
+                out_specs=[whole] * 5,
+                compiler_params=params,
+                name="update",
+            )(lab, outs[0], there, left, right)
+    return outs[1], new_labels.T
 
 
 def make_plan(mesh, flux, coeffs):

time: 310 us -> 304 us (0.981)
  starting transfers between devices: 54 us -> 73.3 us
  waiting for transfers between devices: 174 us -> 160 us
  local copies, waits for them, and re-layouts: 9.99 us -> 3.26 us
  other arithmetic: 15.5 us -> 9.6 us
    ppermute x48, starting transfers between devices: 53.9 us -> 73.2 us  [exchange(): return lax.ppermute(value, ('star', 'pix'), pairs)]
    ppermute x48, waiting for transfers between devices: 171 us -> 156 us  [exchange(): return lax.ppermute(value, ('star', 'pix'), pairs)]
    unnamed x38 -> x18, local copies, waits for them, and re-layouts: 8.83 us -> 2.23 us
    add x24, other arithmetic: 13.8 us -> 7.98 us  [the longest x12 7.65 us: reduced(): kept = kept[:size] + arrived[:size]]
    pallas_call x5, Pallas kernels: 52.2 us -> 56 us  [the longest x4 55.3 us: call(): pl.pallas_call(kernel, out_shape=shapes, in_specs=[scalar] + (specs or [w...]
  transfers between devices with their start and end apart: 50 -> 50, of which waited for: 33 -> 33; matrix products, arithmetic and copies ran while one was open for 5% -> 3% of each run, Pallas kernels for 0% -> 0%
where the time goes in v4:
time: 304 us; the launch traced here: 303 us
  waiting for transfers between devices  160 us (53%)
  starting transfers between devices  73.3 us (24%)
  Pallas kernels  56.6 us (19%)
  other arithmetic  9.6 us (3%)
  local copies, waits for them, and re-layouts  3.26 us (1%)
    ppermute x48, waiting for transfers between devices, exchange(): return lax.ppermute(value, ('star', 'pix'), pairs)  156 us
    ppermute x48, starting transfers between devices, exchange(): return lax.ppermute(value, ('star', 'pix'), pairs)  73.2 us
    pallas_call x4, Pallas kernels, call(): pl.pallas_call(kernel, out_shape=shapes, in_specs=[scalar] + (specs or [w...  55.3 us
    add x12, other arithmetic, reduced(): kept = kept[:size] + arrived[:size]  7.65 us
  transfers between devices with their start and end apart: 50, of which 33 were waited for; matrix products, arithmetic and copies ran while one was open for 3% of the time, Pallas kernels for 0%

profile of v4, /device:TPU:0, one launch (start us, length us, event | category | flops | bytes accessed | tf_op | source)
XLA Modules:
  0.0 303.4 jit_solution(15835414603673556845)
XLA Ops:
  2.9 8.4 %first.1 = (f32[320,32]{1,0:T(8,128)S(1)}, bf16[320,256]{1,0:T(8,128)(2,1)S(1)}, bf16[256,320]{1,0:T(8,128)(2,1)}, bf16[256,320]{1,0:T(8,128)(2,1)}, bf16[320,32...) custom-call(s32[2]{0:T(128)S(1)} %pad_add_fusion.me_ref, ...), custom_call_target="tpu_custom_call" | custom-call | flops 1824522240 | bytes 17241088 | tf_op jit(solution)/shard_map/first/pallas_call | solution.py:349
  11.3 3.1 %collective-permute-start.16 = (f32[8,144,256]{2,1,0:T(8,128)S(1)}, f32[8,144,256]{2,1,0:T(8,128)S(1)}, u32[]{:S(2)}, u32[]{:S(2)}) collective-permute-start(f32[8,144,256]{2,1,0:T(8,128)S(1)} %get-tuple-element.32), channel_id=1, source_target_pairs={{0,8},{1,17},{2,10},{3,19},{4,12},{5,21},{6,14},{7,23},{8,0},{9,25... | collective-permute-start | bytes 3538952 | tf_op jit(solution)/shard_map/ppermute | solution.py:320
  17.4 23.4 %collective-permute-done.16 = f32[8,144,256]{2,1,0:T(8,128)S(1)} collective-permute-done((f32[8,144,256]{2,1,0:T(8,128)S(1)}, f32[8,144,256]{2,1,0:T(8,128)S(1)}, u32[]{:S(2)}, u32[]{:S(2)}) %collective-permute-start.16) | collective-permute-done | bytes 1179680 | tf_op jit(solution)/shard_map/ppermute | solution.py:320
  41.8 1.9 collective-permute-start.17
  43.7 2.3 collective-permute-done
  50.8 7.6 %collective-permute-done.17 = f32[4,144,256]{2,1,0:T(8,128)} collective-permute-done((f32[4,144,256]{2,1,0:T(8,128)}, f32[4,144,256]{2,1,0:T(8,128)}, u32[]{:S(2)}, u32[]{:S(2)}) %collective-permute-start.17) | collective-permute-done | bytes 589856 | tf_op jit(solution)/shard_map/ppermute | solution.py:320
  59.6 1.6 collective-permute-start.18
  61.1 4.0 %collective-permute-done.1 = f32[4,160,256]{2,1,0:T(8,128)} collective-permute-done((f32[4,160,256]{2,1,0:T(8,128)}, f32[4,160,256]{2,1,0:T(8,128)}, u32[]{:S(2)}, u32[]{:S(2)}) %collective-permute-start.1) | collective-permute-done | bytes 655392 | tf_op jit(solution)/shard_map/ppermute | solution.py:320
  70.4 8.7 %collective-permute-done.2 = f32[2,160,256]{2,1,0:T(8,128)S(1)} collective-permute-done((f32[2,160,256]{2,1,0:T(8,128)S(1)}, f32[2,160,256]{2,1,0:T(8,128)S(1)}, u32[]{:S(2)}, u32[]{:S(2)}) %collective-permute-start.2) | collective-permute-done | bytes 327712 | tf_op jit(solution)/shard_map/ppermute | solution.py:320
  79.9 2.3 collective-permute-start.11
  82.2 5.4 %collective-permute-done.3 = f32[1,160,256]{2,1,0:T(8,128)S(1)} collective-permute-done((f32[1,160,256]{2,1,0:T(8,128)S(1)}, f32[1,160,256]{2,1,0:T(8,128)S(1)}, u32[]{:S(2)}, u32[]{:S(2)}) %collective-permute-start.3) | collective-permute-done | bytes 163872 | tf_op jit(solution)/shard_map/ppermute | solution.py:320
  87.6 2.8 collective-permute-done.11
  91.5 3.0 collective-permute-start.4
  94.5 7.8 %collective-permute-done.12 = f32[1,80,256]{2,1,0:T(8,128)S(1)} collective-permute-done((f32[1,80,256]{2,1,0:T(8,128)S(1)}, f32[1,80,256]{2,1,0:T(8,128)S(1)}, u32[]{:S(2)}, u32[]{:S(2)}) %collective-permute-start.12) | collective-permute-done | bytes 81952 | tf_op jit(solution)/shard_map/ppermute | solution.py:320
  104.1 2.1 collective-permute-start.5
  108.9 3.2 %collective-permute-start.21 = (f32[2,72,256]{2,1,0:T(8,128)S(1)}, f32[2,72,256]{2,1,0:T(8,128)S(1)}, u32[]{:S(2)}, u32[]{:S(2)}) collective-permute-start(f32[2,72,256]{2,1,0:T(8,128)S(1)} %pad_maximum_fusion.16), channel_id=1, source_target_pairs={{0,4},{1,5},{2,6},{3,7},{4,0},{5,1},{6,2},{7,3},{8,12},{9,13},{10,... | collective-permute-start | bytes 442376 | tf_op jit(solution)/shard_map/ppermute | solution.py:320
  112.8 4.0 %collective-permute-done.21 = f32[2,72,256]{2,1,0:T(8,128)S(1)} collective-permute-done((f32[2,72,256]{2,1,0:T(8,128)S(1)}, f32[2,72,256]{2,1,0:T(8,128)S(1)}, u32[]{:S(2)}, u32[]{:S(2)}) %collective-permute-start.21) | collective-permute-done | bytes 147488 | tf_op jit(solution)/shard_map/ppermute | solution.py:320
  117.7 3.7 %collective-permute-start.15 = (f32[8,80,256]{2,1,0:T(8,128)S(1)}, f32[8,80,256]{2,1,0:T(8,128)S(1)}, u32[]{:S(2)}, u32[]{:S(2)}) collective-permute-start(f32[8,80,256]{2,1,0:T(8,128)S(1)} %pad_maximum_fusion.1.refs_2_), channel_id=1, source_target_pairs={{0,4},{1,5},{2,6},{3,7},{4,0},{5,1},{6,2},{7,3},{8,12},{9,13},{10,... | collective-permute-start | bytes 1966088 | tf_op jit(solution)/shard_map/ppermute | solution.py:320
  121.3 1.9 collective-permute-done.6
  125.8 8.6 %collective-permute-done.23.refs_5_ = f32[8,72,256]{2,1,0:T(8,128)S(1)} collective-permute-done((f32[8,72,256]{2,1,0:T(8,128)S(1)}, f32[8,72,256]{2,1,0:T(8,128)S(1)}, u32[]{:S(2)}, u32[]{:S(2)}) %collective-permute-start.23) | collective-permute-done | bytes 589856 | tf_op jit(solution)/shard_map/ppermute | solution.py:320
  134.4 21.1 %labels.2.here_ref = f32[320,256]{1,0:T(8,128)S(1)} custom-call(s32[2]{0:T(128)S(1)} %pad_add_fusion.me_ref, bf16[320,4096]{1,0:T(8,128)(2,1)S(1)} %copy-done, bf16[320,4096]{1,0:T(8,128)(2,1)S(1)} %copy-done.1, bf16[320,256]{1,0:T(8,128)(2,1)S(1)} %get-tuple-element.25.feat_ref, bf16[320,32]{1,0:T(8,128)(2,1)S(1)} %get-tuple-element.26.lab1_ref, ...), custom_call_target="tpu_custom_call" | custom-call | flops 14763950080 | bytes 9883648 | tf_op jit(solution)/shard_map/labels/pallas_call | solution.py:349
  155.6 1.6 collective-permute-done.24.there_ref
  157.8 4.5 %gradient.1 = (f32[8,160,256]{2,1,0:T(8,128)S(1)}, f32[8,160,256]{2,1,0:T(8,128)S(1)}, f32[8,160,256]{2,1,0:T(8,128)S(1)}, f32[8,160,256]{2,1,0:T(8,128)S(1)}, f...) custom-call(s32[2]{0:T(128)S(1)} %pad_add_fusion.me_ref, bf16[320,4096]{1,0:T(8,128)(2,1)S(1)} %copy-done, ...), custom_call_target="tpu_custom_call" | custom-call | flops 1824522240 | bytes 17137664 | tf_op jit(solution)/shard_map/gradient/pallas_call | solution.py:349
  164.3 2.0 collective-permute-start.33
  166.3 24.8 %collective-permute-done.41 = f32[8,144,256]{2,1,0:T(8,128)S(1)} collective-permute-done((f32[8,144,256]{2,1,0:T(8,128)S(1)}, f32[8,144,256]{2,1,0:T(8,128)S(1)}, u32[]{:S(2)}, u32[]{:S(2)}) %collective-permute-start.41) | collective-permute-done | bytes 1179680 | tf_op jit(solution)/shard_map/ppermute | solution.py:320
  192.3 2.4 collective-permute-done.25
  194.9 2.5 collective-permute-start.26
  197.8 8.8 %collective-permute-done.42 = f32[4,144,256]{2,1,0:T(8,128)S(1)} collective-permute-done((f32[4,144,256]{2,1,0:T(8,128)S(1)}, f32[4,144,256]{2,1,0:T(8,128)S(1)}, u32[]{:S(2)}, u32[]{:S(2)}) %collective-permute-start.42) | collective-permute-done | bytes 589856 | tf_op jit(solution)/shard_map/ppermute | solution.py:320
  206.6 1.8 collective-permute-start.43
  208.5 2.4 collective-permute-done.26
  211.0 3.0 collective-permute-start.27
  213.9 2.0 collective-permute-done.43
  216.0 2.4 collective-permute-start.44
  219.4 3.1 %collective-permute-done.44 = f32[1,144,256]{2,1,0:T(8,128)S(1)} collective-permute-done((f32[1,144,256]{2,1,0:T(8,128)S(1)}, f32[1,144,256]{2,1,0:T(8,128)S(1)}, u32[]{:S(2)}, u32[]{:S(2)}) %collective-permute-start.44) | collective-permute-done | bytes 147488 | tf_op jit(solution)/shard_map/ppermute | solution.py:320
  222.5 3.7 %collective-permute-start.28 = (f32[1,160,256]{2,1,0:T(8,128)S(1)}, f32[1,160,256]{2,1,0:T(8,128)S(1)}, u32[]{:S(2)}, u32[]{:S(2)}) collective-permute-start(f32[1,160,256]{2,1,0:T(8,128)S(1)} %slice_add_fusion.26), channel_id=1, source_target_pairs={{0,16},{1,9},{2,18},{3,11},{4,20},{5,13},{6,22},{7,15},{8,24},{9,1... | collective-permute-start | bytes 491528 | tf_op jit(solution)/shard_map/ppermute | solution.py:320
  226.2 1.9 collective-permute-done.35
  230.5 3.4 %collective-permute-start.29 = (f32[1,80,256]{2,1,0:T(8,128)S(1)}, f32[1,80,256]{2,1,0:T(8,128)S(1)}, u32[]{:S(2)}, u32[]{:S(2)}) collective-permute-start(f32[1,80,256]{2,1,0:T(8,128)S(1)} %fusion.13), channel_id=1, source_target_pairs={{0,16},{1,9},{2,18},{3,11},{4,20},{5,13},{6,22},{7,15},{8,24},{9,1... | collective-permute-start | bytes 245768 | tf_op jit(solution)/shard_map/ppermute | solution.py:320
  233.9 2.1 collective-permute-done.36
  237.1 5.2 %collective-permute-start.30 = (f32[2,80,256]{2,1,0:T(8,128)S(1)}, f32[2,80,256]{2,1,0:T(8,128)S(1)}, u32[]{:S(2)}, u32[]{:S(2)}) collective-permute-start(f32[2,80,256]{2,1,0:T(8,128)S(1)} %pad_maximum_fusion.14), channel_id=1, source_target_pairs={{0,8},{1,17},{2,10},{3,19},{4,12},{5,21},{6,14},{7,23},{8,0},{9,25... | collective-permute-start | bytes 491528 | tf_op jit(solution)/shard_map/ppermute | solution.py:320
  242.2 3.4 %collective-permute-start.45 = (f32[1,72,256]{2,1,0:T(8,128)S(1)}, f32[1,72,256]{2,1,0:T(8,128)S(1)}, u32[]{:S(2)}, u32[]{:S(2)}) collective-permute-start(f32[1,72,256]{2,1,0:T(8,128)S(1)} %fusion.24), channel_id=1, source_target_pairs={{0,16},{1,9},{2,18},{3,11},{4,20},{5,13},{6,22},{7,15},{8,24},{9,1... | collective-permute-start | bytes 221192 | tf_op jit(solution)/shard_map/ppermute | solution.py:320
  248.7 2.4 collective-permute-done.38
  251.2 6.0 %collective-permute-done.46 = f32[2,72,256]{2,1,0:T(8,128)S(1)} collective-permute-done((f32[2,72,256]{2,1,0:T(8,128)S(1)}, f32[2,72,256]{2,1,0:T(8,128)S(1)}, u32[]{:S(2)}, u32[]{:S(2)}) %collective-permute-start.46) | collective-permute-done | bytes 147488 | tf_op jit(solution)/shard_map/ppermute | solution.py:320
  257.8 1.6 collective-permute-start.32
  259.7 1.6 collective-permute-start.40
  261.3 5.9 %collective-permute-done.47 = f32[4,72,256]{2,1,0:T(8,128)S(1)} collective-permute-done((f32[4,72,256]{2,1,0:T(8,128)S(1)}, f32[4,72,256]{2,1,0:T(8,128)S(1)}, u32[]{:S(2)}, u32[]{:S(2)}) %collective-permute-start.47) | collective-permute-done | bytes 294944 | tf_op jit(solution)/shard_map/ppermute | solution.py:320
  267.3 12.3 %collective-permute-done.48.refs_5_ = f32[8,72,256]{2,1,0:T(8,128)S(1)} collective-permute-done((f32[8,72,256]{2,1,0:T(8,128)S(1)}, f32[8,72,256]{2,1,0:T(8,128)S(1)}, u32[]{:S(2)}, u32[]{:S(2)}) %collective-permute-start.48) | collective-permute-done | bytes 589856 | tf_op jit(solution)/shard_map/ppermute | solution.py:320
  279.6 21.4 %labels.3 = (f32[320,256]{1,0:T(8,128)S(1)}, f32[231,4096]{1,0:T(8,128)}) custom-call(s32[2]{0:T(128)S(1)} %pad_add_fusion.me_ref, bf16[320,4096]{1,0:T(8,128)(2,1)S(1)} %copy-done, bf16[320,4096]{1,0:T(8,128)(2,1)S(1)} %copy-done.1, bf16[320,256]{1,0:T(8,128)(2,1)S(1)} %get-tuple-element.33.feat_ref, bf16[320,32]{1,0:T(8,128)(2,1)S(1)} %get-tuple-element.34.lab1_ref, ...), custom_call_target="tpu_custom_call" | custom-call | flops 14763950080 | bytes 13668352 | tf_op jit(solution)/shard_map/labels/pallas_call | solution.py:349
  301.1 1.6 collective-permute-done.49.there_ref
  (125 shorter events, 42.0 us)
Async XLA Ops:
  11.3 29.5 %collective-permute-start.16 = (f32[8,144,256]{2,1,0:T(8,128)S(1)}, f32[8,144,256]{2,1,0:T(8,128)S(1)}, u32[]{:S(2)}, u32[]{:S(2)}) collective-permute-start(f32[8,144,256]{2,1,0:T(8,128)S(1)} %get-tuple-element.32), channel_id=1, source_target_pairs={{0,8},{1,17},{2,10},{3,19},{4,12},{5,21},{6,14},{7,23},{8,0},{9,25... | collective-permute-start | bytes 3538952 | tf_op jit(solution)/shard_map/ppermute | solution.py:320
  14.4 31.6 %collective-permute-start = (f32[8,160,256]{2,1,0:T(8,128)S(1)}, f32[8,160,256]{2,1,0:T(8,128)S(1)}, u32[]{:S(2)}, u32[]{:S(2)}) collective-permute-start(f32[8,160,256]{2,1,0:T(8,128)S(1)} %get-tuple-element.28), channel_id=1, source_target_pairs={{0,2},{1,3},{2,0},{3,1},{4,6},{5,7},{6,4},{7,5},{8,10},{9,11},{10,... | collective-permute-start | bytes 3932168 | tf_op jit(solution)/shard_map/ppermute | solution.py:320
  15.9 32.9 %collective-permute-start.8 = (f32[8,160,256]{2,1,0:T(8,128)}, f32[8,160,256]{2,1,0:T(8,128)S(1)}, u32[]{:S(2)}, u32[]{:S(2)}) collective-permute-start(f32[8,160,256]{2,1,0:T(8,128)} %get-tuple-element.30), channel_id=1, source_target_pairs={{0,4},{1,5},{2,6},{3,7},{4,0},{5,1},{6,2},{7,3},{8,12},{9,13},{10,... | collective-permute-start | bytes 3932168 | tf_op jit(solution)/shard_map/ppermute | solution.py:320
  41.8 16.6 %collective-permute-start.17 = (f32[4,144,256]{2,1,0:T(8,128)}, f32[4,144,256]{2,1,0:T(8,128)}, u32[]{:S(2)}, u32[]{:S(2)}) collective-permute-start(f32[4,144,256]{2,1,0:T(8,128)} %get-tuple-element.59), channel_id=1, source_target_pairs={{0,2},{1,3},{2,0},{3,1},{4,6},{5,7},{6,4},{7,5},{8,10},{9,11},{10,... | collective-permute-start | bytes 1769480 | tf_op jit(solution)/shard_map/ppermute | solution.py:320
  47.2 17.9 %collective-permute-start.1 = (f32[4,160,256]{2,1,0:T(8,128)}, f32[4,160,256]{2,1,0:T(8,128)}, u32[]{:S(2)}, u32[]{:S(2)}) collective-permute-start(f32[4,160,256]{2,1,0:T(8,128)} %get-tuple-element.55), channel_id=1, source_target_pairs={{0,4},{1,5},{2,6},{3,7},{4,0},{5,1},{6,2},{7,3},{8,12},{9,13},{10,... | collective-permute-start | bytes 1966088 | tf_op jit(solution)/shard_map/ppermute | solution.py:320
  49.7 17.2 %collective-permute-start.9 = (f32[4,160,256]{2,1,0:T(8,128)}, f32[4,160,256]{2,1,0:T(8,128)}, u32[]{:S(2)}, u32[]{:S(2)}) collective-permute-start(f32[4,160,256]{2,1,0:T(8,128)} %get-tuple-element.53), channel_id=1, source_target_pairs={{0,8},{1,17},{2,10},{3,19},{4,12},{5,21},{6,14},{7,23},{8,0},{9,25... | collective-permute-start | bytes 1966088 | tf_op jit(solution)/shard_map/ppermute | solution.py:320
  59.6 10.3 %collective-permute-start.18 = (f32[2,144,256]{2,1,0:T(8,128)S(1)}, f32[2,144,256]{2,1,0:T(8,128)S(1)}, u32[]{:S(2)}, u32[]{:S(2)}) collective-permute-start(f32[2,144,256]{2,1,0:T(8,128)S(1)} %get-tuple-element.71), channel_id=1, source_target_pairs={{0,4},{1,5},{2,6},{3,7},{4,0},{5,1},{6,2},{7,3},{8,12},{9,13},{10,... | collective-permute-start | bytes 884744 | tf_op jit(solution)/shard_map/ppermute | solution.py:320
  66.3 12.7 %collective-permute-start.2 = (f32[2,160,256]{2,1,0:T(8,128)S(1)}, f32[2,160,256]{2,1,0:T(8,128)S(1)}, u32[]{:S(2)}, u32[]{:S(2)}) collective-permute-start(f32[2,160,256]{2,1,0:T(8,128)S(1)} %get-tuple-element.67), channel_id=1, source_target_pairs={{0,8},{1,17},{2,10},{3,19},{4,12},{5,21},{6,14},{7,23},{8,0},{9,25... | collective-permute-start | bytes 983048 | tf_op jit(solution)/shard_map/ppermute | solution.py:320
  68.1 11.7 %collective-permute-start.10 = (f32[2,160,256]{2,1,0:T(8,128)S(1)}, f32[2,160,256]{2,1,0:T(8,128)S(1)}, u32[]{:S(2)}, u32[]{:S(2)}) collective-permute-start(f32[2,160,256]{2,1,0:T(8,128)S(1)} %get-tuple-element.65), channel_id=1, source_target_pairs={{0,2},{1,3},{2,0},{3,1},{4,6},{5,7},{6,4},{7,5},{8,10},{9,11},{10,... | collective-permute-start | bytes 983048 | tf_op jit(solution)/shard_map/ppermute | solution.py:320
  69.9 21.6 %collective-permute-start.19 = (f32[1,144,256]{2,1,0:T(8,128)S(1)}, f32[1,144,256]{2,1,0:T(8,128)S(1)}, u32[]{:S(2)}, u32[]{:S(2)}) collective-permute-start(f32[1,144,256]{2,1,0:T(8,128)S(1)} %slice_add_fusion.34), channel_id=1, source_target_pairs={{0,16},{1,9},{2,18},{3,11},{4,20},{5,13},{6,22},{7,15},{8,24},{9,1... | collective-permute-start | bytes 442376 | tf_op jit(solution)/shard_map/ppermute | solution.py:320
  79.1 8.5 %collective-permute-start.3 = (f32[1,160,256]{2,1,0:T(8,128)S(1)}, f32[1,160,256]{2,1,0:T(8,128)S(1)}, u32[]{:S(2)}, u32[]{:S(2)}) collective-permute-start(f32[1,160,256]{2,1,0:T(8,128)S(1)} %slice_add_fusion.30), channel_id=1, source_target_pairs={{0,16},{1,9},{2,18},{3,11},{4,20},{5,13},{6,22},{7,15},{8,24},{9,1... | collective-permute-start | bytes 491528 | tf_op jit(solution)/shard_map/ppermute | solution.py:320
  79.9 10.5 %collective-permute-start.11 = (f32[1,160,256]{2,1,0:T(8,128)S(1)}, f32[1,160,256]{2,1,0:T(8,128)S(1)}, u32[]{:S(2)}, u32[]{:S(2)}) collective-permute-start(f32[1,160,256]{2,1,0:T(8,128)S(1)} %slice_add_fusion.28), channel_id=1, source_target_pairs={{0,16},{1,9},{2,18},{3,11},{4,20},{5,13},{6,22},{7,15},{8,24},{9,1... | collective-permute-start | bytes 491528 | tf_op jit(solution)/shard_map/ppermute | solution.py:320
  91.4 10.9 %collective-permute-start.12 = (f32[1,80,256]{2,1,0:T(8,128)S(1)}, f32[1,80,256]{2,1,0:T(8,128)S(1)}, u32[]{:S(2)}, u32[]{:S(2)}) collective-permute-start(f32[1,80,256]{2,1,0:T(8,128)S(1)} %bitcast.44), channel_id=1, source_target_pairs={{0,16},{1,9},{2,18},{3,11},{4,20},{5,13},{6,22},{7,15},{8,24},{9,1... | collective-permute-start | bytes 245768 | tf_op jit(solution)/shard_map/ppermute | solution.py:320
  91.5 12.6 %collective-permute-start.4 = (f32[1,80,256]{2,1,0:T(8,128)S(1)}, f32[1,80,256]{2,1,0:T(8,128)S(1)}, u32[]{:S(2)}, u32[]{:S(2)}) collective-permute-start(f32[1,80,256]{2,1,0:T(8,128)S(1)} %bitcast.48), channel_id=1, source_target_pairs={{0,16},{1,9},{2,18},{3,11},{4,20},{5,13},{6,22},{7,15},{8,24},{9,1... | collective-permute-start | bytes 245768 | tf_op jit(solution)/shard_map/ppermute | solution.py:320
  102.4 5.4 %collective-permute-start.13 = (f32[2,80,256]{2,1,0:T(8,128)S(1)}, f32[2,80,256]{2,1,0:T(8,128)S(1)}, u32[]{:S(2)}, u32[]{:S(2)}) collective-permute-start(f32[2,80,256]{2,1,0:T(8,128)S(1)} %pad_maximum_fusion.13), channel_id=1, source_target_pairs={{0,2},{1,3},{2,0},{3,1},{4,6},{5,7},{6,4},{7,5},{8,10},{9,11},{10,... | collective-permute-start | bytes 491528 | tf_op jit(solution)/shard_map/ppermute | solution.py:320
  103.3 5.6 %collective-permute-start.20 = (f32[1,72,256]{2,1,0:T(8,128)S(1)}, f32[1,72,256]{2,1,0:T(8,128)S(1)}, u32[]{:S(2)}, u32[]{:S(2)}) collective-permute-start(f32[1,72,256]{2,1,0:T(8,128)S(1)} %bitcast.52), channel_id=1, source_target_pairs={{0,16},{1,9},{2,18},{3,11},{4,20},{5,13},{6,22},{7,15},{8,24},{9,1... | collective-permute-start | bytes 221192 | tf_op jit(solution)/shard_map/ppermute | solution.py:320
  104.1 7.9 %collective-permute-start.5 = (f32[2,80,256]{2,1,0:T(8,128)S(1)}, f32[2,80,256]{2,1,0:T(8,128)S(1)}, u32[]{:S(2)}, u32[]{:S(2)}) collective-permute-start(f32[2,80,256]{2,1,0:T(8,128)S(1)} %pad_maximum_fusion.12), channel_id=1, source_target_pairs={{0,8},{1,17},{2,10},{3,19},{4,12},{5,21},{6,14},{7,23},{8,0},{9,25... | collective-permute-start | bytes 491528 | tf_op jit(solution)/shard_map/ppermute | solution.py:320
  107.8 9.8 %collective-permute-start.14 = (f32[4,80,256]{2,1,0:T(8,128)S(1)}, f32[4,80,256]{2,1,0:T(8,128)S(1)}, u32[]{:S(2)}, u32[]{:S(2)}) collective-permute-start(f32[4,80,256]{2,1,0:T(8,128)S(1)} %pad_maximum_fusion.7), channel_id=1, source_target_pairs={{0,8},{1,17},{2,10},{3,19},{4,12},{5,21},{6,14},{7,23},{8,0},{9,25... | collective-permute-start | bytes 983048 | tf_op jit(solution)/shard_map/ppermute | solution.py:320
  108.9 7.9 %collective-permute-start.21 = (f32[2,72,256]{2,1,0:T(8,128)S(1)}, f32[2,72,256]{2,1,0:T(8,128)S(1)}, u32[]{:S(2)}, u32[]{:S(2)}) collective-permute-start(f32[2,72,256]{2,1,0:T(8,128)S(1)} %pad_maximum_fusion.16), channel_id=1, source_target_pairs={{0,4},{1,5},{2,6},{3,7},{4,0},{5,1},{6,2},{7,3},{8,12},{9,13},{10,... | collective-permute-start | bytes 442376 | tf_op jit(solution)/shard_map/ppermute | solution.py:320
  112.1 11.1 %collective-permute-start.6 = (f32[4,80,256]{2,1,0:T(8,128)S(1)}, f32[4,80,256]{2,1,0:T(8,128)S(1)}, u32[]{:S(2)}, u32[]{:S(2)}) collective-permute-start(f32[4,80,256]{2,1,0:T(8,128)S(1)} %pad_maximum_fusion.6), channel_id=1, source_target_pairs={{0,4},{1,5},{2,6},{3,7},{4,0},{5,1},{6,2},{7,3},{8,12},{9,13},{10,... | collective-permute-start | bytes 983048 | tf_op jit(solution)/shard_map/ppermute | solution.py:320
  116.9 7.5 %collective-permute-start.22 = (f32[4,72,256]{2,1,0:T(8,128)S(1)}, f32[4,72,256]{2,1,0:T(8,128)S(1)}, u32[]{:S(2)}, u32[]{:S(2)}) collective-permute-start(f32[4,72,256]{2,1,0:T(8,128)S(1)} %pad_maximum_fusion.10), channel_id=1, source_target_pairs={{0,2},{1,3},{2,0},{3,1},{4,6},{5,7},{6,4},{7,5},{8,10},{9,11},{10,... | collective-permute-start | bytes 884744 | tf_op jit(solution)/shard_map/ppermute | solution.py:320
  117.7 16.7 %collective-permute-start.15 = (f32[8,80,256]{2,1,0:T(8,128)S(1)}, f32[8,80,256]{2,1,0:T(8,128)S(1)}, u32[]{:S(2)}, u32[]{:S(2)}) collective-permute-start(f32[8,80,256]{2,1,0:T(8,128)S(1)} %pad_maximum_fusion.1.refs_2_), channel_id=1, source_target_pairs={{0,4},{1,5},{2,6},{3,7},{4,0},{5,1},{6,2},{7,3},{8,12},{9,13},{10,... | collective-permute-start | bytes 1966088 | tf_op jit(solution)/shard_map/ppermute | solution.py:320
  123.3 11.1 %collective-permute-start.7 = (f32[8,80,256]{2,1,0:T(8,128)S(1)}, f32[8,80,256]{2,1,0:T(8,128)S(1)}, u32[]{:S(2)}, u32[]{:S(2)}) collective-permute-start(f32[8,80,256]{2,1,0:T(8,128)S(1)} %pad_maximum_fusion.refs_0_), channel_id=1, source_target_pairs={{0,2},{1,3},{2,0},{3,1},{4,6},{5,7},{6,4},{7,5},{8,10},{9,11},{10,... | collective-permute-start | bytes 1966088 | tf_op jit(solution)/shard_map/ppermute | solution.py:320
  124.4 9.9 %collective-permute-start.23 = (f32[8,72,256]{2,1,0:T(8,128)S(1)}, f32[8,72,256]{2,1,0:T(8,128)S(1)}, u32[]{:S(2)}, u32[]{:S(2)}) collective-permute-start(f32[8,72,256]{2,1,0:T(8,128)S(1)} %pad_maximum_fusion.4.refs_4_), channel_id=1, source_target_pairs={{0,8},{1,17},{2,10},{3,19},{4,12},{5,21},{6,14},{7,23},{8,0},{9,25... | collective-permute-start | bytes 1769480 | tf_op jit(solution)/shard_map/ppermute | solution.py:320
  162.2 28.9 %collective-permute-start.41 = (f32[8,144,256]{2,1,0:T(8,128)S(1)}, f32[8,144,256]{2,1,0:T(8,128)S(1)}, u32[]{:S(2)}, u32[]{:S(2)}) collective-permute-start(f32[8,144,256]{2,1,0:T(8,128)S(1)} %get-tuple-element.42), channel_id=1, source_target_pairs={{0,8},{1,17},{2,10},{3,19},{4,12},{5,21},{6,14},{7,23},{8,0},{9,25... | collective-permute-start | bytes 3538952 | tf_op jit(solution)/shard_map/ppermute | solution.py:320
  163.6 31.1 %collective-permute-start.25 = (f32[8,160,256]{2,1,0:T(8,128)S(1)}, f32[8,160,256]{2,1,0:T(8,128)S(1)}, u32[]{:S(2)}, u32[]{:S(2)}) collective-permute-start(f32[8,160,256]{2,1,0:T(8,128)S(1)} %get-tuple-element.38), channel_id=1, source_target_pairs={{0,2},{1,3},{2,0},{3,1},{4,6},{5,7},{6,4},{7,5},{8,10},{9,11},{10,... | collective-permute-start | bytes 3932168 | tf_op jit(solution)/shard_map/ppermute | solution.py:320
  164.3 33.2 %collective-permute-start.33 = (f32[8,160,256]{2,1,0:T(8,128)S(1)}, f32[8,160,256]{2,1,0:T(8,128)S(1)}, u32[]{:S(2)}, u32[]{:S(2)}) collective-permute-start(f32[8,160,256]{2,1,0:T(8,128)S(1)} %get-tuple-element.40), channel_id=1, source_target_pairs={{0,4},{1,5},{2,6},{3,7},{4,0},{5,1},{6,2},{7,3},{8,12},{9,13},{10,... | collective-permute-start | bytes 3932168 | tf_op jit(solution)/shard_map/ppermute | solution.py:320
  191.3 15.3 %collective-permute-start.42 = (f32[4,144,256]{2,1,0:T(8,128)S(1)}, f32[4,144,256]{2,1,0:T(8,128)S(1)}, u32[]{:S(2)}, u32[]{:S(2)}) collective-permute-start(f32[4,144,256]{2,1,0:T(8,128)S(1)} %get-tuple-element.57), channel_id=1, source_target_pairs={{0,2},{1,3},{2,0},{3,1},{4,6},{5,7},{6,4},{7,5},{8,10},{9,11},{10,... | collective-permute-start | bytes 1769480 | tf_op jit(solution)/shard_map/ppermute | solution.py:320
  194.9 15.9 %collective-permute-start.26 = (f32[4,160,256]{2,1,0:T(8,128)S(1)}, f32[4,160,256]{2,1,0:T(8,128)S(1)}, u32[]{:S(2)}, u32[]{:S(2)}) collective-permute-start(f32[4,160,256]{2,1,0:T(8,128)S(1)} %get-tuple-element.51), channel_id=1, source_target_pairs={{0,4},{1,5},{2,6},{3,7},{4,0},{5,1},{6,2},{7,3},{8,12},{9,13},{10,... | collective-permute-start | bytes 1966088 | tf_op jit(solution)/shard_map/ppermute | solution.py:320
  197.7 20.6 %collective-permute-start.34 = (f32[4,160,256]{2,1,0:T(8,128)S(1)}, f32[4,160,256]{2,1,0:T(8,128)S(1)}, u32[]{:S(2)}, u32[]{:S(2)}) collective-permute-start(f32[4,160,256]{2,1,0:T(8,128)S(1)} %get-tuple-element.49), channel_id=1, source_target_pairs={{0,8},{1,17},{2,10},{3,19},{4,12},{5,21},{6,14},{7,23},{8,0},{9,25... | collective-permute-start | bytes 1966088 | tf_op jit(solution)/shard_map/ppermute | solution.py:320
  206.6 9.3 %collective-permute-start.43 = (f32[2,144,256]{2,1,0:T(8,128)S(1)}, f32[2,144,256]{2,1,0:T(8,128)S(1)}, u32[]{:S(2)}, u32[]{:S(2)}) collective-permute-start(f32[2,144,256]{2,1,0:T(8,128)S(1)} %get-tuple-element.69), channel_id=1, source_target_pairs={{0,4},{1,5},{2,6},{3,7},{4,0},{5,1},{6,2},{7,3},{8,12},{9,13},{10,... | collective-permute-start | bytes 884744 | tf_op jit(solution)/shard_map/ppermute | solution.py:320
  211.0 11.5 %collective-permute-start.27 = (f32[2,160,256]{2,1,0:T(8,128)S(1)}, f32[2,160,256]{2,1,0:T(8,128)S(1)}, u32[]{:S(2)}, u32[]{:S(2)}) collective-permute-start(f32[2,160,256]{2,1,0:T(8,128)S(1)} %get-tuple-element.63), channel_id=1, source_target_pairs={{0,8},{1,17},{2,10},{3,19},{4,12},{5,21},{6,14},{7,23},{8,0},{9,25... | collective-permute-start | bytes 983048 | tf_op jit(solution)/shard_map/ppermute | solution.py:320
  216.0 6.4 %collective-permute-start.44 = (f32[1,144,256]{2,1,0:T(8,128)S(1)}, f32[1,144,256]{2,1,0:T(8,128)S(1)}, u32[]{:S(2)}, u32[]{:S(2)}) collective-permute-start(f32[1,144,256]{2,1,0:T(8,128)S(1)} %slice_add_fusion.32), channel_id=1, source_target_pairs={{0,16},{1,9},{2,18},{3,11},{4,20},{5,13},{6,22},{7,15},{8,24},{9,1... | collective-permute-start | bytes 442376 | tf_op jit(solution)/shard_map/ppermute | solution.py:320
  218.4 9.6 %collective-permute-start.35 = (f32[2,160,256]{2,1,0:T(8,128)S(1)}, f32[2,160,256]{2,1,0:T(8,128)S(1)}, u32[]{:S(2)}, u32[]{:S(2)}) collective-permute-start(f32[2,160,256]{2,1,0:T(8,128)S(1)} %get-tuple-element.61), channel_id=1, source_target_pairs={{0,2},{1,3},{2,0},{3,1},{4,6},{5,7},{6,4},{7,5},{8,10},{9,11},{10,... | collective-permute-start | bytes 983048 | tf_op jit(solution)/shard_map/ppermute | solution.py:320
  222.5 7.9 %collective-permute-start.28 = (f32[1,160,256]{2,1,0:T(8,128)S(1)}, f32[1,160,256]{2,1,0:T(8,128)S(1)}, u32[]{:S(2)}, u32[]{:S(2)}) collective-permute-start(f32[1,160,256]{2,1,0:T(8,128)S(1)} %slice_add_fusion.26), channel_id=1, source_target_pairs={{0,16},{1,9},{2,18},{3,11},{4,20},{5,13},{6,22},{7,15},{8,24},{9,1... | collective-permute-start | bytes 491528 | tf_op jit(solution)/shard_map/ppermute | solution.py:320
  228.1 7.9 %collective-permute-start.36 = (f32[1,160,256]{2,1,0:T(8,128)S(1)}, f32[1,160,256]{2,1,0:T(8,128)S(1)}, u32[]{:S(2)}, u32[]{:S(2)}) collective-permute-start(f32[1,160,256]{2,1,0:T(8,128)S(1)} %slice_add_fusion.24), channel_id=1, source_target_pairs={{0,16},{1,9},{2,18},{3,11},{4,20},{5,13},{6,22},{7,15},{8,24},{9,1... | collective-permute-start | bytes 491528 | tf_op jit(solution)/shard_map/ppermute | solution.py:320
  230.5 6.5 %collective-permute-start.29 = (f32[1,80,256]{2,1,0:T(8,128)S(1)}, f32[1,80,256]{2,1,0:T(8,128)S(1)}, u32[]{:S(2)}, u32[]{:S(2)}) collective-permute-start(f32[1,80,256]{2,1,0:T(8,128)S(1)} %fusion.13), channel_id=1, source_target_pairs={{0,16},{1,9},{2,18},{3,11},{4,20},{5,13},{6,22},{7,15},{8,24},{9,1... | collective-permute-start | bytes 245768 | tf_op jit(solution)/shard_map/ppermute | solution.py:320
  236.1 9.6 %collective-permute-start.37 = (f32[1,80,256]{2,1,0:T(8,128)S(1)}, f32[1,80,256]{2,1,0:T(8,128)S(1)}, u32[]{:S(2)}, u32[]{:S(2)}) collective-permute-start(f32[1,80,256]{2,1,0:T(8,128)S(1)} %fusion.9), channel_id=1, source_target_pairs={{0,16},{1,9},{2,18},{3,11},{4,20},{5,13},{6,22},{7,15},{8,24},{9,1... | collective-permute-start | bytes 245768 | tf_op jit(solution)/shard_map/ppermute | solution.py:320
  237.1 9.4 %collective-permute-start.30 = (f32[2,80,256]{2,1,0:T(8,128)S(1)}, f32[2,80,256]{2,1,0:T(8,128)S(1)}, u32[]{:S(2)}, u32[]{:S(2)}) collective-permute-start(f32[2,80,256]{2,1,0:T(8,128)S(1)} %pad_maximum_fusion.14), channel_id=1, source_target_pairs={{0,8},{1,17},{2,10},{3,19},{4,12},{5,21},{6,14},{7,23},{8,0},{9,25... | collective-permute-start | bytes 491528 | tf_op jit(solution)/shard_map/ppermute | solution.py:320
  242.2 6.1 %collective-permute-start.45 = (f32[1,72,256]{2,1,0:T(8,128)S(1)}, f32[1,72,256]{2,1,0:T(8,128)S(1)}, u32[]{:S(2)}, u32[]{:S(2)}) collective-permute-start(f32[1,72,256]{2,1,0:T(8,128)S(1)} %fusion.24), channel_id=1, source_target_pairs={{0,16},{1,9},{2,18},{3,11},{4,20},{5,13},{6,22},{7,15},{8,24},{9,1... | collective-permute-start | bytes 221192 | tf_op jit(solution)/shard_map/ppermute | solution.py:320
  245.7 5.4 %collective-permute-start.38 = (f32[2,80,256]{2,1,0:T(8,128)S(1)}, f32[2,80,256]{2,1,0:T(8,128)S(1)}, u32[]{:S(2)}, u32[]{:S(2)}) collective-permute-start(f32[2,80,256]{2,1,0:T(8,128)S(1)} %pad_maximum_fusion.15), channel_id=1, source_target_pairs={{0,2},{1,3},{2,0},{3,1},{4,6},{5,7},{6,4},{7,5},{8,10},{9,11},{10,... | collective-permute-start | bytes 491528 | tf_op jit(solution)/shard_map/ppermute | solution.py:320
  246.5 11.3 %collective-permute-start.31 = (f32[4,80,256]{2,1,0:T(8,128)S(1)}, f32[4,80,256]{2,1,0:T(8,128)S(1)}, u32[]{:S(2)}, u32[]{:S(2)}) collective-permute-start(f32[4,80,256]{2,1,0:T(8,128)S(1)} %pad_maximum_fusion.8), channel_id=1, source_target_pairs={{0,4},{1,5},{2,6},{3,7},{4,0},{5,1},{6,2},{7,3},{8,12},{9,13},{10,... | collective-permute-start | bytes 983048 | tf_op jit(solution)/shard_map/ppermute | solution.py:320
  248.4 8.8 %collective-permute-start.46 = (f32[2,72,256]{2,1,0:T(8,128)S(1)}, f32[2,72,256]{2,1,0:T(8,128)S(1)}, u32[]{:S(2)}, u32[]{:S(2)}) collective-permute-start(f32[2,72,256]{2,1,0:T(8,128)S(1)} %pad_maximum_fusion.17), channel_id=1, source_target_pairs={{0,4},{1,5},{2,6},{3,7},{4,0},{5,1},{6,2},{7,3},{8,12},{9,13},{10,... | collective-permute-start | bytes 442376 | tf_op jit(solution)/shard_map/ppermute | solution.py:320
  251.1 8.5 %collective-permute-start.39 = (f32[4,80,256]{2,1,0:T(8,128)S(1)}, f32[4,80,256]{2,1,0:T(8,128)S(1)}, u32[]{:S(2)}, u32[]{:S(2)}) collective-permute-start(f32[4,80,256]{2,1,0:T(8,128)S(1)} %pad_maximum_fusion.9), channel_id=1, source_target_pairs={{0,8},{1,17},{2,10},{3,19},{4,12},{5,21},{6,14},{7,23},{8,0},{9,25... | collective-permute-start | bytes 983048 | tf_op jit(solution)/shard_map/ppermute | solution.py:320
  257.2 10.0 %collective-permute-start.47 = (f32[4,72,256]{2,1,0:T(8,128)S(1)}, f32[4,72,256]{2,1,0:T(8,128)S(1)}, u32[]{:S(2)}, u32[]{:S(2)}) collective-permute-start(f32[4,72,256]{2,1,0:T(8,128)S(1)} %pad_maximum_fusion.11), channel_id=1, source_target_pairs={{0,2},{1,3},{2,0},{3,1},{4,6},{5,7},{6,4},{7,5},{8,10},{9,11},{10,... | collective-permute-start | bytes 884744 | tf_op jit(solution)/shard_map/ppermute | solution.py:320
  257.8 21.8 %collective-permute-start.32 = (f32[8,80,256]{2,1,0:T(8,128)S(1)}, f32[8,80,256]{2,1,0:T(8,128)S(1)}, u32[]{:S(2)}, u32[]{:S(2)}) collective-permute-start(f32[8,80,256]{2,1,0:T(8,128)S(1)} %pad_maximum_fusion.2.refs_0_), channel_id=1, source_target_pairs={{0,2},{1,3},{2,0},{3,1},{4,6},{5,7},{6,4},{7,5},{8,10},{9,11},{10,... | collective-permute-start | bytes 1966088 | tf_op jit(solution)/shard_map/ppermute | solution.py:320
  259.7 19.9 %collective-permute-start.40 = (f32[8,80,256]{2,1,0:T(8,128)S(1)}, f32[8,80,256]{2,1,0:T(8,128)S(1)}, u32[]{:S(2)}, u32[]{:S(2)}) collective-permute-start(f32[8,80,256]{2,1,0:T(8,128)S(1)} %pad_maximum_fusion.3.refs_2_), channel_id=1, source_target_pairs={{0,4},{1,5},{2,6},{3,7},{4,0},{5,1},{6,2},{7,3},{8,12},{9,13},{10,... | collective-permute-start | bytes 1966088 | tf_op jit(solution)/shard_map/ppermute | solution.py:320
  267.3 12.4 %collective-permute-start.48 = (f32[8,72,256]{2,1,0:T(8,128)S(1)}, f32[8,72,256]{2,1,0:T(8,128)S(1)}, u32[]{:S(2)}, u32[]{:S(2)}) collective-permute-start(f32[8,72,256]{2,1,0:T(8,128)S(1)} %pad_maximum_fusion.5.refs_4_), channel_id=1, source_target_pairs={{0,8},{1,17},{2,10},{3,19},{4,12},{5,21},{6,14},{7,23},{8,0},{9,25... | collective-permute-start | bytes 1769480 | tf_op jit(solution)/shard_map/ppermute | solution.py:320
  (11 other events, 126.7 us)

commit v5 on v4

--- a/solution.py
+++ b/solution.py
@@ -487,7 +487,7 @@
     third = round_up(height // 3, 16)
     cuts = [0, third, 2 * third, height]
     rest = list(range(3, bits))
-    orders = [[0, 1, 2] + rest, [1, 2, 0] + rest, [2, 0, 1] + rest]
+    orders = [[1, 2, 0] + rest, [2, 0, 1] + rest, [0, 1, 2] + rest]
     parts = [
         {"start": cuts[i], "rows": cuts[i + 1] - cuts[i], "order": orders[i]} for i in range(3)
     ]

time: 304 us -> 302 us (level)
  starting transfers between devices: 73.3 us -> 58.9 us
  waiting for transfers between devices: 160 us -> 172 us
    ppermute x48, starting transfers between devices: 73.2 us -> 58.8 us  [exchange(): return lax.ppermute(value, ('star', 'pix'), pairs)]
    ppermute x48, waiting for transfers between devices: 156 us -> 169 us  [exchange(): return lax.ppermute(value, ('star', 'pix'), pairs)]
  transfers between devices with their start and end apart: 50 -> 50, of which waited for: 33 -> 32; matrix products, arithmetic and copies ran while one was open for 3% -> 4% of each run, Pallas kernels for 0% -> 0%
where the time goes in v5:
time: 302 us; the launch traced here: 301 us
  waiting for transfers between devices  172 us (57%)
  starting transfers between devices  58.9 us (20%)
  Pallas kernels  56.6 us (19%)
  other arithmetic  9.61 us (3%)
  local copies, waits for them, and re-layouts  3.26 us (1%)
    ppermute x48, waiting for transfers between devices, exchange(): return lax.ppermute(value, ('star', 'pix'), pairs)  169 us
    ppermute x48, starting transfers between devices, exchange(): return lax.ppermute(value, ('star', 'pix'), pairs)  58.8 us
    pallas_call x4, Pallas kernels, call(): pl.pallas_call(kernel, out_shape=shapes, in_specs=[scalar] + (specs or [w...  55.3 us
    add x12, other arithmetic, reduced(): kept = kept[:size] + arrived[:size]  7.65 us
  transfers between devices with their start and end apart: 50, of which 32 were waited for; matrix products, arithmetic and copies ran while one was open for 4% of the time, Pallas kernels for 0%

profile of v5, /device:TPU:0, one launch (start us, length us, event | category | flops | bytes accessed | tf_op | source)
XLA Modules:
  0.0 301.5 jit_solution(9942704845304523022)
XLA Ops:
  2.9 8.4 %first.1 = (f32[320,32]{1,0:T(8,128)S(1)}, bf16[320,256]{1,0:T(8,128)(2,1)S(1)}, bf16[256,320]{1,0:T(8,128)(2,1)}, bf16[256,320]{1,0:T(8,128)(2,1)}, bf16[320,32...) custom-call(s32[2]{0:T(128)S(1)} %pad_add_fusion.me_ref, ...), custom_call_target="tpu_custom_call" | custom-call | flops 1824522240 | bytes 17241088 | tf_op jit(solution)/shard_map/first/pallas_call | solution.py:349
  11.3 3.0 collective-permute-start.16
  17.4 22.9 %collective-permute-done.16 = f32[8,144,256]{2,1,0:T(8,128)S(1)} collective-permute-done((f32[8,144,256]{2,1,0:T(8,128)S(1)}, f32[8,144,256]{2,1,0:T(8,128)S(1)}, u32[]{:S(2)}, u32[]{:S(2)}) %collective-permute-start.16) | collective-permute-done | bytes 1179680 | tf_op jit(solution)/shard_map/ppermute | solution.py:320
  41.2 1.8 collective-permute-start.17
  43.0 2.7 collective-permute-done
  46.9 1.6 collective-permute-start.1
  50.6 6.7 %collective-permute-done.17 = f32[4,144,256]{2,1,0:T(8,128)} collective-permute-done((f32[4,144,256]{2,1,0:T(8,128)}, f32[4,144,256]{2,1,0:T(8,128)}, u32[]{:S(2)}, u32[]{:S(2)}) %collective-permute-start.17) | collective-permute-done | bytes 589856 | tf_op jit(solution)/shard_map/ppermute | solution.py:320
  58.4 1.6 collective-permute-start.18
  60.1 4.8 %collective-permute-done.1 = f32[4,160,256]{2,1,0:T(8,128)} collective-permute-done((f32[4,160,256]{2,1,0:T(8,128)}, f32[4,160,256]{2,1,0:T(8,128)}, u32[]{:S(2)}, u32[]{:S(2)}) %collective-permute-start.1) | collective-permute-done | bytes 655392 | tf_op jit(solution)/shard_map/ppermute | solution.py:320
  67.4 1.7 collective-permute-start.10
  70.0 2.8 collective-permute-start.19
  73.3 2.8 collective-permute-start.3
  77.3 3.6 %collective-permute-done.3 = f32[1,160,256]{2,1,0:T(8,128)S(1)} collective-permute-done((f32[1,160,256]{2,1,0:T(8,128)S(1)}, f32[1,160,256]{2,1,0:T(8,128)S(1)}, u32[]{:S(2)}, u32[]{:S(2)}) %collective-permute-start.3) | collective-permute-done | bytes 163872 | tf_op jit(solution)/shard_map/ppermute | solution.py:320
  81.0 4.7 %collective-permute-done.11 = f32[1,160,256]{2,1,0:T(8,128)S(1)} collective-permute-done((f32[1,160,256]{2,1,0:T(8,128)S(1)}, f32[1,160,256]{2,1,0:T(8,128)S(1)}, u32[]{:S(2)}, u32[]{:S(2)}) %collective-permute-start.11) | collective-permute-done | bytes 163872 | tf_op jit(solution)/shard_map/ppermute | solution.py:320
  86.9 3.0 collective-permute-start.4
  89.8 2.7 collective-permute-done.12
  92.5 2.2 collective-permute-start.13
  95.2 2.8 collective-permute-done.13
  98.0 1.7 collective-permute-start.14
  99.7 4.4 %collective-permute-done.20 = f32[1,72,256]{2,1,0:T(8,128)S(1)} collective-permute-done((f32[1,72,256]{2,1,0:T(8,128)S(1)}, f32[1,72,256]{2,1,0:T(8,128)S(1)}, u32[]{:S(2)}, u32[]{:S(2)}) %collective-permute-start.20) | collective-permute-done | bytes 73760 | tf_op jit(solution)/shard_map/ppermute | solution.py:320
  104.2 2.1 collective-permute-start.6
  106.3 3.8 %collective-permute-done.21 = f32[2,72,256]{2,1,0:T(8,128)S(1)} collective-permute-done((f32[2,72,256]{2,1,0:T(8,128)S(1)}, f32[2,72,256]{2,1,0:T(8,128)S(1)}, u32[]{:S(2)}, u32[]{:S(2)}) %collective-permute-start.21) | collective-permute-done | bytes 147488 | tf_op jit(solution)/shard_map/ppermute | solution.py:320
  111.9 5.2 %collective-permute-done.6 = f32[4,80,256]{2,1,0:T(8,128)S(1)} collective-permute-done((f32[4,80,256]{2,1,0:T(8,128)S(1)}, f32[4,80,256]{2,1,0:T(8,128)S(1)}, u32[]{:S(2)}, u32[]{:S(2)}) %collective-permute-start.6) | collective-permute-done | bytes 327712 | tf_op jit(solution)/shard_map/ppermute | solution.py:320
  118.2 1.9 collective-permute-done.22
  121.1 9.0 %collective-permute-done.23.refs_5_ = f32[8,72,256]{2,1,0:T(8,128)S(1)} collective-permute-done((f32[8,72,256]{2,1,0:T(8,128)S(1)}, f32[8,72,256]{2,1,0:T(8,128)S(1)}, u32[]{:S(2)}, u32[]{:S(2)}) %collective-permute-start.23) | collective-permute-done | bytes 589856 | tf_op jit(solution)/shard_map/ppermute | solution.py:320
  130.2 21.1 %labels.2.here_ref = f32[320,256]{1,0:T(8,128)S(1)} custom-call(s32[2]{0:T(128)S(1)} %pad_add_fusion.me_ref, bf16[320,4096]{1,0:T(8,128)(2,1)S(1)} %copy-done, bf16[320,4096]{1,0:T(8,128)(2,1)S(1)} %copy-done.1, bf16[320,256]{1,0:T(8,128)(2,1)S(1)} %get-tuple-element.25.feat_ref, bf16[320,32]{1,0:T(8,128)(2,1)S(1)} %get-tuple-element.26.lab1_ref, ...), custom_call_target="tpu_custom_call" | custom-call | flops 14763950080 | bytes 9883648 | tf_op jit(solution)/shard_map/labels/pallas_call | solution.py:349
  153.5 4.5 %gradient.1 = (f32[8,160,256]{2,1,0:T(8,128)S(1)}, f32[8,160,256]{2,1,0:T(8,128)S(1)}, f32[8,160,256]{2,1,0:T(8,128)S(1)}, f32[8,160,256]{2,1,0:T(8,128)S(1)}, f...) custom-call(s32[2]{0:T(128)S(1)} %pad_add_fusion.me_ref, bf16[320,4096]{1,0:T(8,128)(2,1)S(1)} %copy-done, ...), custom_call_target="tpu_custom_call" | custom-call | flops 1824522240 | bytes 17137664 | tf_op jit(solution)/shard_map/gradient/pallas_call | solution.py:349
  161.0 25.0 %collective-permute-done.41 = f32[8,144,256]{2,1,0:T(8,128)S(1)} collective-permute-done((f32[8,144,256]{2,1,0:T(8,128)S(1)}, f32[8,144,256]{2,1,0:T(8,128)S(1)}, u32[]{:S(2)}, u32[]{:S(2)}) %collective-permute-start.41) | collective-permute-done | bytes 1179680 | tf_op jit(solution)/shard_map/ppermute | solution.py:320
  187.3 3.3 %collective-permute-done.25 = f32[8,160,256]{2,1,0:T(8,128)S(1)} collective-permute-done((f32[8,160,256]{2,1,0:T(8,128)S(1)}, f32[8,160,256]{2,1,0:T(8,128)S(1)}, u32[]{:S(2)}, u32[]{:S(2)}) %collective-permute-start.25) | collective-permute-done | bytes 1310752 | tf_op jit(solution)/shard_map/ppermute | solution.py:320
  192.8 9.3 %collective-permute-done.42 = f32[4,144,256]{2,1,0:T(8,128)S(1)} collective-permute-done((f32[4,144,256]{2,1,0:T(8,128)S(1)}, f32[4,144,256]{2,1,0:T(8,128)S(1)}, u32[]{:S(2)}, u32[]{:S(2)}) %collective-permute-start.42) | collective-permute-done | bytes 589856 | tf_op jit(solution)/shard_map/ppermute | solution.py:320
  203.0 5.5 %collective-permute-done.26 = f32[4,160,256]{2,1,0:T(8,128)S(1)} collective-permute-done((f32[4,160,256]{2,1,0:T(8,128)S(1)}, f32[4,160,256]{2,1,0:T(8,128)S(1)}, u32[]{:S(2)}, u32[]{:S(2)}) %collective-permute-start.26) | collective-permute-done | bytes 655392 | tf_op jit(solution)/shard_map/ppermute | solution.py:320
  208.6 1.8 collective-permute-start.27
  210.4 4.0 %collective-permute-done.43 = f32[2,144,256]{2,1,0:T(8,128)S(1)} collective-permute-done((f32[2,144,256]{2,1,0:T(8,128)S(1)}, f32[2,144,256]{2,1,0:T(8,128)S(1)}, u32[]{:S(2)}, u32[]{:S(2)}) %collective-permute-start.43) | collective-permute-done | bytes 294944 | tf_op jit(solution)/shard_map/ppermute | solution.py:320
  214.6 1.7 collective-permute-start.35
  216.3 4.9 %collective-permute-done.44 = f32[1,144,256]{2,1,0:T(8,128)S(1)} collective-permute-done((f32[1,144,256]{2,1,0:T(8,128)S(1)}, f32[1,144,256]{2,1,0:T(8,128)S(1)}, u32[]{:S(2)}, u32[]{:S(2)}) %collective-permute-start.44) | collective-permute-done | bytes 147488 | tf_op jit(solution)/shard_map/ppermute | solution.py:320
  222.5 2.3 collective-permute-start.36
  224.7 5.8 %collective-permute-done.28 = f32[1,160,256]{2,1,0:T(8,128)S(1)} collective-permute-done((f32[1,160,256]{2,1,0:T(8,128)S(1)}, f32[1,160,256]{2,1,0:T(8,128)S(1)}, u32[]{:S(2)}, u32[]{:S(2)}) %collective-permute-start.28) | collective-permute-done | bytes 163872 | tf_op jit(solution)/shard_map/ppermute | solution.py:320
  233.8 8.9 %collective-permute-done.29 = f32[1,80,256]{2,1,0:T(8,128)S(1)} collective-permute-done((f32[1,80,256]{2,1,0:T(8,128)S(1)}, f32[1,80,256]{2,1,0:T(8,128)S(1)}, u32[]{:S(2)}, u32[]{:S(2)}) %collective-permute-start.29) | collective-permute-done | bytes 81952 | tf_op jit(solution)/shard_map/ppermute | solution.py:320
  242.7 2.2 collective-permute-start.30
  246.4 1.9 collective-permute-done.30
  248.4 1.9 collective-permute-done.45
  250.5 2.1 collective-permute-start.39
  252.6 8.3 %collective-permute-done.46 = f32[2,72,256]{2,1,0:T(8,128)S(1)} collective-permute-done((f32[2,72,256]{2,1,0:T(8,128)S(1)}, f32[2,72,256]{2,1,0:T(8,128)S(1)}, u32[]{:S(2)}, u32[]{:S(2)}) %collective-permute-start.46) | collective-permute-done | bytes 147488 | tf_op jit(solution)/shard_map/ppermute | solution.py:320
  260.9 1.7 collective-permute-start.47
  263.2 2.3 collective-permute-start.40
  265.5 2.2 collective-permute-done.47
  269.2 8.5 %collective-permute-done.48.refs_5_ = f32[8,72,256]{2,1,0:T(8,128)S(1)} collective-permute-done((f32[8,72,256]{2,1,0:T(8,128)S(1)}, f32[8,72,256]{2,1,0:T(8,128)S(1)}, u32[]{:S(2)}, u32[]{:S(2)}) %collective-permute-start.48) | collective-permute-done | bytes 589856 | tf_op jit(solution)/shard_map/ppermute | solution.py:320
  277.7 21.3 %labels.3 = (f32[320,256]{1,0:T(8,128)S(1)}, f32[231,4096]{1,0:T(8,128)}) custom-call(s32[2]{0:T(128)S(1)} %pad_add_fusion.me_ref, bf16[320,4096]{1,0:T(8,128)(2,1)S(1)} %copy-done, bf16[320,4096]{1,0:T(8,128)(2,1)S(1)} %copy-done.1, bf16[320,256]{1,0:T(8,128)(2,1)S(1)} %get-tuple-element.33.feat_ref, bf16[320,32]{1,0:T(8,128)(2,1)S(1)} %get-tuple-element.34.lab1_ref, ...), custom_call_target="tpu_custom_call" | custom-call | flops 14763950080 | bytes 13668352 | tf_op jit(solution)/shard_map/labels/pallas_call | solution.py:349
  (125 shorter events, 42.1 us)
Async XLA Ops:
  11.3 28.9 %collective-permute-start.16 = (f32[8,144,256]{2,1,0:T(8,128)S(1)}, f32[8,144,256]{2,1,0:T(8,128)S(1)}, u32[]{:S(2)}, u32[]{:S(2)}) collective-permute-start(f32[8,144,256]{2,1,0:T(8,128)S(1)} %get-tuple-element.32), channel_id=1, source_target_pairs={{0,2},{1,3},{2,0},{3,1},{4,6},{5,7},{6,4},{7,5},{8,10},{9,11},{10,... | collective-permute-start | bytes 3538952 | tf_op jit(solution)/shard_map/ppermute | solution.py:320
  14.3 31.4 %collective-permute-start = (f32[8,160,256]{2,1,0:T(8,128)S(1)}, f32[8,160,256]{2,1,0:T(8,128)S(1)}, u32[]{:S(2)}, u32[]{:S(2)}) collective-permute-start(f32[8,160,256]{2,1,0:T(8,128)S(1)} %get-tuple-element.28), channel_id=1, source_target_pairs={{0,4},{1,5},{2,6},{3,7},{4,0},{5,1},{6,2},{7,3},{8,12},{9,13},{10,... | collective-permute-start | bytes 3932168 | tf_op jit(solution)/shard_map/ppermute | solution.py:320
  15.8 32.7 %collective-permute-start.8 = (f32[8,160,256]{2,1,0:T(8,128)}, f32[8,160,256]{2,1,0:T(8,128)S(1)}, u32[]{:S(2)}, u32[]{:S(2)}) collective-permute-start(f32[8,160,256]{2,1,0:T(8,128)} %get-tuple-element.30), channel_id=1, source_target_pairs={{0,8},{1,17},{2,10},{3,19},{4,12},{5,21},{6,14},{7,23},{8,0},{9,25... | collective-permute-start | bytes 3932168 | tf_op jit(solution)/shard_map/ppermute | solution.py:320
  41.2 16.0 %collective-permute-start.17 = (f32[4,144,256]{2,1,0:T(8,128)}, f32[4,144,256]{2,1,0:T(8,128)}, u32[]{:S(2)}, u32[]{:S(2)}) collective-permute-start(f32[4,144,256]{2,1,0:T(8,128)} %get-tuple-element.59), channel_id=1, source_target_pairs={{0,4},{1,5},{2,6},{3,7},{4,0},{5,1},{6,2},{7,3},{8,12},{9,13},{10,... | collective-permute-start | bytes 1769480 | tf_op jit(solution)/shard_map/ppermute | solution.py:320
  46.9 18.0 %collective-permute-start.1 = (f32[4,160,256]{2,1,0:T(8,128)}, f32[4,160,256]{2,1,0:T(8,128)}, u32[]{:S(2)}, u32[]{:S(2)}) collective-permute-start(f32[4,160,256]{2,1,0:T(8,128)} %get-tuple-element.55), channel_id=1, source_target_pairs={{0,8},{1,17},{2,10},{3,19},{4,12},{5,21},{6,14},{7,23},{8,0},{9,25... | collective-permute-start | bytes 1966088 | tf_op jit(solution)/shard_map/ppermute | solution.py:320
  49.6 16.6 %collective-permute-start.9 = (f32[4,160,256]{2,1,0:T(8,128)}, f32[4,160,256]{2,1,0:T(8,128)}, u32[]{:S(2)}, u32[]{:S(2)}) collective-permute-start(f32[4,160,256]{2,1,0:T(8,128)} %get-tuple-element.53), channel_id=1, source_target_pairs={{0,2},{1,3},{2,0},{3,1},{4,6},{5,7},{6,4},{7,5},{8,10},{9,11},{10,... | collective-permute-start | bytes 1966088 | tf_op jit(solution)/shard_map/ppermute | solution.py:320
  58.4 11.5 %collective-permute-start.18 = (f32[2,144,256]{2,1,0:T(8,128)S(1)}, f32[2,144,256]{2,1,0:T(8,128)S(1)}, u32[]{:S(2)}, u32[]{:S(2)}) collective-permute-start(f32[2,144,256]{2,1,0:T(8,128)S(1)} %get-tuple-element.71), channel_id=1, source_target_pairs={{0,8},{1,17},{2,10},{3,19},{4,12},{5,21},{6,14},{7,23},{8,0},{9,25... | collective-permute-start | bytes 884744 | tf_op jit(solution)/shard_map/ppermute | solution.py:320
  66.1 7.2 %collective-permute-start.2 = (f32[2,160,256]{2,1,0:T(8,128)S(1)}, f32[2,160,256]{2,1,0:T(8,128)S(1)}, u32[]{:S(2)}, u32[]{:S(2)}) collective-permute-start(f32[2,160,256]{2,1,0:T(8,128)S(1)} %get-tuple-element.67), channel_id=1, source_target_pairs={{0,2},{1,3},{2,0},{3,1},{4,6},{5,7},{6,4},{7,5},{8,10},{9,11},{10,... | collective-permute-start | bytes 983048 | tf_op jit(solution)/shard_map/ppermute | solution.py:320
  67.4 8.7 %collective-permute-start.10 = (f32[2,160,256]{2,1,0:T(8,128)S(1)}, f32[2,160,256]{2,1,0:T(8,128)S(1)}, u32[]{:S(2)}, u32[]{:S(2)}) collective-permute-start(f32[2,160,256]{2,1,0:T(8,128)S(1)} %get-tuple-element.65), channel_id=1, source_target_pairs={{0,4},{1,5},{2,6},{3,7},{4,0},{5,1},{6,2},{7,3},{8,12},{9,13},{10,... | collective-permute-start | bytes 983048 | tf_op jit(solution)/shard_map/ppermute | solution.py:320
  70.0 16.8 %collective-permute-start.19 = (f32[1,144,256]{2,1,0:T(8,128)S(1)}, f32[1,144,256]{2,1,0:T(8,128)S(1)}, u32[]{:S(2)}, u32[]{:S(2)}) collective-permute-start(f32[1,144,256]{2,1,0:T(8,128)S(1)} %slice_add_fusion.34), channel_id=1, source_target_pairs={{0,16},{1,9},{2,18},{3,11},{4,20},{5,13},{6,22},{7,15},{8,24},{9,1... | collective-permute-start | bytes 442376 | tf_op jit(solution)/shard_map/ppermute | solution.py:320
  73.3 7.7 %collective-permute-start.3 = (f32[1,160,256]{2,1,0:T(8,128)S(1)}, f32[1,160,256]{2,1,0:T(8,128)S(1)}, u32[]{:S(2)}, u32[]{:S(2)}) collective-permute-start(f32[1,160,256]{2,1,0:T(8,128)S(1)} %slice_add_fusion.30), channel_id=1, source_target_pairs={{0,16},{1,9},{2,18},{3,11},{4,20},{5,13},{6,22},{7,15},{8,24},{9,1... | collective-permute-start | bytes 491528 | tf_op jit(solution)/shard_map/ppermute | solution.py:320
  76.1 9.6 %collective-permute-start.11 = (f32[1,160,256]{2,1,0:T(8,128)S(1)}, f32[1,160,256]{2,1,0:T(8,128)S(1)}, u32[]{:S(2)}, u32[]{:S(2)}) collective-permute-start(f32[1,160,256]{2,1,0:T(8,128)S(1)} %slice_add_fusion.28), channel_id=1, source_target_pairs={{0,16},{1,9},{2,18},{3,11},{4,20},{5,13},{6,22},{7,15},{8,24},{9,1... | collective-permute-start | bytes 491528 | tf_op jit(solution)/shard_map/ppermute | solution.py:320
  86.7 5.8 %collective-permute-start.12 = (f32[1,80,256]{2,1,0:T(8,128)S(1)}, f32[1,80,256]{2,1,0:T(8,128)S(1)}, u32[]{:S(2)}, u32[]{:S(2)}) collective-permute-start(f32[1,80,256]{2,1,0:T(8,128)S(1)} %bitcast.44), channel_id=1, source_target_pairs={{0,16},{1,9},{2,18},{3,11},{4,20},{5,13},{6,22},{7,15},{8,24},{9,1... | collective-permute-start | bytes 245768 | tf_op jit(solution)/shard_map/ppermute | solution.py:320
  86.9 7.9 %collective-permute-start.4 = (f32[1,80,256]{2,1,0:T(8,128)S(1)}, f32[1,80,256]{2,1,0:T(8,128)S(1)}, u32[]{:S(2)}, u32[]{:S(2)}) collective-permute-start(f32[1,80,256]{2,1,0:T(8,128)S(1)} %bitcast.48), channel_id=1, source_target_pairs={{0,16},{1,9},{2,18},{3,11},{4,20},{5,13},{6,22},{7,15},{8,24},{9,1... | collective-permute-start | bytes 245768 | tf_op jit(solution)/shard_map/ppermute | solution.py:320
  92.5 5.5 %collective-permute-start.13 = (f32[2,80,256]{2,1,0:T(8,128)S(1)}, f32[2,80,256]{2,1,0:T(8,128)S(1)}, u32[]{:S(2)}, u32[]{:S(2)}) collective-permute-start(f32[2,80,256]{2,1,0:T(8,128)S(1)} %pad_maximum_fusion.13), channel_id=1, source_target_pairs={{0,4},{1,5},{2,6},{3,7},{4,0},{5,1},{6,2},{7,3},{8,12},{9,13},{10,... | collective-permute-start | bytes 491528 | tf_op jit(solution)/shard_map/ppermute | solution.py:320
  94.7 9.4 %collective-permute-start.20 = (f32[1,72,256]{2,1,0:T(8,128)S(1)}, f32[1,72,256]{2,1,0:T(8,128)S(1)}, u32[]{:S(2)}, u32[]{:S(2)}) collective-permute-start(f32[1,72,256]{2,1,0:T(8,128)S(1)} %bitcast.52), channel_id=1, source_target_pairs={{0,16},{1,9},{2,18},{3,11},{4,20},{5,13},{6,22},{7,15},{8,24},{9,1... | collective-permute-start | bytes 221192 | tf_op jit(solution)/shard_map/ppermute | solution.py:320
  94.8 9.4 %collective-permute-start.5 = (f32[2,80,256]{2,1,0:T(8,128)S(1)}, f32[2,80,256]{2,1,0:T(8,128)S(1)}, u32[]{:S(2)}, u32[]{:S(2)}) collective-permute-start(f32[2,80,256]{2,1,0:T(8,128)S(1)} %pad_maximum_fusion.12), channel_id=1, source_target_pairs={{0,2},{1,3},{2,0},{3,1},{4,6},{5,7},{6,4},{7,5},{8,10},{9,11},{10,... | collective-permute-start | bytes 491528 | tf_op jit(solution)/shard_map/ppermute | solution.py:320
  98.0 13.2 %collective-permute-start.14 = (f32[4,80,256]{2,1,0:T(8,128)S(1)}, f32[4,80,256]{2,1,0:T(8,128)S(1)}, u32[]{:S(2)}, u32[]{:S(2)}) collective-permute-start(f32[4,80,256]{2,1,0:T(8,128)S(1)} %pad_maximum_fusion.7), channel_id=1, source_target_pairs={{0,2},{1,3},{2,0},{3,1},{4,6},{5,7},{6,4},{7,5},{8,10},{9,11},{10,... | collective-permute-start | bytes 983048 | tf_op jit(solution)/shard_map/ppermute | solution.py:320
  104.1 6.0 %collective-permute-start.21 = (f32[2,72,256]{2,1,0:T(8,128)S(1)}, f32[2,72,256]{2,1,0:T(8,128)S(1)}, u32[]{:S(2)}, u32[]{:S(2)}) collective-permute-start(f32[2,72,256]{2,1,0:T(8,128)S(1)} %pad_maximum_fusion.16), channel_id=1, source_target_pairs={{0,8},{1,17},{2,10},{3,19},{4,12},{5,21},{6,14},{7,23},{8,0},{9,25... | collective-permute-start | bytes 442376 | tf_op jit(solution)/shard_map/ppermute | solution.py:320
  104.2 12.9 %collective-permute-start.6 = (f32[4,80,256]{2,1,0:T(8,128)S(1)}, f32[4,80,256]{2,1,0:T(8,128)S(1)}, u32[]{:S(2)}, u32[]{:S(2)}) collective-permute-start(f32[4,80,256]{2,1,0:T(8,128)S(1)} %pad_maximum_fusion.6), channel_id=1, source_target_pairs={{0,8},{1,17},{2,10},{3,19},{4,12},{5,21},{6,14},{7,23},{8,0},{9,25... | collective-permute-start | bytes 983048 | tf_op jit(solution)/shard_map/ppermute | solution.py:320
  110.1 10.0 %collective-permute-start.22 = (f32[4,72,256]{2,1,0:T(8,128)S(1)}, f32[4,72,256]{2,1,0:T(8,128)S(1)}, u32[]{:S(2)}, u32[]{:S(2)}) collective-permute-start(f32[4,72,256]{2,1,0:T(8,128)S(1)} %pad_maximum_fusion.10), channel_id=1, source_target_pairs={{0,4},{1,5},{2,6},{3,7},{4,0},{5,1},{6,2},{7,3},{8,12},{9,13},{10,... | collective-permute-start | bytes 884744 | tf_op jit(solution)/shard_map/ppermute | solution.py:320
  111.2 18.9 %collective-permute-start.15 = (f32[8,80,256]{2,1,0:T(8,128)S(1)}, f32[8,80,256]{2,1,0:T(8,128)S(1)}, u32[]{:S(2)}, u32[]{:S(2)}) collective-permute-start(f32[8,80,256]{2,1,0:T(8,128)S(1)} %pad_maximum_fusion.1.refs_2_), channel_id=1, source_target_pairs={{0,8},{1,17},{2,10},{3,19},{4,12},{5,21},{6,14},{7,23},{8,0},{9,25... | collective-permute-start | bytes 1966088 | tf_op jit(solution)/shard_map/ppermute | solution.py:320
  117.1 13.0 %collective-permute-start.7 = (f32[8,80,256]{2,1,0:T(8,128)S(1)}, f32[8,80,256]{2,1,0:T(8,128)S(1)}, u32[]{:S(2)}, u32[]{:S(2)}) collective-permute-start(f32[8,80,256]{2,1,0:T(8,128)S(1)} %pad_maximum_fusion.refs_0_), channel_id=1, source_target_pairs={{0,4},{1,5},{2,6},{3,7},{4,0},{5,1},{6,2},{7,3},{8,12},{9,13},{10,... | collective-permute-start | bytes 1966088 | tf_op jit(solution)/shard_map/ppermute | solution.py:320
  120.2 9.9 %collective-permute-start.23 = (f32[8,72,256]{2,1,0:T(8,128)S(1)}, f32[8,72,256]{2,1,0:T(8,128)S(1)}, u32[]{:S(2)}, u32[]{:S(2)}) collective-permute-start(f32[8,72,256]{2,1,0:T(8,128)S(1)} %pad_maximum_fusion.4.refs_4_), channel_id=1, source_target_pairs={{0,2},{1,3},{2,0},{3,1},{4,6},{5,7},{6,4},{7,5},{8,10},{9,11},{10,... | collective-permute-start | bytes 1769480 | tf_op jit(solution)/shard_map/ppermute | solution.py:320
  158.0 28.1 %collective-permute-start.41 = (f32[8,144,256]{2,1,0:T(8,128)S(1)}, f32[8,144,256]{2,1,0:T(8,128)S(1)}, u32[]{:S(2)}, u32[]{:S(2)}) collective-permute-start(f32[8,144,256]{2,1,0:T(8,128)S(1)} %get-tuple-element.42), channel_id=1, source_target_pairs={{0,2},{1,3},{2,0},{3,1},{4,6},{5,7},{6,4},{7,5},{8,10},{9,11},{10,... | collective-permute-start | bytes 3538952 | tf_op jit(solution)/shard_map/ppermute | solution.py:320
  158.9 31.7 %collective-permute-start.25 = (f32[8,160,256]{2,1,0:T(8,128)S(1)}, f32[8,160,256]{2,1,0:T(8,128)S(1)}, u32[]{:S(2)}, u32[]{:S(2)}) collective-permute-start(f32[8,160,256]{2,1,0:T(8,128)S(1)} %get-tuple-element.38), channel_id=1, source_target_pairs={{0,4},{1,5},{2,6},{3,7},{4,0},{5,1},{6,2},{7,3},{8,12},{9,13},{10,... | collective-permute-start | bytes 3932168 | tf_op jit(solution)/shard_map/ppermute | solution.py:320
  160.0 31.7 %collective-permute-start.33 = (f32[8,160,256]{2,1,0:T(8,128)S(1)}, f32[8,160,256]{2,1,0:T(8,128)S(1)}, u32[]{:S(2)}, u32[]{:S(2)}) collective-permute-start(f32[8,160,256]{2,1,0:T(8,128)S(1)} %get-tuple-element.40), channel_id=1, source_target_pairs={{0,8},{1,17},{2,10},{3,19},{4,12},{5,21},{6,14},{7,23},{8,0},{9,25... | collective-permute-start | bytes 3932168 | tf_op jit(solution)/shard_map/ppermute | solution.py:320
  186.2 15.9 %collective-permute-start.42 = (f32[4,144,256]{2,1,0:T(8,128)S(1)}, f32[4,144,256]{2,1,0:T(8,128)S(1)}, u32[]{:S(2)}, u32[]{:S(2)}) collective-permute-start(f32[4,144,256]{2,1,0:T(8,128)S(1)} %get-tuple-element.57), channel_id=1, source_target_pairs={{0,4},{1,5},{2,6},{3,7},{4,0},{5,1},{6,2},{7,3},{8,12},{9,13},{10,... | collective-permute-start | bytes 1769480 | tf_op jit(solution)/shard_map/ppermute | solution.py:320
  190.9 17.7 %collective-permute-start.26 = (f32[4,160,256]{2,1,0:T(8,128)S(1)}, f32[4,160,256]{2,1,0:T(8,128)S(1)}, u32[]{:S(2)}, u32[]{:S(2)}) collective-permute-start(f32[4,160,256]{2,1,0:T(8,128)S(1)} %get-tuple-element.51), channel_id=1, source_target_pairs={{0,8},{1,17},{2,10},{3,19},{4,12},{5,21},{6,14},{7,23},{8,0},{9,25... | collective-permute-start | bytes 1966088 | tf_op jit(solution)/shard_map/ppermute | solution.py:320
  191.9 22.6 %collective-permute-start.34 = (f32[4,160,256]{2,1,0:T(8,128)S(1)}, f32[4,160,256]{2,1,0:T(8,128)S(1)}, u32[]{:S(2)}, u32[]{:S(2)}) collective-permute-start(f32[4,160,256]{2,1,0:T(8,128)S(1)} %get-tuple-element.49), channel_id=1, source_target_pairs={{0,2},{1,3},{2,0},{3,1},{4,6},{5,7},{6,4},{7,5},{8,10},{9,11},{10,... | collective-permute-start | bytes 1966088 | tf_op jit(solution)/shard_map/ppermute | solution.py:320
  202.2 12.2 %collective-permute-start.43 = (f32[2,144,256]{2,1,0:T(8,128)S(1)}, f32[2,144,256]{2,1,0:T(8,128)S(1)}, u32[]{:S(2)}, u32[]{:S(2)}) collective-permute-start(f32[2,144,256]{2,1,0:T(8,128)S(1)} %get-tuple-element.69), channel_id=1, source_target_pairs={{0,8},{1,17},{2,10},{3,19},{4,12},{5,21},{6,14},{7,23},{8,0},{9,25... | collective-permute-start | bytes 884744 | tf_op jit(solution)/shard_map/ppermute | solution.py:320
  208.6 12.6 %collective-permute-start.27 = (f32[2,160,256]{2,1,0:T(8,128)S(1)}, f32[2,160,256]{2,1,0:T(8,128)S(1)}, u32[]{:S(2)}, u32[]{:S(2)}) collective-permute-start(f32[2,160,256]{2,1,0:T(8,128)S(1)} %get-tuple-element.63), channel_id=1, source_target_pairs={{0,2},{1,3},{2,0},{3,1},{4,6},{5,7},{6,4},{7,5},{8,10},{9,11},{10,... | collective-permute-start | bytes 983048 | tf_op jit(solution)/shard_map/ppermute | solution.py:320
  214.4 6.8 %collective-permute-start.44 = (f32[1,144,256]{2,1,0:T(8,128)S(1)}, f32[1,144,256]{2,1,0:T(8,128)S(1)}, u32[]{:S(2)}, u32[]{:S(2)}) collective-permute-start(f32[1,144,256]{2,1,0:T(8,128)S(1)} %slice_add_fusion.32), channel_id=1, source_target_pairs={{0,16},{1,9},{2,18},{3,11},{4,20},{5,13},{6,22},{7,15},{8,24},{9,1... | collective-permute-start | bytes 442376 | tf_op jit(solution)/shard_map/ppermute | solution.py:320
  214.6 7.8 %collective-permute-start.35 = (f32[2,160,256]{2,1,0:T(8,128)S(1)}, f32[2,160,256]{2,1,0:T(8,128)S(1)}, u32[]{:S(2)}, u32[]{:S(2)}) collective-permute-start(f32[2,160,256]{2,1,0:T(8,128)S(1)} %get-tuple-element.61), channel_id=1, source_target_pairs={{0,4},{1,5},{2,6},{3,7},{4,0},{5,1},{6,2},{7,3},{8,12},{9,13},{10,... | collective-permute-start | bytes 983048 | tf_op jit(solution)/shard_map/ppermute | solution.py:320
  221.3 9.3 %collective-permute-start.28 = (f32[1,160,256]{2,1,0:T(8,128)S(1)}, f32[1,160,256]{2,1,0:T(8,128)S(1)}, u32[]{:S(2)}, u32[]{:S(2)}) collective-permute-start(f32[1,160,256]{2,1,0:T(8,128)S(1)} %slice_add_fusion.26), channel_id=1, source_target_pairs={{0,16},{1,9},{2,18},{3,11},{4,20},{5,13},{6,22},{7,15},{8,24},{9,1... | collective-permute-start | bytes 491528 | tf_op jit(solution)/shard_map/ppermute | solution.py:320
  222.5 9.9 %collective-permute-start.36 = (f32[1,160,256]{2,1,0:T(8,128)S(1)}, f32[1,160,256]{2,1,0:T(8,128)S(1)}, u32[]{:S(2)}, u32[]{:S(2)}) collective-permute-start(f32[1,160,256]{2,1,0:T(8,128)S(1)} %slice_add_fusion.24), channel_id=1, source_target_pairs={{0,16},{1,9},{2,18},{3,11},{4,20},{5,13},{6,22},{7,15},{8,24},{9,1... | collective-permute-start | bytes 491528 | tf_op jit(solution)/shard_map/ppermute | solution.py:320
  230.6 12.0 %collective-permute-start.29 = (f32[1,80,256]{2,1,0:T(8,128)S(1)}, f32[1,80,256]{2,1,0:T(8,128)S(1)}, u32[]{:S(2)}, u32[]{:S(2)}) collective-permute-start(f32[1,80,256]{2,1,0:T(8,128)S(1)} %fusion.13), channel_id=1, source_target_pairs={{0,16},{1,9},{2,18},{3,11},{4,20},{5,13},{6,22},{7,15},{8,24},{9,1... | collective-permute-start | bytes 245768 | tf_op jit(solution)/shard_map/ppermute | solution.py:320
  232.4 12.6 %collective-permute-start.37 = (f32[1,80,256]{2,1,0:T(8,128)S(1)}, f32[1,80,256]{2,1,0:T(8,128)S(1)}, u32[]{:S(2)}, u32[]{:S(2)}) collective-permute-start(f32[1,80,256]{2,1,0:T(8,128)S(1)} %fusion.9), channel_id=1, source_target_pairs={{0,16},{1,9},{2,18},{3,11},{4,20},{5,13},{6,22},{7,15},{8,24},{9,1... | collective-permute-start | bytes 245768 | tf_op jit(solution)/shard_map/ppermute | solution.py:320
  242.7 5.5 %collective-permute-start.30 = (f32[2,80,256]{2,1,0:T(8,128)S(1)}, f32[2,80,256]{2,1,0:T(8,128)S(1)}, u32[]{:S(2)}, u32[]{:S(2)}) collective-permute-start(f32[2,80,256]{2,1,0:T(8,128)S(1)} %pad_maximum_fusion.14), channel_id=1, source_target_pairs={{0,2},{1,3},{2,0},{3,1},{4,6},{5,7},{6,4},{7,5},{8,10},{9,11},{10,... | collective-permute-start | bytes 491528 | tf_op jit(solution)/shard_map/ppermute | solution.py:320
  245.0 5.3 %collective-permute-start.45 = (f32[1,72,256]{2,1,0:T(8,128)S(1)}, f32[1,72,256]{2,1,0:T(8,128)S(1)}, u32[]{:S(2)}, u32[]{:S(2)}) collective-permute-start(f32[1,72,256]{2,1,0:T(8,128)S(1)} %fusion.24), channel_id=1, source_target_pairs={{0,16},{1,9},{2,18},{3,11},{4,20},{5,13},{6,22},{7,15},{8,24},{9,1... | collective-permute-start | bytes 221192 | tf_op jit(solution)/shard_map/ppermute | solution.py:320
  245.1 5.4 %collective-permute-start.38 = (f32[2,80,256]{2,1,0:T(8,128)S(1)}, f32[2,80,256]{2,1,0:T(8,128)S(1)}, u32[]{:S(2)}, u32[]{:S(2)}) collective-permute-start(f32[2,80,256]{2,1,0:T(8,128)S(1)} %pad_maximum_fusion.15), channel_id=1, source_target_pairs={{0,4},{1,5},{2,6},{3,7},{4,0},{5,1},{6,2},{7,3},{8,12},{9,13},{10,... | collective-permute-start | bytes 491528 | tf_op jit(solution)/shard_map/ppermute | solution.py:320
  248.3 14.3 %collective-permute-start.31 = (f32[4,80,256]{2,1,0:T(8,128)S(1)}, f32[4,80,256]{2,1,0:T(8,128)S(1)}, u32[]{:S(2)}, u32[]{:S(2)}) collective-permute-start(f32[4,80,256]{2,1,0:T(8,128)S(1)} %pad_maximum_fusion.8), channel_id=1, source_target_pairs={{0,8},{1,17},{2,10},{3,19},{4,12},{5,21},{6,14},{7,23},{8,0},{9,25... | collective-permute-start | bytes 983048 | tf_op jit(solution)/shard_map/ppermute | solution.py:320
  250.3 10.6 %collective-permute-start.46 = (f32[2,72,256]{2,1,0:T(8,128)S(1)}, f32[2,72,256]{2,1,0:T(8,128)S(1)}, u32[]{:S(2)}, u32[]{:S(2)}) collective-permute-start(f32[2,72,256]{2,1,0:T(8,128)S(1)} %pad_maximum_fusion.17), channel_id=1, source_target_pairs={{0,8},{1,17},{2,10},{3,19},{4,12},{5,21},{6,14},{7,23},{8,0},{9,25... | collective-permute-start | bytes 442376 | tf_op jit(solution)/shard_map/ppermute | solution.py:320
  250.5 12.6 %collective-permute-start.39 = (f32[4,80,256]{2,1,0:T(8,128)S(1)}, f32[4,80,256]{2,1,0:T(8,128)S(1)}, u32[]{:S(2)}, u32[]{:S(2)}) collective-permute-start(f32[4,80,256]{2,1,0:T(8,128)S(1)} %pad_maximum_fusion.9), channel_id=1, source_target_pairs={{0,2},{1,3},{2,0},{3,1},{4,6},{5,7},{6,4},{7,5},{8,10},{9,11},{10,... | collective-permute-start | bytes 983048 | tf_op jit(solution)/shard_map/ppermute | solution.py:320
  260.9 6.8 %collective-permute-start.47 = (f32[4,72,256]{2,1,0:T(8,128)S(1)}, f32[4,72,256]{2,1,0:T(8,128)S(1)}, u32[]{:S(2)}, u32[]{:S(2)}) collective-permute-start(f32[4,72,256]{2,1,0:T(8,128)S(1)} %pad_maximum_fusion.11), channel_id=1, source_target_pairs={{0,4},{1,5},{2,6},{3,7},{4,0},{5,1},{6,2},{7,3},{8,12},{9,13},{10,... | collective-permute-start | bytes 884744 | tf_op jit(solution)/shard_map/ppermute | solution.py:320
  262.6 15.1 %collective-permute-start.32 = (f32[8,80,256]{2,1,0:T(8,128)S(1)}, f32[8,80,256]{2,1,0:T(8,128)S(1)}, u32[]{:S(2)}, u32[]{:S(2)}) collective-permute-start(f32[8,80,256]{2,1,0:T(8,128)S(1)} %pad_maximum_fusion.2.refs_0_), channel_id=1, source_target_pairs={{0,4},{1,5},{2,6},{3,7},{4,0},{5,1},{6,2},{7,3},{8,12},{9,13},{10,... | collective-permute-start | bytes 1966088 | tf_op jit(solution)/shard_map/ppermute | solution.py:320
  263.2 14.5 %collective-permute-start.40 = (f32[8,80,256]{2,1,0:T(8,128)S(1)}, f32[8,80,256]{2,1,0:T(8,128)S(1)}, u32[]{:S(2)}, u32[]{:S(2)}) collective-permute-start(f32[8,80,256]{2,1,0:T(8,128)S(1)} %pad_maximum_fusion.3.refs_2_), channel_id=1, source_target_pairs={{0,8},{1,17},{2,10},{3,19},{4,12},{5,21},{6,14},{7,23},{8,0},{9,25... | collective-permute-start | bytes 1966088 | tf_op jit(solution)/shard_map/ppermute | solution.py:320
  267.7 9.9 %collective-permute-start.48 = (f32[8,72,256]{2,1,0:T(8,128)S(1)}, f32[8,72,256]{2,1,0:T(8,128)S(1)}, u32[]{:S(2)}, u32[]{:S(2)}) collective-permute-start(f32[8,72,256]{2,1,0:T(8,128)S(1)} %pad_maximum_fusion.5.refs_4_), channel_id=1, source_target_pairs={{0,2},{1,3},{2,0},{3,1},{4,6},{5,7},{6,4},{7,5},{8,10},{9,11},{10,... | collective-permute-start | bytes 1769480 | tf_op jit(solution)/shard_map/ppermute | solution.py:320
  (11 other events, 136.6 us)

commit v6 on v5

--- a/solution.py
+++ b/solution.py
@@ -488,8 +488,9 @@
     cuts = [0, third, 2 * third, height]
     rest = list(range(3, bits))
     orders = [[1, 2, 0] + rest, [2, 0, 1] + rest, [0, 1, 2] + rest]
+    back = [[1, 2, 0] + rest, [0, 1, 2] + rest, [2, 0, 1] + rest]
     parts = [
-        {"start": cuts[i], "rows": cuts[i + 1] - cuts[i], "order": orders[i]} for i in range(3)
+        {"start": cuts[i], "rows": cuts[i + 1] - cuts[i], "order": back[i]} for i in range(3)
     ]
     sums = [
         {"curv": (cuts[i], cuts[i + 1]), "grad": (cuts[i], cuts[i + 1]), "rows": 2 * parts[i]["rows"], "order": orders[i]}

time: 302 us -> 301 us (level)
  transfers between devices with their start and end apart: 50 -> 50, of which waited for: 32 -> 33; matrix products, arithmetic and copies ran while one was open for 4% -> 4% of each run, Pallas kernels for 0% -> 0%
where the time goes in v6:
time: 301 us
  waiting for transfers between devices  173 us (57%)
  starting transfers between devices  57.7 us (19%)
  Pallas kernels  56.6 us (19%)
  other arithmetic  9.61 us (3%)
  local copies, waits for them, and re-layouts  3.26 us (1%)
    ppermute x48, waiting for transfers between devices, exchange(): return lax.ppermute(value, ('star', 'pix'), pairs)  169 us
    ppermute x48, starting transfers between devices, exchange(): return lax.ppermute(value, ('star', 'pix'), pairs)  57.6 us
    pallas_call x4, Pallas kernels, call(): pl.pallas_call(kernel, out_shape=shapes, in_specs=[scalar] + (specs or [w...  55.3 us
    add x12, other arithmetic, reduced(): kept = kept[:size] + arrived[:size]  7.65 us
  transfers between devices with their start and end apart: 50, of which 33 were waited for; matrix products, arithmetic and copies ran while one was open for 4% of the time, Pallas kernels for 0%

profile of v6, /device:TPU:0, one launch (start us, length us, event | category | flops | bytes accessed | tf_op | source)
XLA Modules:
  0.0 300.8 jit_solution(5427540318023611638)
XLA Ops:
  2.9 8.4 %first.1 = (f32[320,32]{1,0:T(8,128)S(1)}, bf16[320,256]{1,0:T(8,128)(2,1)S(1)}, bf16[256,320]{1,0:T(8,128)(2,1)}, bf16[256,320]{1,0:T(8,128)(2,1)}, bf16[320,32...) custom-call(s32[2]{0:T(128)S(1)} %pad_add_fusion.me_ref, ...), custom_call_target="tpu_custom_call" | custom-call | flops 1824522240 | bytes 17241088 | tf_op jit(solution)/shard_map/first/pallas_call | solution.py:349
  11.3 3.0 collective-permute-start.16
  15.8 1.6 collective-permute-start.8
  17.4 22.9 %collective-permute-done.16 = f32[8,144,256]{2,1,0:T(8,128)S(1)} collective-permute-done((f32[8,144,256]{2,1,0:T(8,128)S(1)}, f32[8,144,256]{2,1,0:T(8,128)S(1)}, u32[]{:S(2)}, u32[]{:S(2)}) %collective-permute-start.16) | collective-permute-done | bytes 1179680 | tf_op jit(solution)/shard_map/ppermute | solution.py:320
  41.2 1.8 collective-permute-start.17
  43.0 2.7 collective-permute-done
  46.9 1.6 collective-permute-start.1
  50.6 6.7 %collective-permute-done.17 = f32[4,144,256]{2,1,0:T(8,128)} collective-permute-done((f32[4,144,256]{2,1,0:T(8,128)}, f32[4,144,256]{2,1,0:T(8,128)}, u32[]{:S(2)}, u32[]{:S(2)}) %collective-permute-start.17) | collective-permute-done | bytes 589856 | tf_op jit(solution)/shard_map/ppermute | solution.py:320
  58.4 1.6 collective-permute-start.18
  60.1 4.8 %collective-permute-done.1 = f32[4,160,256]{2,1,0:T(8,128)} collective-permute-done((f32[4,160,256]{2,1,0:T(8,128)}, f32[4,160,256]{2,1,0:T(8,128)}, u32[]{:S(2)}, u32[]{:S(2)}) %collective-permute-start.1) | collective-permute-done | bytes 655392 | tf_op jit(solution)/shard_map/ppermute | solution.py:320
  67.4 1.7 collective-permute-start.10
  70.0 2.8 collective-permute-start.19
  73.3 2.8 collective-permute-start.3
  77.3 3.6 %collective-permute-done.3 = f32[1,160,256]{2,1,0:T(8,128)S(1)} collective-permute-done((f32[1,160,256]{2,1,0:T(8,128)S(1)}, f32[1,160,256]{2,1,0:T(8,128)S(1)}, u32[]{:S(2)}, u32[]{:S(2)}) %collective-permute-start.3) | collective-permute-done | bytes 163872 | tf_op jit(solution)/shard_map/ppermute | solution.py:320
  81.0 4.7 %collective-permute-done.11 = f32[1,160,256]{2,1,0:T(8,128)S(1)} collective-permute-done((f32[1,160,256]{2,1,0:T(8,128)S(1)}, f32[1,160,256]{2,1,0:T(8,128)S(1)}, u32[]{:S(2)}, u32[]{:S(2)}) %collective-permute-start.11) | collective-permute-done | bytes 163872 | tf_op jit(solution)/shard_map/ppermute | solution.py:320
  86.9 3.0 collective-permute-start.4
  89.8 6.0 %collective-permute-done.12 = f32[1,80,256]{2,1,0:T(8,128)S(1)} collective-permute-done((f32[1,80,256]{2,1,0:T(8,128)S(1)}, f32[1,80,256]{2,1,0:T(8,128)S(1)}, u32[]{:S(2)}, u32[]{:S(2)}) %collective-permute-start.12) | collective-permute-done | bytes 81952 | tf_op jit(solution)/shard_map/ppermute | solution.py:320
  95.9 2.3 collective-permute-start.20
  99.6 2.7 collective-permute-done.13
  102.3 1.5 collective-permute-start.14
  105.8 5.2 %collective-permute-done.21 = f32[2,72,256]{2,1,0:T(8,128)S(1)} collective-permute-done((f32[2,72,256]{2,1,0:T(8,128)S(1)}, f32[2,72,256]{2,1,0:T(8,128)S(1)}, u32[]{:S(2)}, u32[]{:S(2)}) %collective-permute-start.21) | collective-permute-done | bytes 147488 | tf_op jit(solution)/shard_map/ppermute | solution.py:320
  111.1 1.6 collective-permute-start.22
  113.4 1.5 collective-permute-start.7
  114.9 5.1 %collective-permute-done.22 = f32[4,72,256]{2,1,0:T(8,128)S(1)} collective-permute-done((f32[4,72,256]{2,1,0:T(8,128)S(1)}, f32[4,72,256]{2,1,0:T(8,128)S(1)}, u32[]{:S(2)}, u32[]{:S(2)}) %collective-permute-start.22) | collective-permute-done | bytes 294944 | tf_op jit(solution)/shard_map/ppermute | solution.py:320
  120.3 12.4 %collective-permute-done.23.refs_5_ = f32[8,72,256]{2,1,0:T(8,128)S(1)} collective-permute-done((f32[8,72,256]{2,1,0:T(8,128)S(1)}, f32[8,72,256]{2,1,0:T(8,128)S(1)}, u32[]{:S(2)}, u32[]{:S(2)}) %collective-permute-start.23) | collective-permute-done | bytes 589856 | tf_op jit(solution)/shard_map/ppermute | solution.py:320
  132.8 21.1 %labels.2.here_ref = f32[320,256]{1,0:T(8,128)S(1)} custom-call(s32[2]{0:T(128)S(1)} %pad_add_fusion.me_ref, bf16[320,4096]{1,0:T(8,128)(2,1)S(1)} %copy-done, bf16[320,4096]{1,0:T(8,128)(2,1)S(1)} %copy-done.1, bf16[320,256]{1,0:T(8,128)(2,1)S(1)} %get-tuple-element.25.feat_ref, bf16[320,32]{1,0:T(8,128)(2,1)S(1)} %get-tuple-element.26.lab1_ref, ...), custom_call_target="tpu_custom_call" | custom-call | flops 14763950080 | bytes 9883648 | tf_op jit(solution)/shard_map/labels/pallas_call | solution.py:349
  153.9 1.6 collective-permute-done.24.there_ref
  156.1 4.5 %gradient.1 = (f32[8,160,256]{2,1,0:T(8,128)S(1)}, f32[8,160,256]{2,1,0:T(8,128)S(1)}, f32[8,160,256]{2,1,0:T(8,128)S(1)}, f32[8,160,256]{2,1,0:T(8,128)S(1)}, f...) custom-call(s32[2]{0:T(128)S(1)} %pad_add_fusion.me_ref, bf16[320,4096]{1,0:T(8,128)(2,1)S(1)} %copy-done, ...), custom_call_target="tpu_custom_call" | custom-call | flops 1824522240 | bytes 17137664 | tf_op jit(solution)/shard_map/gradient/pallas_call | solution.py:349
  162.5 26.2 %collective-permute-done.41 = f32[8,144,256]{2,1,0:T(8,128)S(1)} collective-permute-done((f32[8,144,256]{2,1,0:T(8,128)S(1)}, f32[8,144,256]{2,1,0:T(8,128)S(1)}, u32[]{:S(2)}, u32[]{:S(2)}) %collective-permute-start.41) | collective-permute-done | bytes 1179680 | tf_op jit(solution)/shard_map/ppermute | solution.py:320
  190.3 2.9 collective-permute-done.25
  194.1 1.7 collective-permute-start.34
  195.8 8.9 %collective-permute-done.42 = f32[4,144,256]{2,1,0:T(8,128)S(1)} collective-permute-done((f32[4,144,256]{2,1,0:T(8,128)S(1)}, f32[4,144,256]{2,1,0:T(8,128)S(1)}, u32[]{:S(2)}, u32[]{:S(2)}) %collective-permute-start.42) | collective-permute-done | bytes 589856 | tf_op jit(solution)/shard_map/ppermute | solution.py:320
  204.9 6.9 %collective-permute-done.26 = f32[4,160,256]{2,1,0:T(8,128)S(1)} collective-permute-done((f32[4,160,256]{2,1,0:T(8,128)S(1)}, f32[4,160,256]{2,1,0:T(8,128)S(1)}, u32[]{:S(2)}, u32[]{:S(2)}) %collective-permute-start.26) | collective-permute-done | bytes 655392 | tf_op jit(solution)/shard_map/ppermute | solution.py:320
  211.9 1.8 collective-permute-start.27
  213.6 3.3 %collective-permute-done.43 = f32[2,144,256]{2,1,0:T(8,128)S(1)} collective-permute-done((f32[2,144,256]{2,1,0:T(8,128)S(1)}, f32[2,144,256]{2,1,0:T(8,128)S(1)}, u32[]{:S(2)}, u32[]{:S(2)}) %collective-permute-start.43) | collective-permute-done | bytes 294944 | tf_op jit(solution)/shard_map/ppermute | solution.py:320
  217.9 5.8 %collective-permute-done.44 = f32[1,144,256]{2,1,0:T(8,128)S(1)} collective-permute-done((f32[1,144,256]{2,1,0:T(8,128)S(1)}, f32[1,144,256]{2,1,0:T(8,128)S(1)}, u32[]{:S(2)}, u32[]{:S(2)}) %collective-permute-start.44) | collective-permute-done | bytes 147488 | tf_op jit(solution)/shard_map/ppermute | solution.py:320
  224.3 3.0 collective-permute-start.36
  227.3 5.8 %collective-permute-done.28 = f32[1,160,256]{2,1,0:T(8,128)S(1)} collective-permute-done((f32[1,160,256]{2,1,0:T(8,128)S(1)}, f32[1,160,256]{2,1,0:T(8,128)S(1)}, u32[]{:S(2)}, u32[]{:S(2)}) %collective-permute-start.28) | collective-permute-done | bytes 163872 | tf_op jit(solution)/shard_map/ppermute | solution.py:320
  233.3 8.4 %collective-permute-done.36 = f32[1,160,256]{2,1,0:T(8,128)S(1)} collective-permute-done((f32[1,160,256]{2,1,0:T(8,128)S(1)}, f32[1,160,256]{2,1,0:T(8,128)S(1)}, u32[]{:S(2)}, u32[]{:S(2)}) %collective-permute-start.36) | collective-permute-done | bytes 163872 | tf_op jit(solution)/shard_map/ppermute | solution.py:320
  241.8 1.6 collective-permute-done.29
  243.4 2.6 collective-permute-start.30
  248.3 2.2 collective-permute-done.30
  254.5 4.4 %collective-permute-done.46 = f32[2,72,256]{2,1,0:T(8,128)S(1)} collective-permute-done((f32[2,72,256]{2,1,0:T(8,128)S(1)}, f32[2,72,256]{2,1,0:T(8,128)S(1)}, u32[]{:S(2)}, u32[]{:S(2)}) %collective-permute-start.46) | collective-permute-done | bytes 147488 | tf_op jit(solution)/shard_map/ppermute | solution.py:320
  261.6 2.0 collective-permute-done.39
  263.6 3.4 %collective-permute-start.40 = (f32[8,80,256]{2,1,0:T(8,128)S(1)}, f32[8,80,256]{2,1,0:T(8,128)S(1)}, u32[]{:S(2)}, u32[]{:S(2)}) collective-permute-start(f32[8,80,256]{2,1,0:T(8,128)S(1)} %pad_maximum_fusion.3.refs_2_), channel_id=1, source_target_pairs={{0,2},{1,3},{2,0},{3,1},{4,6},{5,7},{6,4},{7,5},{8,10},{9,11},{10,... | collective-permute-start | bytes 1966088 | tf_op jit(solution)/shard_map/ppermute | solution.py:320
  267.1 9.9 %collective-permute-done.48.refs_5_ = f32[8,72,256]{2,1,0:T(8,128)S(1)} collective-permute-done((f32[8,72,256]{2,1,0:T(8,128)S(1)}, f32[8,72,256]{2,1,0:T(8,128)S(1)}, u32[]{:S(2)}, u32[]{:S(2)}) %collective-permute-start.48) | collective-permute-done | bytes 589856 | tf_op jit(solution)/shard_map/ppermute | solution.py:320
  277.0 21.4 %labels.3 = (f32[320,256]{1,0:T(8,128)S(1)}, f32[231,4096]{1,0:T(8,128)}) custom-call(s32[2]{0:T(128)S(1)} %pad_add_fusion.me_ref, bf16[320,4096]{1,0:T(8,128)(2,1)S(1)} %copy-done, bf16[320,4096]{1,0:T(8,128)(2,1)S(1)} %copy-done.1, bf16[320,256]{1,0:T(8,128)(2,1)S(1)} %get-tuple-element.33.feat_ref, bf16[320,32]{1,0:T(8,128)(2,1)S(1)} %get-tuple-element.34.lab1_ref, ...), custom_call_target="tpu_custom_call" | custom-call | flops 14763950080 | bytes 13668352 | tf_op jit(solution)/shard_map/labels/pallas_call | solution.py:349
  298.4 1.6 collective-permute-done.49.there_ref
  (125 shorter events, 36.9 us)
Async XLA Ops:
  11.3 28.9 %collective-permute-start.16 = (f32[8,144,256]{2,1,0:T(8,128)S(1)}, f32[8,144,256]{2,1,0:T(8,128)S(1)}, u32[]{:S(2)}, u32[]{:S(2)}) collective-permute-start(f32[8,144,256]{2,1,0:T(8,128)S(1)} %get-tuple-element.32), channel_id=1, source_target_pairs={{0,2},{1,3},{2,0},{3,1},{4,6},{5,7},{6,4},{7,5},{8,10},{9,11},{10,... | collective-permute-start | bytes 3538952 | tf_op jit(solution)/shard_map/ppermute | solution.py:320
  14.3 31.4 %collective-permute-start = (f32[8,160,256]{2,1,0:T(8,128)S(1)}, f32[8,160,256]{2,1,0:T(8,128)S(1)}, u32[]{:S(2)}, u32[]{:S(2)}) collective-permute-start(f32[8,160,256]{2,1,0:T(8,128)S(1)} %get-tuple-element.28), channel_id=1, source_target_pairs={{0,4},{1,5},{2,6},{3,7},{4,0},{5,1},{6,2},{7,3},{8,12},{9,13},{10,... | collective-permute-start | bytes 3932168 | tf_op jit(solution)/shard_map/ppermute | solution.py:320
  15.8 32.7 %collective-permute-start.8 = (f32[8,160,256]{2,1,0:T(8,128)}, f32[8,160,256]{2,1,0:T(8,128)S(1)}, u32[]{:S(2)}, u32[]{:S(2)}) collective-permute-start(f32[8,160,256]{2,1,0:T(8,128)} %get-tuple-element.30), channel_id=1, source_target_pairs={{0,8},{1,17},{2,10},{3,19},{4,12},{5,21},{6,14},{7,23},{8,0},{9,25... | collective-permute-start | bytes 3932168 | tf_op jit(solution)/shard_map/ppermute | solution.py:320
  41.2 16.0 %collective-permute-start.17 = (f32[4,144,256]{2,1,0:T(8,128)}, f32[4,144,256]{2,1,0:T(8,128)}, u32[]{:S(2)}, u32[]{:S(2)}) collective-permute-start(f32[4,144,256]{2,1,0:T(8,128)} %get-tuple-element.59), channel_id=1, source_target_pairs={{0,4},{1,5},{2,6},{3,7},{4,0},{5,1},{6,2},{7,3},{8,12},{9,13},{10,... | collective-permute-start | bytes 1769480 | tf_op jit(solution)/shard_map/ppermute | solution.py:320
  46.9 18.0 %collective-permute-start.1 = (f32[4,160,256]{2,1,0:T(8,128)}, f32[4,160,256]{2,1,0:T(8,128)}, u32[]{:S(2)}, u32[]{:S(2)}) collective-permute-start(f32[4,160,256]{2,1,0:T(8,128)} %get-tuple-element.55), channel_id=1, source_target_pairs={{0,8},{1,17},{2,10},{3,19},{4,12},{5,21},{6,14},{7,23},{8,0},{9,25... | collective-permute-start | bytes 1966088 | tf_op jit(solution)/shard_map/ppermute | solution.py:320
  49.6 16.6 %collective-permute-start.9 = (f32[4,160,256]{2,1,0:T(8,128)}, f32[4,160,256]{2,1,0:T(8,128)}, u32[]{:S(2)}, u32[]{:S(2)}) collective-permute-start(f32[4,160,256]{2,1,0:T(8,128)} %get-tuple-element.53), channel_id=1, source_target_pairs={{0,2},{1,3},{2,0},{3,1},{4,6},{5,7},{6,4},{7,5},{8,10},{9,11},{10,... | collective-permute-start | bytes 1966088 | tf_op jit(solution)/shard_map/ppermute | solution.py:320
  58.4 11.5 %collective-permute-start.18 = (f32[2,144,256]{2,1,0:T(8,128)S(1)}, f32[2,144,256]{2,1,0:T(8,128)S(1)}, u32[]{:S(2)}, u32[]{:S(2)}) collective-permute-start(f32[2,144,256]{2,1,0:T(8,128)S(1)} %get-tuple-element.71), channel_id=1, source_target_pairs={{0,8},{1,17},{2,10},{3,19},{4,12},{5,21},{6,14},{7,23},{8,0},{9,25... | collective-permute-start | bytes 884744 | tf_op jit(solution)/shard_map/ppermute | solution.py:320
  66.1 7.2 %collective-permute-start.2 = (f32[2,160,256]{2,1,0:T(8,128)S(1)}, f32[2,160,256]{2,1,0:T(8,128)S(1)}, u32[]{:S(2)}, u32[]{:S(2)}) collective-permute-start(f32[2,160,256]{2,1,0:T(8,128)S(1)} %get-tuple-element.67), channel_id=1, source_target_pairs={{0,2},{1,3},{2,0},{3,1},{4,6},{5,7},{6,4},{7,5},{8,10},{9,11},{10,... | collective-permute-start | bytes 983048 | tf_op jit(solution)/shard_map/ppermute | solution.py:320
  67.4 8.7 %collective-permute-start.10 = (f32[2,160,256]{2,1,0:T(8,128)S(1)}, f32[2,160,256]{2,1,0:T(8,128)S(1)}, u32[]{:S(2)}, u32[]{:S(2)}) collective-permute-start(f32[2,160,256]{2,1,0:T(8,128)S(1)} %get-tuple-element.65), channel_id=1, source_target_pairs={{0,4},{1,5},{2,6},{3,7},{4,0},{5,1},{6,2},{7,3},{8,12},{9,13},{10,... | collective-permute-start | bytes 983048 | tf_op jit(solution)/shard_map/ppermute | solution.py:320
  70.0 16.8 %collective-permute-start.19 = (f32[1,144,256]{2,1,0:T(8,128)S(1)}, f32[1,144,256]{2,1,0:T(8,128)S(1)}, u32[]{:S(2)}, u32[]{:S(2)}) collective-permute-start(f32[1,144,256]{2,1,0:T(8,128)S(1)} %slice_add_fusion.34), channel_id=1, source_target_pairs={{0,16},{1,9},{2,18},{3,11},{4,20},{5,13},{6,22},{7,15},{8,24},{9,1... | collective-permute-start | bytes 442376 | tf_op jit(solution)/shard_map/ppermute | solution.py:320
  73.3 7.7 %collective-permute-start.3 = (f32[1,160,256]{2,1,0:T(8,128)S(1)}, f32[1,160,256]{2,1,0:T(8,128)S(1)}, u32[]{:S(2)}, u32[]{:S(2)}) collective-permute-start(f32[1,160,256]{2,1,0:T(8,128)S(1)} %slice_add_fusion.30), channel_id=1, source_target_pairs={{0,16},{1,9},{2,18},{3,11},{4,20},{5,13},{6,22},{7,15},{8,24},{9,1... | collective-permute-start | bytes 491528 | tf_op jit(solution)/shard_map/ppermute | solution.py:320
  76.1 9.6 %collective-permute-start.11 = (f32[1,160,256]{2,1,0:T(8,128)S(1)}, f32[1,160,256]{2,1,0:T(8,128)S(1)}, u32[]{:S(2)}, u32[]{:S(2)}) collective-permute-start(f32[1,160,256]{2,1,0:T(8,128)S(1)} %slice_add_fusion.28), channel_id=1, source_target_pairs={{0,16},{1,9},{2,18},{3,11},{4,20},{5,13},{6,22},{7,15},{8,24},{9,1... | collective-permute-start | bytes 491528 | tf_op jit(solution)/shard_map/ppermute | solution.py:320
  86.7 9.1 %collective-permute-start.12 = (f32[1,80,256]{2,1,0:T(8,128)S(1)}, f32[1,80,256]{2,1,0:T(8,128)S(1)}, u32[]{:S(2)}, u32[]{:S(2)}) collective-permute-start(f32[1,80,256]{2,1,0:T(8,128)S(1)} %bitcast.44), channel_id=1, source_target_pairs={{0,16},{1,9},{2,18},{3,11},{4,20},{5,13},{6,22},{7,15},{8,24},{9,1... | collective-permute-start | bytes 245768 | tf_op jit(solution)/shard_map/ppermute | solution.py:320
  86.9 11.4 %collective-permute-start.4 = (f32[1,80,256]{2,1,0:T(8,128)S(1)}, f32[1,80,256]{2,1,0:T(8,128)S(1)}, u32[]{:S(2)}, u32[]{:S(2)}) collective-permute-start(f32[1,80,256]{2,1,0:T(8,128)S(1)} %bitcast.48), channel_id=1, source_target_pairs={{0,16},{1,9},{2,18},{3,11},{4,20},{5,13},{6,22},{7,15},{8,24},{9,1... | collective-permute-start | bytes 245768 | tf_op jit(solution)/shard_map/ppermute | solution.py:320
  95.8 6.5 %collective-permute-start.13 = (f32[2,80,256]{2,1,0:T(8,128)S(1)}, f32[2,80,256]{2,1,0:T(8,128)S(1)}, u32[]{:S(2)}, u32[]{:S(2)}) collective-permute-start(f32[2,80,256]{2,1,0:T(8,128)S(1)} %pad_maximum_fusion.13), channel_id=1, source_target_pairs={{0,8},{1,17},{2,10},{3,19},{4,12},{5,21},{6,14},{7,23},{8,0},{9,25... | collective-permute-start | bytes 491528 | tf_op jit(solution)/shard_map/ppermute | solution.py:320
  95.9 8.0 %collective-permute-start.20 = (f32[1,72,256]{2,1,0:T(8,128)S(1)}, f32[1,72,256]{2,1,0:T(8,128)S(1)}, u32[]{:S(2)}, u32[]{:S(2)}) collective-permute-start(f32[1,72,256]{2,1,0:T(8,128)S(1)} %bitcast.52), channel_id=1, source_target_pairs={{0,16},{1,9},{2,18},{3,11},{4,20},{5,13},{6,22},{7,15},{8,24},{9,1... | collective-permute-start | bytes 221192 | tf_op jit(solution)/shard_map/ppermute | solution.py:320
  98.3 6.2 %collective-permute-start.5 = (f32[2,80,256]{2,1,0:T(8,128)S(1)}, f32[2,80,256]{2,1,0:T(8,128)S(1)}, u32[]{:S(2)}, u32[]{:S(2)}) collective-permute-start(f32[2,80,256]{2,1,0:T(8,128)S(1)} %pad_maximum_fusion.12), channel_id=1, source_target_pairs={{0,2},{1,3},{2,0},{3,1},{4,6},{5,7},{6,4},{7,5},{8,10},{9,11},{10,... | collective-permute-start | bytes 491528 | tf_op jit(solution)/shard_map/ppermute | solution.py:320
  102.3 10.3 %collective-permute-start.14 = (f32[4,80,256]{2,1,0:T(8,128)S(1)}, f32[4,80,256]{2,1,0:T(8,128)S(1)}, u32[]{:S(2)}, u32[]{:S(2)}) collective-permute-start(f32[4,80,256]{2,1,0:T(8,128)S(1)} %pad_maximum_fusion.7), channel_id=1, source_target_pairs={{0,4},{1,5},{2,6},{3,7},{4,0},{5,1},{6,2},{7,3},{8,12},{9,13},{10,... | collective-permute-start | bytes 983048 | tf_op jit(solution)/shard_map/ppermute | solution.py:320
  103.9 7.2 %collective-permute-start.21 = (f32[2,72,256]{2,1,0:T(8,128)S(1)}, f32[2,72,256]{2,1,0:T(8,128)S(1)}, u32[]{:S(2)}, u32[]{:S(2)}) collective-permute-start(f32[2,72,256]{2,1,0:T(8,128)S(1)} %pad_maximum_fusion.16), channel_id=1, source_target_pairs={{0,4},{1,5},{2,6},{3,7},{4,0},{5,1},{6,2},{7,3},{8,12},{9,13},{10,... | collective-permute-start | bytes 442376 | tf_op jit(solution)/shard_map/ppermute | solution.py:320
  104.5 8.8 %collective-permute-start.6 = (f32[4,80,256]{2,1,0:T(8,128)S(1)}, f32[4,80,256]{2,1,0:T(8,128)S(1)}, u32[]{:S(2)}, u32[]{:S(2)}) collective-permute-start(f32[4,80,256]{2,1,0:T(8,128)S(1)} %pad_maximum_fusion.6), channel_id=1, source_target_pairs={{0,8},{1,17},{2,10},{3,19},{4,12},{5,21},{6,14},{7,23},{8,0},{9,25... | collective-permute-start | bytes 983048 | tf_op jit(solution)/shard_map/ppermute | solution.py:320
  111.1 8.9 %collective-permute-start.22 = (f32[4,72,256]{2,1,0:T(8,128)S(1)}, f32[4,72,256]{2,1,0:T(8,128)S(1)}, u32[]{:S(2)}, u32[]{:S(2)}) collective-permute-start(f32[4,72,256]{2,1,0:T(8,128)S(1)} %pad_maximum_fusion.10), channel_id=1, source_target_pairs={{0,2},{1,3},{2,0},{3,1},{4,6},{5,7},{6,4},{7,5},{8,10},{9,11},{10,... | collective-permute-start | bytes 884744 | tf_op jit(solution)/shard_map/ppermute | solution.py:320
  112.7 20.0 %collective-permute-start.15 = (f32[8,80,256]{2,1,0:T(8,128)S(1)}, f32[8,80,256]{2,1,0:T(8,128)S(1)}, u32[]{:S(2)}, u32[]{:S(2)}) collective-permute-start(f32[8,80,256]{2,1,0:T(8,128)S(1)} %pad_maximum_fusion.1.refs_2_), channel_id=1, source_target_pairs={{0,2},{1,3},{2,0},{3,1},{4,6},{5,7},{6,4},{7,5},{8,10},{9,11},{10,... | collective-permute-start | bytes 1966088 | tf_op jit(solution)/shard_map/ppermute | solution.py:320
  113.4 19.4 %collective-permute-start.7 = (f32[8,80,256]{2,1,0:T(8,128)S(1)}, f32[8,80,256]{2,1,0:T(8,128)S(1)}, u32[]{:S(2)}, u32[]{:S(2)}) collective-permute-start(f32[8,80,256]{2,1,0:T(8,128)S(1)} %pad_maximum_fusion.refs_0_), channel_id=1, source_target_pairs={{0,4},{1,5},{2,6},{3,7},{4,0},{5,1},{6,2},{7,3},{8,12},{9,13},{10,... | collective-permute-start | bytes 1966088 | tf_op jit(solution)/shard_map/ppermute | solution.py:320
  120.1 12.7 %collective-permute-start.23 = (f32[8,72,256]{2,1,0:T(8,128)S(1)}, f32[8,72,256]{2,1,0:T(8,128)S(1)}, u32[]{:S(2)}, u32[]{:S(2)}) collective-permute-start(f32[8,72,256]{2,1,0:T(8,128)S(1)} %pad_maximum_fusion.4.refs_4_), channel_id=1, source_target_pairs={{0,8},{1,17},{2,10},{3,19},{4,12},{5,21},{6,14},{7,23},{8,0},{9,25... | collective-permute-start | bytes 1769480 | tf_op jit(solution)/shard_map/ppermute | solution.py:320
  160.6 28.1 %collective-permute-start.41 = (f32[8,144,256]{2,1,0:T(8,128)S(1)}, f32[8,144,256]{2,1,0:T(8,128)S(1)}, u32[]{:S(2)}, u32[]{:S(2)}) collective-permute-start(f32[8,144,256]{2,1,0:T(8,128)S(1)} %get-tuple-element.42), channel_id=1, source_target_pairs={{0,2},{1,3},{2,0},{3,1},{4,6},{5,7},{6,4},{7,5},{8,10},{9,11},{10,... | collective-permute-start | bytes 3538952 | tf_op jit(solution)/shard_map/ppermute | solution.py:320
  161.5 31.7 %collective-permute-start.25 = (f32[8,160,256]{2,1,0:T(8,128)S(1)}, f32[8,160,256]{2,1,0:T(8,128)S(1)}, u32[]{:S(2)}, u32[]{:S(2)}) collective-permute-start(f32[8,160,256]{2,1,0:T(8,128)S(1)} %get-tuple-element.38), channel_id=1, source_target_pairs={{0,4},{1,5},{2,6},{3,7},{4,0},{5,1},{6,2},{7,3},{8,12},{9,13},{10,... | collective-permute-start | bytes 3932168 | tf_op jit(solution)/shard_map/ppermute | solution.py:320
  162.5 31.4 %collective-permute-start.33 = (f32[8,160,256]{2,1,0:T(8,128)S(1)}, f32[8,160,256]{2,1,0:T(8,128)S(1)}, u32[]{:S(2)}, u32[]{:S(2)}) collective-permute-start(f32[8,160,256]{2,1,0:T(8,128)S(1)} %get-tuple-element.40), channel_id=1, source_target_pairs={{0,8},{1,17},{2,10},{3,19},{4,12},{5,21},{6,14},{7,23},{8,0},{9,25... | collective-permute-start | bytes 3932168 | tf_op jit(solution)/shard_map/ppermute | solution.py:320
  188.8 15.9 %collective-permute-start.42 = (f32[4,144,256]{2,1,0:T(8,128)S(1)}, f32[4,144,256]{2,1,0:T(8,128)S(1)}, u32[]{:S(2)}, u32[]{:S(2)}) collective-permute-start(f32[4,144,256]{2,1,0:T(8,128)S(1)} %get-tuple-element.57), channel_id=1, source_target_pairs={{0,4},{1,5},{2,6},{3,7},{4,0},{5,1},{6,2},{7,3},{8,12},{9,13},{10,... | collective-permute-start | bytes 1769480 | tf_op jit(solution)/shard_map/ppermute | solution.py:320
  193.4 18.3 %collective-permute-start.26 = (f32[4,160,256]{2,1,0:T(8,128)S(1)}, f32[4,160,256]{2,1,0:T(8,128)S(1)}, u32[]{:S(2)}, u32[]{:S(2)}) collective-permute-start(f32[4,160,256]{2,1,0:T(8,128)S(1)} %get-tuple-element.51), channel_id=1, source_target_pairs={{0,8},{1,17},{2,10},{3,19},{4,12},{5,21},{6,14},{7,23},{8,0},{9,25... | collective-permute-start | bytes 1966088 | tf_op jit(solution)/shard_map/ppermute | solution.py:320
  194.1 23.0 %collective-permute-start.34 = (f32[4,160,256]{2,1,0:T(8,128)S(1)}, f32[4,160,256]{2,1,0:T(8,128)S(1)}, u32[]{:S(2)}, u32[]{:S(2)}) collective-permute-start(f32[4,160,256]{2,1,0:T(8,128)S(1)} %get-tuple-element.49), channel_id=1, source_target_pairs={{0,2},{1,3},{2,0},{3,1},{4,6},{5,7},{6,4},{7,5},{8,10},{9,11},{10,... | collective-permute-start | bytes 1966088 | tf_op jit(solution)/shard_map/ppermute | solution.py:320
  204.8 12.2 %collective-permute-start.43 = (f32[2,144,256]{2,1,0:T(8,128)S(1)}, f32[2,144,256]{2,1,0:T(8,128)S(1)}, u32[]{:S(2)}, u32[]{:S(2)}) collective-permute-start(f32[2,144,256]{2,1,0:T(8,128)S(1)} %get-tuple-element.69), channel_id=1, source_target_pairs={{0,8},{1,17},{2,10},{3,19},{4,12},{5,21},{6,14},{7,23},{8,0},{9,25... | collective-permute-start | bytes 884744 | tf_op jit(solution)/shard_map/ppermute | solution.py:320
  211.9 11.9 %collective-permute-start.27 = (f32[2,160,256]{2,1,0:T(8,128)S(1)}, f32[2,160,256]{2,1,0:T(8,128)S(1)}, u32[]{:S(2)}, u32[]{:S(2)}) collective-permute-start(f32[2,160,256]{2,1,0:T(8,128)S(1)} %get-tuple-element.63), channel_id=1, source_target_pairs={{0,2},{1,3},{2,0},{3,1},{4,6},{5,7},{6,4},{7,5},{8,10},{9,11},{10,... | collective-permute-start | bytes 983048 | tf_op jit(solution)/shard_map/ppermute | solution.py:320
  217.0 6.7 %collective-permute-start.44 = (f32[1,144,256]{2,1,0:T(8,128)S(1)}, f32[1,144,256]{2,1,0:T(8,128)S(1)}, u32[]{:S(2)}, u32[]{:S(2)}) collective-permute-start(f32[1,144,256]{2,1,0:T(8,128)S(1)} %slice_add_fusion.32), channel_id=1, source_target_pairs={{0,16},{1,9},{2,18},{3,11},{4,20},{5,13},{6,22},{7,15},{8,24},{9,1... | collective-permute-start | bytes 442376 | tf_op jit(solution)/shard_map/ppermute | solution.py:320
  217.2 7.1 %collective-permute-start.35 = (f32[2,160,256]{2,1,0:T(8,128)S(1)}, f32[2,160,256]{2,1,0:T(8,128)S(1)}, u32[]{:S(2)}, u32[]{:S(2)}) collective-permute-start(f32[2,160,256]{2,1,0:T(8,128)S(1)} %get-tuple-element.61), channel_id=1, source_target_pairs={{0,4},{1,5},{2,6},{3,7},{4,0},{5,1},{6,2},{7,3},{8,12},{9,13},{10,... | collective-permute-start | bytes 983048 | tf_op jit(solution)/shard_map/ppermute | solution.py:320
  223.8 9.4 %collective-permute-start.28 = (f32[1,160,256]{2,1,0:T(8,128)S(1)}, f32[1,160,256]{2,1,0:T(8,128)S(1)}, u32[]{:S(2)}, u32[]{:S(2)}) collective-permute-start(f32[1,160,256]{2,1,0:T(8,128)S(1)} %slice_add_fusion.26), channel_id=1, source_target_pairs={{0,16},{1,9},{2,18},{3,11},{4,20},{5,13},{6,22},{7,15},{8,24},{9,1... | collective-permute-start | bytes 491528 | tf_op jit(solution)/shard_map/ppermute | solution.py:320
  224.3 17.3 %collective-permute-start.36 = (f32[1,160,256]{2,1,0:T(8,128)S(1)}, f32[1,160,256]{2,1,0:T(8,128)S(1)}, u32[]{:S(2)}, u32[]{:S(2)}) collective-permute-start(f32[1,160,256]{2,1,0:T(8,128)S(1)} %slice_add_fusion.24), channel_id=1, source_target_pairs={{0,16},{1,9},{2,18},{3,11},{4,20},{5,13},{6,22},{7,15},{8,24},{9,1... | collective-permute-start | bytes 491528 | tf_op jit(solution)/shard_map/ppermute | solution.py:320
  233.2 10.2 %collective-permute-start.29 = (f32[1,80,256]{2,1,0:T(8,128)S(1)}, f32[1,80,256]{2,1,0:T(8,128)S(1)}, u32[]{:S(2)}, u32[]{:S(2)}) collective-permute-start(f32[1,80,256]{2,1,0:T(8,128)S(1)} %fusion.13), channel_id=1, source_target_pairs={{0,16},{1,9},{2,18},{3,11},{4,20},{5,13},{6,22},{7,15},{8,24},{9,1... | collective-permute-start | bytes 245768 | tf_op jit(solution)/shard_map/ppermute | solution.py:320
  241.7 6.3 %collective-permute-start.37 = (f32[1,80,256]{2,1,0:T(8,128)S(1)}, f32[1,80,256]{2,1,0:T(8,128)S(1)}, u32[]{:S(2)}, u32[]{:S(2)}) collective-permute-start(f32[1,80,256]{2,1,0:T(8,128)S(1)} %fusion.9), channel_id=1, source_target_pairs={{0,16},{1,9},{2,18},{3,11},{4,20},{5,13},{6,22},{7,15},{8,24},{9,1... | collective-permute-start | bytes 245768 | tf_op jit(solution)/shard_map/ppermute | solution.py:320
  243.4 7.1 %collective-permute-start.30 = (f32[2,80,256]{2,1,0:T(8,128)S(1)}, f32[2,80,256]{2,1,0:T(8,128)S(1)}, u32[]{:S(2)}, u32[]{:S(2)}) collective-permute-start(f32[2,80,256]{2,1,0:T(8,128)S(1)} %pad_maximum_fusion.14), channel_id=1, source_target_pairs={{0,2},{1,3},{2,0},{3,1},{4,6},{5,7},{6,4},{7,5},{8,10},{9,11},{10,... | collective-permute-start | bytes 491528 | tf_op jit(solution)/shard_map/ppermute | solution.py:320
  246.0 6.1 %collective-permute-start.45 = (f32[1,72,256]{2,1,0:T(8,128)S(1)}, f32[1,72,256]{2,1,0:T(8,128)S(1)}, u32[]{:S(2)}, u32[]{:S(2)}) collective-permute-start(f32[1,72,256]{2,1,0:T(8,128)S(1)} %fusion.24), channel_id=1, source_target_pairs={{0,16},{1,9},{2,18},{3,11},{4,20},{5,13},{6,22},{7,15},{8,24},{9,1... | collective-permute-start | bytes 221192 | tf_op jit(solution)/shard_map/ppermute | solution.py:320
  248.1 5.8 %collective-permute-start.38 = (f32[2,80,256]{2,1,0:T(8,128)S(1)}, f32[2,80,256]{2,1,0:T(8,128)S(1)}, u32[]{:S(2)}, u32[]{:S(2)}) collective-permute-start(f32[2,80,256]{2,1,0:T(8,128)S(1)} %pad_maximum_fusion.15), channel_id=1, source_target_pairs={{0,8},{1,17},{2,10},{3,19},{4,12},{5,21},{6,14},{7,23},{8,0},{9,25... | collective-permute-start | bytes 491528 | tf_op jit(solution)/shard_map/ppermute | solution.py:320
  250.5 9.7 %collective-permute-start.31 = (f32[4,80,256]{2,1,0:T(8,128)S(1)}, f32[4,80,256]{2,1,0:T(8,128)S(1)}, u32[]{:S(2)}, u32[]{:S(2)}) collective-permute-start(f32[4,80,256]{2,1,0:T(8,128)S(1)} %pad_maximum_fusion.8), channel_id=1, source_target_pairs={{0,8},{1,17},{2,10},{3,19},{4,12},{5,21},{6,14},{7,23},{8,0},{9,25... | collective-permute-start | bytes 983048 | tf_op jit(solution)/shard_map/ppermute | solution.py:320
  252.1 6.9 %collective-permute-start.46 = (f32[2,72,256]{2,1,0:T(8,128)S(1)}, f32[2,72,256]{2,1,0:T(8,128)S(1)}, u32[]{:S(2)}, u32[]{:S(2)}) collective-permute-start(f32[2,72,256]{2,1,0:T(8,128)S(1)} %pad_maximum_fusion.17), channel_id=1, source_target_pairs={{0,4},{1,5},{2,6},{3,7},{4,0},{5,1},{6,2},{7,3},{8,12},{9,13},{10,... | collective-permute-start | bytes 442376 | tf_op jit(solution)/shard_map/ppermute | solution.py:320
  253.9 9.7 %collective-permute-start.39 = (f32[4,80,256]{2,1,0:T(8,128)S(1)}, f32[4,80,256]{2,1,0:T(8,128)S(1)}, u32[]{:S(2)}, u32[]{:S(2)}) collective-permute-start(f32[4,80,256]{2,1,0:T(8,128)S(1)} %pad_maximum_fusion.9), channel_id=1, source_target_pairs={{0,4},{1,5},{2,6},{3,7},{4,0},{5,1},{6,2},{7,3},{8,12},{9,13},{10,... | collective-permute-start | bytes 983048 | tf_op jit(solution)/shard_map/ppermute | solution.py:320
  259.0 8.0 %collective-permute-start.47 = (f32[4,72,256]{2,1,0:T(8,128)S(1)}, f32[4,72,256]{2,1,0:T(8,128)S(1)}, u32[]{:S(2)}, u32[]{:S(2)}) collective-permute-start(f32[4,72,256]{2,1,0:T(8,128)S(1)} %pad_maximum_fusion.11), channel_id=1, source_target_pairs={{0,2},{1,3},{2,0},{3,1},{4,6},{5,7},{6,4},{7,5},{8,10},{9,11},{10,... | collective-permute-start | bytes 884744 | tf_op jit(solution)/shard_map/ppermute | solution.py:320
  260.3 16.7 %collective-permute-start.32 = (f32[8,80,256]{2,1,0:T(8,128)S(1)}, f32[8,80,256]{2,1,0:T(8,128)S(1)}, u32[]{:S(2)}, u32[]{:S(2)}) collective-permute-start(f32[8,80,256]{2,1,0:T(8,128)S(1)} %pad_maximum_fusion.2.refs_0_), channel_id=1, source_target_pairs={{0,4},{1,5},{2,6},{3,7},{4,0},{5,1},{6,2},{7,3},{8,12},{9,13},{10,... | collective-permute-start | bytes 1966088 | tf_op jit(solution)/shard_map/ppermute | solution.py:320
  263.6 13.4 %collective-permute-start.40 = (f32[8,80,256]{2,1,0:T(8,128)S(1)}, f32[8,80,256]{2,1,0:T(8,128)S(1)}, u32[]{:S(2)}, u32[]{:S(2)}) collective-permute-start(f32[8,80,256]{2,1,0:T(8,128)S(1)} %pad_maximum_fusion.3.refs_2_), channel_id=1, source_target_pairs={{0,2},{1,3},{2,0},{3,1},{4,6},{5,7},{6,4},{7,5},{8,10},{9,11},{10,... | collective-permute-start | bytes 1966088 | tf_op jit(solution)/shard_map/ppermute | solution.py:320
  267.0 9.9 %collective-permute-start.48 = (f32[8,72,256]{2,1,0:T(8,128)S(1)}, f32[8,72,256]{2,1,0:T(8,128)S(1)}, u32[]{:S(2)}, u32[]{:S(2)}) collective-permute-start(f32[8,72,256]{2,1,0:T(8,128)S(1)} %pad_maximum_fusion.5.refs_4_), channel_id=1, source_target_pairs={{0,8},{1,17},{2,10},{3,19},{4,12},{5,21},{6,14},{7,23},{8,0},{9,25... | collective-permute-start | bytes 1769480 | tf_op jit(solution)/shard_map/ppermute | solution.py:320
  (11 other events, 137.1 us)
